TPU v7x, 32 devices: a whole 2x2x4 slice. The times are simulated.
32 devices in a mesh: rows: 8 (over z, x), cols: 4 (over y, core).
Axes of the slice: x: 2, y: 2, z: 4, core: 2. Of those that a mesh axis runs over, the one named last changes fastest.
Arguments:
- tokens: bfloat16 [2048, 4096], P('rows', 'cols'), may hold values from -6 to 6
- cotangent: bfloat16 [2048, 4096], P('rows', 'cols'), may hold values from -6 to 6
- gate_weight: bfloat16 [4096, 7168], P('rows', 'cols'), may hold values from -0.09375 to 0.09375
- down_weight: bfloat16 [4096, 7168], P('rows', 'cols'), may hold values from -0.0625 to 0.0625
- proj_in: bfloat16 [4096, 128], replicated, may hold values from -0.09375 to 0.09375
- proj_out: bfloat16 [7168, 64], P('cols'), may hold values from -0.0625 to 0.0625
- lengths: int32 [32], P('rows'), may hold values from 16 to 64
- loss_mask: int32 [32, 64], P('rows'), may hold values 0 or 1
- gram_in: float32 [8, 1024, 8, 1024], P(None, 'rows', None, 'cols'), as said below
- queries: float32 [256, 8, 1024], P('cols', None, 'rows'), may hold values from -6 to 6
Outputs:
- gram_next: float32 [8, 1024, 8, 1024], P(None, 'rows', None, 'cols')
- query_next: float32 [256, 8, 1024], P('cols', None, 'rows')
- scores: float32 [256, 32], P('cols', 'rows')
Inputs may be any that keep to these rules, and one draw needn't show every extreme that they name: gram_in, read as a 8192 x 8192 matrix, is symmetric positive definite.
All inputs are finite; a program needn't handle non-finite values. No bound on the sum of `loss_mask` on one device may be relied on, other than what follows from the above.
Results may differ from a plain program's by a relative error of at most 0.004.
Values may be sent and summed in bfloat16 or wider, within the bound.
No kernel may reach another device: no remote copies, remote signals or barrier semaphores. Data moves between devices by JAX's collectives and lax.ppermute only.
A program may use at most 128 MiB of HBM per device.

v0:
```python
import jax
import jax.numpy as jnp
from jax import lax
from jax.sharding import PartitionSpec as P

highest = lax.Precision.HIGHEST


def local(
    tokens,
    cotangent,
    gate_weight,
    down_weight,
    proj_in,
    proj_out,
    lengths,
    loss_mask,
    gram_in,
    queries,
):
    row_count = lax.axis_size("rows")
    row_index = lax.axis_index("rows")
    col_index = lax.axis_index("cols")
    full_tokens, full_cotangent = (
        lax.all_gather(tokens, "cols", axis=1, tiled=True),
        lax.all_gather(cotangent, "cols", axis=1, tiled=True),
    )
    gate_pre = jnp.dot(
        full_tokens,
        lax.all_gather(gate_weight, "rows", axis=0, tiled=True),
        preferred_element_type=jnp.float32,
    )
    grad_hidden = jnp.dot(
        full_cotangent,
        lax.all_gather(down_weight, "rows", axis=0, tiled=True),
        preferred_element_type=jnp.float32,
    )
    grad_up = (grad_hidden * jax.nn.silu(gate_pre)).astype(jnp.bfloat16)
    outer_part = jnp.dot(grad_up, proj_out, preferred_element_type=jnp.float32)
    band_width = tokens.shape[1]
    proj_slice = lax.dynamic_slice_in_dim(proj_in, col_index * band_width, band_width, 0)
    inner_part = jnp.dot(tokens, proj_slice, preferred_element_type=jnp.float32)
    proj_inner, proj_outer = lax.psum((inner_part, outer_part), "cols")
    seq_count, window = loss_mask.shape
    inner_width = proj_in.shape[1]
    outer_width = proj_out.shape[1]
    positions = jnp.arange(window, dtype=jnp.int32)
    token_live = (positions[None, :] >= (window - lengths)[:, None]).astype(
        jnp.float32
    ) * loss_mask.astype(jnp.float32)
    weighted = proj_inner.reshape(seq_count, window, inner_width) * token_live[:, :, None]
    features = jnp.einsum(
        "stk,stl->skl",
        weighted,
        proj_outer.reshape(seq_count, window, outer_width),
        precision=highest,
    )
    cycles, band_rows, _, band_cols = gram_in.shape
    panel_width = band_rows * row_count
    features = features.reshape(seq_count, cycles, panel_width)
    every_seq = lax.all_gather(features, "rows", axis=0, tiled=True)
    row_part = lax.dynamic_slice_in_dim(every_seq, row_index * band_rows, band_rows, 2)
    col_part = lax.dynamic_slice_in_dim(every_seq, col_index * band_cols, band_cols, 2)
    seq_total = row_part.shape[0]
    row_flat = row_part.reshape(seq_total, cycles * band_rows)
    col_flat = col_part.reshape(seq_total, cycles * band_cols)
    update = (
        jnp.dot(row_flat.T, col_flat, precision=highest, preferred_element_type=jnp.float32)
        / seq_total
    )
    updated = gram_in + update.reshape(cycles, band_rows, cycles, band_cols)
    panel_rows = lax.all_gather(updated[:, :, 0, :], "cols", axis=2, tiled=True)
    query_heads = jnp.transpose(queries[:, 0, :])
    diag_block, head_cols = (
        lax.all_gather(panel_rows[0], "rows", axis=0, tiled=True),
        lax.all_gather(query_heads, "rows", axis=0, tiled=True),
    )
    factor = jnp.linalg.cholesky(diag_block)
    below_rows = panel_rows[1:].reshape((cycles - 1) * band_rows, panel_width)
    lower_part = jax.scipy.linalg.solve_triangular(factor, below_rows.T, lower=True).T
    own_factor = lax.dynamic_slice_in_dim(factor, row_index * band_rows, band_rows, 0)
    column_block = jnp.concatenate(
        [own_factor[None], lower_part.reshape(cycles - 1, band_rows, panel_width)], axis=0
    )
    panel_part = lax.dynamic_slice_in_dim(column_block, col_index * band_cols, band_cols, 2)
    gram_next = updated.at[:, :, 0, :].set(panel_part)
    query_count = queries.shape[0]
    solved = jax.scipy.linalg.solve_triangular(factor, head_cols, lower=True)
    query_tail = queries[:, 1:, :].reshape(query_count, (cycles - 1) * band_rows) - jnp.dot(
        solved.T, lower_part.T, precision=highest, preferred_element_type=jnp.float32
    )
    own_head = jnp.transpose(lax.dynamic_slice_in_dim(solved, row_index * band_rows, band_rows, 0))
    query_next = jnp.concatenate(
        [own_head[:, None, :], query_tail.reshape(query_count, cycles - 1, band_rows)], axis=1
    )
    whitened = jax.scipy.linalg.solve_triangular(factor, features[:, 0, :].T, lower=True)
    scores = jnp.dot(solved.T, whitened, precision=highest, preferred_element_type=jnp.float32)
    return (gram_next, query_next, scores)


def solution(mesh):
    return jax.shard_map(
        local,
        mesh=mesh,
        in_specs=(
            P("rows", "cols"),
            P("rows", "cols"),
            P("rows", "cols"),
            P("rows", "cols"),
            P(),
            P("cols", None),
            P("rows"),
            P("rows", None),
            P(None, "rows", None, "cols"),
            P("cols", None, "rows"),
        ),
        out_specs=(P(None, "rows", None, "cols"), P("cols", None, "rows"), P("cols", "rows")),
        check_vma=False,
    )
```

profile of v0, /device:TPU:9, one launch (start us, length us, event | category | flops | bytes accessed | tf_op | source)
XLA Modules:
  0.0 1101.7 jit_solution(16905204325622529960)
XLA Ops:
  11.2 22.6 %all-gather.15.cloned.1.call-done = bf16[256,4096]{1,0:T(8,128)(2,1)} async-done(((bf16[256,1024]{1,0:T(8,128)(2,1)}), bf16[256,4096]{1,0:T(8,128)(2,1)}) %all-gather.15.cloned.1.call-update) | async-done | bytes 2097168 | tf_op jit(solution)/shard_map/all_gather | solution.py:25
  33.8 201.6 %all-gather.17.cloned.1.call-done = bf16[4096,1792]{1,0:T(8,128)(2,1)} async-done(((bf16[512,1792]{1,0:T(8,128)(2,1)}), bf16[4096,1792]{1,0:T(8,128)(2,1)}) %all-gather.17.cloned.1.call-update) | async-done | bytes 14680080 | tf_op jit(solution)/shard_map/all_gather | solution.py:30
  235.4 8.4 fusion.149
  243.8 16.6 %all-gather.11.cloned.1.call-done = bf16[256,4096]{1,0:T(8,128)(2,1)} async-done(((bf16[256,1024]{1,0:T(8,128)(2,1)}), bf16[256,4096]{1,0:T(8,128)(2,1)}) %all-gather.11.cloned.1.call-update) | async-done | bytes 2097168 | tf_op jit(solution)/shard_map/all_gather | solution.py:26
  260.4 201.4 %all-gather.13.cloned.1.call-done = bf16[4096,1792]{1,0:T(8,128)(2,1)} async-done(((bf16[512,1792]{1,0:T(8,128)(2,1)}), bf16[4096,1792]{1,0:T(8,128)(2,1)}) %all-gather.13.cloned.1.call-update) | async-done | bytes 14680080 | tf_op jit(solution)/shard_map/all_gather | solution.py:35
  461.8 10.1 fusion.23
  472.9 31.6 %all-reduce.4.cloned.1.call-done = (f32[4,64,64]{1,2,0:T(8,128)}, f32[4,64,128]{2,1,0:T(8,128)}) async-done(((f32[4,64,64]{1,2,0:T(8,128)}, f32[4,64,128]{2,1,0:T(8,128)}), (f32[4,64,64]{1,2,0:T(8,128)}, f32[4,64,128]{2,1,0:T(8,128)})) %all-reduce.4.cloned.1.call-update) | async-done | bytes 196624 | tf_op jit(solution)/shard_map/psum | solution.py:43
  507.2 9.1 copy.34
  516.3 30.3 %all-gather.19.cloned.1.call-done = f32[32,8,1024]{2,1,0:T(8,128)} async-done(((f32[4,8,1024]{2,1,0:T(8,128)}), f32[32,8,1024]{2,1,0:T(8,128)}) %all-gather.19.cloned.1.call-update) | async-done | bytes 1048592 | tf_op jit(solution)/shard_map/all_gather | solution.py:61
  562.8 9.2 copy.35
  572.0 11.2 %add.112 = f32[8,128,8,256]{1,3,2,0:T(8,128)} add(f32[8,128,8,256]{1,3,2,0:T(8,128)} %copy.34, f32[8,128,8,256]{1,3,2,0:T(8,128)} %copy.35) | non-fusion elementwise | flops 2097152 | bytes 25165824 | tf_op jit(solution)/shard_map/add | solution.py:71
  585.5 35.4 %all-gather.21.cloned.1.call-done = f32[8,128,1,1024]{1,3,2,0:T(8,128)} async-done(((f32[8,128,1,256]{1,3,2,0:T(8,128)}), f32[8,128,1,1024]{1,3,2,0:T(8,128)}) %all-gather.21.cloned.1.call-update) | async-done | bytes 4194320 | tf_op jit(solution)/shard_map/all_gather | solution.py:72
  623.6 23.2 %all_gather.31 = f32[1024,64]{0,1:T(8,128)S(1)} all-gather(f32[128,64]{0,1:T(8,128)S(1)} %bitcast.239), channel_id=1, replica_groups=mesh['rows'=8,'cols'=4] {'rows'}, dimensions={0}, use_global_device_ids=true | all-gather | bytes 294912 | tf_op jit(solution)/shard_map/all_gather | solution.py:76
  661.8 37.2 %all-gather.23.cloned.1.call-done = f32[1,1024,1,1024]{1,3,2,0:T(8,128)} async-done(((f32[1,128,1,1024]{1,3,2,0:T(8,128)}), f32[1,1024,1,1024]{1,3,2,0:T(8,128)}) %all-gather.23.cloned.1.call-update) | async-done | bytes 4194320 | tf_op jit(solution)/shard_map/all_gather | solution.py:75
  711.3 11.7 %cholesky.223 = f32[128,128]{1,0:T(8,128)S(1)} custom-call(f32[128,128]{1,0:T(8,128)S(1)} %cholesky.580), custom_call_target="Cholesky" | custom-call | tf_op jit(solution)/shard_map/jit(cholesky)/cholesky | solution.py:78
  725.6 9.8 custom-call.69
  739.3 11.9 %cholesky.244 = f32[128,128]{1,0:T(8,128)S(1)} custom-call(f32[128,128]{1,0:T(8,128)S(1)} %cholesky.584), custom_call_target="Cholesky" | custom-call | tf_op jit(solution)/shard_map/jit(cholesky)/cholesky | solution.py:78
  751.8 9.8 custom-call.70
  764.9 11.7 %cholesky.468 = f32[128,128]{1,0:T(8,128)S(1)} custom-call(f32[128,128]{1,0:T(8,128)S(1)} %cholesky.589), custom_call_target="Cholesky" | custom-call | tf_op jit(solution)/shard_map/jit(cholesky)/cholesky | solution.py:78
  777.3 9.8 custom-call.71
  790.6 11.9 %cholesky.487 = f32[128,128]{1,0:T(8,128)S(1)} custom-call(f32[128,128]{1,0:T(8,128)S(1)} %cholesky.594), custom_call_target="Cholesky" | custom-call | tf_op jit(solution)/shard_map/jit(cholesky)/cholesky | solution.py:78
  803.1 9.8 custom-call.72
  816.3 11.7 %cholesky.506 = f32[128,128]{1,0:T(8,128)S(1)} custom-call(f32[128,128]{1,0:T(8,128)S(1)} %cholesky.599), custom_call_target="Cholesky" | custom-call | tf_op jit(solution)/shard_map/jit(cholesky)/cholesky | solution.py:78
  828.7 10.2 custom-call.73
  842.2 11.7 %cholesky.526 = f32[128,128]{1,0:T(8,128)S(1)} custom-call(f32[128,128]{1,0:T(8,128)S(1)} %cholesky.604), custom_call_target="Cholesky" | custom-call | tf_op jit(solution)/shard_map/jit(cholesky)/cholesky | solution.py:78
  854.5 9.8 custom-call.74
  867.3 11.7 %cholesky.546 = f32[128,128]{1,0:T(8,128)S(1)} custom-call(f32[128,128]{1,0:T(8,128)S(1)} %cholesky.609), custom_call_target="Cholesky" | custom-call | tf_op jit(solution)/shard_map/jit(cholesky)/cholesky | solution.py:78
  879.7 9.8 custom-call.75
  892.1 11.7 %cholesky.564 = f32[128,128]{1,0:T(8,128)S(1)} custom-call(f32[128,128]{1,0:T(8,128)S(1)} %convolution_subtract_fusion.12), custom_call_target="Cholesky" | custom-call | tf_op jit(solution)/shard_map/jit(cholesky)/cholesky | solution.py:78
  919.1 23.6 %while.2 = (s32[]{:T(128)}, f32[1024,1024]{1,0:T(8,128)}, s32[8,2]{0,1:T(2,128)S(1)}, f32[8,128,128]{2,1,0:T(8,128)S(1)}, s32[]{:T(128)}) while((s32[]{:T(128)}, f32[1024,1024]{1,0:T(8,128)}, s32[8,2]{0,1:T(2,128)S(1)}, f32[8,128,128]{2,1,0:T(8,128)S(1)}, s32[]{:T(128)}) %tuple.113), condition=%wide.while_cond.1, body=%wide.while_body.1.sunk | while | flops 2 | bytes 131189 | solution.py:80
  942.7 78.8 %custom-call.76 = f32[8,128,128]{1,2,0:T(8,128)S(1)} custom-call(f32[8,128,128]{2,1,0:T(8,128)S(1)} %get-tuple-element.22), custom_call_target="InvertDiagBlocksLowerTriangular" | custom-call | tf_op jit(solution)/shard_map/jit(_solve_triangular)/triangular_solve | solution.py:80
  1057.5 9.1 copy.44
  (181 shorter events, 182.6 us)
Async XLA Ops:
  7.2 2.9 copy-start
  7.2 2.9 copy-start.4
  7.2 4.0 copy-start.9
  7.2 26.6 %all-gather.15.cloned.1.call-start = ((), (), s32[]{:S(2)}) async-start(), calls=%async_computation.2 | async-start | bytes 2621440 | tf_op jit(solution)/shard_map/all_gather | solution.py:25
  7.9 227.4 %all-gather.17.cloned.1.call-start = ((), (), s32[]{:S(2)}) async-start(), calls=%async_computation.3 | async-start | bytes 16515072 | tf_op jit(solution)/shard_map/all_gather | solution.py:30
  8.7 251.7 %all-gather.11.cloned.1.call-start = ((), (), s32[]{:S(2)}) async-start(), calls=%async_computation | async-start | bytes 2621440 | tf_op jit(solution)/shard_map/all_gather | solution.py:26
  9.4 452.4 %all-gather.13.cloned.1.call-start = ((), (), s32[]{:S(2)}) async-start(), calls=%async_computation.1 | async-start | bytes 16515072 | tf_op jit(solution)/shard_map/all_gather | solution.py:35
  10.0 494.4 %all-reduce.4.cloned.1.call-start = ((), (), s32[]{:S(2)}) async-start(), calls=%async_computation.7 | async-start | bytes 524288 | tf_op jit(solution)/shard_map/psum | solution.py:43
  11.1 450.7 %copy-start.8 = (bf16[1792,64]{0,1:T(8,128)(2,1)S(1)}, bf16[1792,64]{0,1:T(8,128)(2,1)}, u32[]{:S(2)}) copy-start(bf16[1792,64]{0,1:T(8,128)(2,1)} %param.17) | copy-start | bytes 688132
  243.8 229.0 %copy-start.7 = (s32[4,64]{1,0:T(4,128)S(1)}, s32[4,64]{1,0:T(4,128)}, u32[]{:S(2)}) copy-start(s32[4,64]{1,0:T(4,128)} %param.19) | copy-start | bytes 3076
  472.8 73.8 %all-gather.19.cloned.1.call-start = ((), (), s32[]{:S(2)}) async-start(), calls=%async_computation.4 | async-start | bytes 1179648 | tf_op jit(solution)/shard_map/all_gather | solution.py:61
  506.9 114.0 %all-gather.21.cloned.1.call-start = ((), (), s32[]{:S(2)}) async-start(), calls=%async_computation.5 | async-start | bytes 5242880 | tf_op jit(solution)/shard_map/all_gather | solution.py:72
  583.1 39.7 %copy-start.6 = (f32[64,8,128]{2,1,0:T(8,128)S(1)}, f32[64,8,128]{2,1,0:T(8,128)}, u32[]{:S(2)}) copy-start(f32[64,8,128]{2,1,0:T(8,128)} %param.21) | copy-start | bytes 786436
  583.1 40.4 %slice-start = ((f32[64,8,128]{2,1,0:T(8,128)}), f32[64,1,128]{2,1,0:T(1,128)S(1)}, s32[]{:S(2)}) async-start(f32[64,8,128]{2,1,0:T(8,128)} %param.21), calls=%async_computation.8 | async-start | bytes 65536 | tf_op jit(solution)/shard_map/slice | solution.py:73
  585.5 113.6 %all-gather.23.cloned.1.call-start = ((), (), s32[]{:S(2)}) async-start(), calls=%async_computation.6 | async-start | bytes 4718592 | tf_op jit(solution)/shard_map/all_gather | solution.py:75
  709.3 2.0 copy-start.3
  1021.5 5.6 copy-start.2
  1066.7 11.2 %copy-start.5 = (f32[64,7,128]{2,1,0:T(8,128)S(1)}, f32[64,7,128]{2,1,0:T(8,128)}, u32[]{:S(2)}) copy-start(f32[64,7,128]{2,1,0:T(8,128)} %slice.431) | copy-start | bytes 688132
  1077.7 16.8 %copy-start.1 = (bf16[4096,128]{1,0:T(8,128)(2,1)S(1)}, bf16[4096,128]{1,0:T(8,128)(2,1)}, u32[]{:S(2)}) copy-start(bf16[4096,128]{1,0:T(8,128)(2,1)} %param.16) | copy-start | bytes 3145732
Sparse Core Ops, SparseCore 0:
  9.6 24.1 all-gather.14
  36.0 199.3 all-gather.16
  236.9 23.4 all-gather.10
  262.4 199.3 all-gather.12
  472.9 31.5 all-reduce.3
  507.0 39.5 all-gather.18
  585.6 35.2 all-gather.20
  623.2 75.8 all-gather.22
where the time goes:
time: 1110 us; the launch traced here: 1100 us
  waiting for transfers between devices  579 us (52%)
  other arithmetic  274 us (25%)
  matrix products  105 us (9%)
  local copies, waits for them, and re-layouts  99.3 us (9%)
  blocking collectives  23.2 us (2%)
  between operations  20.2 us (2%)
    all_gather x1, waiting for transfers between devices, local(): lax.all_gather(gate_weight, 'rows', axis=0, tiled=True)  202 us
    all_gather x1, waiting for transfers between devices, local(): lax.all_gather(down_weight, 'rows', axis=0, tiled=True)  201 us
    another operation x30, other arithmetic, local(): factor = jnp.linalg.cholesky(diag_block)  172 us
    another operation x3, other arithmetic, local(): jax.scipy.linalg.solve_triangular(factor, below_rows.T, lower=True)  83.7 us
    all_gather x1, waiting for transfers between devices, local(): lax.all_gather(panel_rows[0], 'rows', axis=0, tiled=True)  37.2 us
    all_gather x1, waiting for transfers between devices, local(): panel_rows = lax.all_gather(updated[:, :, 0, :], 'cols', axis=2, tiled=True)  35.4 us
    psum x1, waiting for transfers between devices, local(): proj_inner, proj_outer = lax.psum((inner_part, outer_part), 'cols')  31.6 us
    all_gather x1, waiting for transfers between devices, local(): every_seq = lax.all_gather(features, 'rows', axis=0, tiled=True)  30.3 us
  transfers between devices with their start and end apart: 8, of which 8 were waited for; matrix products, arithmetic and copies ran while one was open for 3% of the time, Pallas kernels for 0%

commit v1 on v0

v1 whole, which is shorter than its diff:
```python
import functools
import jax
import jax.numpy as jnp
from jax import lax
from jax.experimental import pallas as pl
from jax.experimental.pallas import tpu as pltpu
from jax.sharding import PartitionSpec as P

highest = lax.Precision.HIGHEST


def eliminate(rows, size):
    shape = (8, size)
    sub = lax.broadcasted_iota(jnp.int32, shape, 0)
    lane = lax.broadcasted_iota(jnp.int32, shape, 1)
    count = size // 8

    def row_of(x, k):
        return jnp.broadcast_to(x[k : k + 1, :], shape)

    for p in range(count):
        base = 8 * p
        inside = (lane >= base) & (lane < base + 8)

        def columns(q):
            return [jnp.broadcast_to(rows[q][:, base + k : base + k + 1], shape) for k in range(8)]

        cols = columns(p)
        own = jnp.where(inside, jnp.where(lane - base == sub, 1.0, 0.0), rows[p])
        scaled_cols, scaled_rows, scale = [], [], jnp.zeros(shape, jnp.float32)
        for k in range(8):
            pivot = row_of(cols[k], k)
            inverse = 1.0 / pivot
            scale = jnp.where(sub == k, lax.rsqrt(pivot), scale)
            heads = [row_of(cols[j], k) * inverse for j in range(k + 1, 8)]
            head_row = row_of(own, k) * inverse
            scaled_cols.append(heads)
            scaled_rows.append(head_row)
            below = jnp.where(sub > k, cols[k], 0.0)
            for j in range(k + 1, 8):
                cols[j] = cols[j] - below * heads[j - k - 1]
            own = own - below * head_row
        for q in range(p + 1, count):
            other = columns(q)
            value = jnp.where(inside, 0.0, rows[q])
            for k in range(8):
                for j in range(k + 1, 8):
                    other[j] = other[j] - other[k] * scaled_cols[k][j - k - 1]
                value = value - other[k] * scaled_rows[k]
            rows[q] = value
        rows[p] = jnp.where(lane < base + 8, own * scale, 0.0)
    return rows


def mm(a, b):
    return jnp.dot(a, b, precision=highest, preferred_element_type=jnp.float32)


def mm_t(a, b):
    return lax.dot_general(
        a, b, (((1,), (1,)), ((), ())), precision=highest, preferred_element_type=jnp.float32
    )


def panel_kernel(block, share, diag_ref, below_ref, head_ref, left_ref, right_ref, out_ref, inv_ref, upper_ref):
    width = diag_ref.shape[0]
    low = below_ref.shape[0]
    total = out_ref.shape[0]
    for start in range(0, width, block):
        rows = slice(start, start + block)
        out_ref[rows, :] = (
            diag_ref[rows, :]
            + jnp.dot(left_ref[rows, :], right_ref[...], preferred_element_type=jnp.float32) * share
        )
    step = block if low % block == 0 else low
    for start in range(0, low, step):
        rows = slice(start, start + step)
        left = slice(width + start, width + start + step)
        out_ref[left, :] = (
            below_ref[rows, :]
            + jnp.dot(left_ref[left, :], right_ref[...], preferred_element_type=jnp.float32) * share
        )
    out_ref[width + low :, :] = head_ref[...]
    blocks = width // block

    def one(b, carry):
        off = pl.multiple_of(b * block, block)
        rows = [
            out_ref[pl.ds(pl.multiple_of(off + 8 * q, 8), 8), pl.ds(off, block)]
            for q in range(block // 8)
        ]
        rows = eliminate(rows, block)
        for q in range(block // 8):
            inv_ref[8 * q : 8 * q + 8, :] = rows[q]
        for s in range(blocks):

            @pl.when(b == s)
            def _():
                here = slice(s * block, (s + 1) * block)
                inv = inv_ref[...]
                if s + 1 < blocks:
                    upper_ref[:, (s + 1) * block :] = mm(inv, out_ref[here, (s + 1) * block :])
                chunk = 2 * block
                for start in range(s * block, total, chunk):
                    these = slice(start, min(start + chunk, total))
                    out_ref[these, here] = mm_t(out_ref[these, here], inv)
                for start in range((s + 1) * block, total, chunk):
                    if s + 1 < blocks:
                        these = slice(start, min(start + chunk, total))
                        out_ref[these, (s + 1) * block :] = out_ref[these, (s + 1) * block :] - mm(
                            out_ref[these, here], upper_ref[:, (s + 1) * block :]
                        )

        return carry

    lax.fori_loop(0, blocks, one, 0)


def panel(diag, below, heads, left, right, share):
    block = 128
    width, low, extra = diag.shape[0], below.shape[0], heads.shape[0]
    return pl.pallas_call(
        functools.partial(panel_kernel, block, share),
        out_shape=jax.ShapeDtypeStruct((width + low + extra, width), jnp.float32),
        in_specs=[pl.BlockSpec(memory_space=pltpu.VMEM)] * 5,
        out_specs=pl.BlockSpec(memory_space=pltpu.VMEM),
        scratch_shapes=[pltpu.VMEM((block, block), jnp.float32), pltpu.VMEM((block, width), jnp.float32)],
        compiler_params=pltpu.CompilerParams(vmem_limit_bytes=48 * 1024 * 1024),
        name="panel_factor",
    )(diag, below, heads, left, right)


def pack(x, left):
    high = lax.reduce_precision(x, 8, 7)
    rest = x - high
    mid = lax.reduce_precision(rest, 8, 7)
    low = rest - mid
    high, mid, low = (v.astype(jnp.bfloat16) for v in (high, mid, low))
    parts = (high, high, mid, high, low, mid) if left else (high, mid, high, low, high, mid)
    return jnp.concatenate(parts, axis=-1 if left else -2)


def gram_kernel(cycles, share, gram_ref, left_ref, right_ref, panel_ref, out_ref):
    count = left_ref.shape[1]
    out_ref[pl.ds(0, count, stride=cycles), :] = panel_ref[0]
    for b in range(1, cycles):
        update = jnp.dot(left_ref[0], right_ref[b], preferred_element_type=jnp.float32)
        here = pl.ds(b, count, stride=cycles)
        out_ref[here, :] = gram_ref[here, :] + update * share


def gram_update(gram, left, right, panel_part, share):
    cycles, count, depth = left.shape
    width = gram.shape[1]
    lanes = 128
    if width % lanes:
        update = jnp.einsum("auk,bkv->aubv", left, right, preferred_element_type=jnp.float32)
        full = gram.reshape(cycles, count, cycles, width) + update * share
        return full.at[:, :, 0, :].set(panel_part).reshape(gram.shape)
    return pl.pallas_call(
        functools.partial(gram_kernel, cycles, share),
        out_shape=jax.ShapeDtypeStruct(gram.shape, jnp.float32),
        grid=(cycles, width // lanes),
        in_specs=[
            pl.BlockSpec((count * cycles, lanes), lambda a, v: (a, v)),
            pl.BlockSpec((1, count, depth), lambda a, v: (a, 0, 0)),
            pl.BlockSpec((cycles, depth, lanes), lambda a, v: (0, 0, v)),
            pl.BlockSpec((1, count, lanes), lambda a, v: (a, 0, v)),
        ],
        out_specs=pl.BlockSpec((count * cycles, lanes), lambda a, v: (a, v)),
        compiler_params=pltpu.CompilerParams(vmem_limit_bytes=48 * 1024 * 1024),
        name="gram_update",
    )(gram, left, right, panel_part)


def finish(features, gram_in, queries, panel_rows, diag_block, heads):
    row_count = lax.axis_size("rows")
    row_index = lax.axis_index("rows")
    col_index = lax.axis_index("cols")
    cycles, band_rows, _, band_cols = gram_in.shape
    panel_width = band_rows * row_count
    query_count = queries.shape[0]
    every_seq = lax.all_gather(features, "rows", axis=0, tiled=True)
    seq_count, seq_total = features.shape[0], every_seq.shape[0]
    share = 1.0 / seq_total
    flat = jnp.transpose(every_seq, (1, 2, 0))
    first_left = pack(flat[0], True)
    first_right = pack(every_seq[:, 0, :], False)
    own_left = pack(lax.dynamic_slice_in_dim(flat, row_index * band_rows, band_rows, 1), True)
    col_part = lax.dynamic_slice_in_dim(every_seq, col_index * band_cols, band_cols, 2)
    own_right = pack(jnp.transpose(col_part, (1, 0, 2)), False)
    low = (cycles - 1) * band_rows
    left = jnp.concatenate([first_left, own_left[1:].reshape(low, -1)], axis=0)
    below = panel_rows[1:].reshape(low, panel_width)
    used = low + query_count + seq_count
    spare = -used % 128
    head_rows = jnp.concatenate(
        [heads, features[:, 0, :], jnp.zeros((spare, panel_width), jnp.float32)], axis=0
    )
    solved_all = panel(diag_block, below, head_rows, left, first_right, share)
    own_factor = lax.dynamic_slice_in_dim(solved_all, row_index * band_rows, band_rows, 0)
    place = row_index * band_rows + lax.broadcasted_iota(jnp.int32, own_factor.shape, 0)
    own_factor = jnp.where(
        lax.broadcasted_iota(jnp.int32, own_factor.shape, 1) <= place, own_factor, 0.0
    )
    lower_part = solved_all[panel_width : panel_width + low]
    solved = solved_all[panel_width + low : panel_width + low + query_count]
    whitened = solved_all[panel_width + low + query_count : panel_width + used]
    column_block = jnp.concatenate([own_factor, lower_part], axis=0)
    panel_part = lax.dynamic_slice_in_dim(column_block, col_index * band_cols, band_cols, 1)
    gram_next = gram_update(
        gram_in.reshape(cycles * band_rows * cycles, band_cols),
        own_left,
        own_right,
        panel_part.reshape(cycles, band_rows, band_cols),
        share,
    ).reshape(gram_in.shape)
    query_tail = queries[:, 1:, :] - mm_t(solved, lower_part).reshape(
        query_count, cycles - 1, band_rows
    )
    own_head = lax.dynamic_slice_in_dim(solved, row_index * band_rows, band_rows, 1)
    query_next = jnp.concatenate([own_head[:, None, :], query_tail], axis=1)
    scores = mm_t(solved, whitened)
    return gram_next, query_next, scores


def early(gram_in, queries):
    panel_rows = lax.all_gather(gram_in[:, :, 0, :], "cols", axis=2, tiled=True)
    diag_block = lax.all_gather(panel_rows[0], "rows", axis=0, tiled=True)
    heads = lax.all_gather(queries[:, 0, :], "rows", axis=1, tiled=True)
    return panel_rows, diag_block, heads


def local(
    tokens,
    cotangent,
    gate_weight,
    down_weight,
    proj_in,
    proj_out,
    lengths,
    loss_mask,
    gram_in,
    queries,
):
    col_index = lax.axis_index("cols")
    full_tokens, full_cotangent = (
        lax.all_gather(tokens, "cols", axis=1, tiled=True),
        lax.all_gather(cotangent, "cols", axis=1, tiled=True),
    )
    gate_pre = jnp.dot(
        full_tokens,
        lax.all_gather(gate_weight, "rows", axis=0, tiled=True),
        preferred_element_type=jnp.float32,
    )
    grad_hidden = jnp.dot(
        full_cotangent,
        lax.all_gather(down_weight, "rows", axis=0, tiled=True),
        preferred_element_type=jnp.float32,
    )
    grad_up = (grad_hidden * jax.nn.silu(gate_pre)).astype(jnp.bfloat16)
    outer_part = jnp.dot(grad_up, proj_out, preferred_element_type=jnp.float32)
    band_width = tokens.shape[1]
    proj_slice = lax.dynamic_slice_in_dim(proj_in, col_index * band_width, band_width, 0)
    inner_part = jnp.dot(tokens, proj_slice, preferred_element_type=jnp.float32)
    proj_inner, proj_outer = lax.psum((inner_part, outer_part), "cols")
    seq_count, window = loss_mask.shape
    inner_width = proj_in.shape[1]
    outer_width = proj_out.shape[1]
    positions = jnp.arange(window, dtype=jnp.int32)
    token_live = (positions[None, :] >= (window - lengths)[:, None]).astype(
        jnp.float32
    ) * loss_mask.astype(jnp.float32)
    weighted = proj_inner.reshape(seq_count, window, inner_width) * token_live[:, :, None]
    features = jnp.einsum(
        "stk,stl->skl",
        weighted,
        proj_outer.reshape(seq_count, window, outer_width),
        precision=highest,
    )
    cycles, band_rows, _, band_cols = gram_in.shape
    features = features.reshape(seq_count, cycles, band_rows * lax.axis_size("rows"))
    panel_rows, diag_block, heads = early(gram_in, queries)
    return finish(features, gram_in, queries, panel_rows, diag_block, heads)


def solution(mesh):
    return jax.shard_map(
        local,
        mesh=mesh,
        in_specs=(
            P("rows", "cols"),
            P("rows", "cols"),
            P("rows", "cols"),
            P("rows", "cols"),
            P(),
            P("cols", None),
            P("rows"),
            P("rows", None),
            P(None, "rows", None, "cols"),
            P("cols", None, "rows"),
        ),
        out_specs=(P(None, "rows", None, "cols"), P("cols", None, "rows"), P("cols", "rows")),
        check_vma=False,
    )
```

time: 1110 us -> 788 us (0.71)
  other arithmetic: 274 us -> 5.44 us
  Pallas kernels: 0 us -> 98.2 us
  local copies, waits for them, and re-layouts: 99.3 us -> 20.2 us
  matrix products: 105 us -> 27.2 us
    another operation x33 -> x0, other arithmetic: 256 us -> none  [the longest x30 172 us: local(): factor = jnp.linalg.cholesky(diag_block)]
    pallas_call x0 -> x2, Pallas kernels: none -> 98.2 us  [the longest x1 84.1 us: panel(): pl.pallas_call(functools.partial(panel_kernel, block, share), out_shape=j...]
    another operation x59 -> x0, matrix products: 72.8 us -> none  [the longest x15 28.3 us: local(): jax.scipy.linalg.solve_triangular(factor, below_rows.T, lower=True)]
    another operation x33 -> x0, local copies, waits for them, and re-layouts: 26 us -> none
    unnamed x25 -> x20, local copies, waits for them, and re-layouts: 27.7 us -> 3.13 us
    reshape x4 -> x2, local copies, waits for them, and re-layouts: 15 us -> 0.82 us  [the longest x1 0.78 us: local(): features.reshape(seq_count, cycles, band_rows * lax.axis_size('rows'))]
    add x1, other arithmetic: 11.2 us -> 0.01 us  [finish(): row_index * band_rows + lax.broadcasted_iota(jnp.int32, own_factor.shape, 0)]
  transfers between devices with their start and end apart: 8 -> 8, of which waited for: 8 -> 8; matrix products, arithmetic and copies ran while one was open for 3% -> 4% of each run, Pallas kernels for 0% -> 0%
where the time goes in v1:
time: 788 us; the launch traced here: 777 us
  waiting for transfers between devices  588 us (75%)
  Pallas kernels  98.2 us (12%)
  matrix products  27.2 us (3%)
  blocking collectives  22.2 us (3%)
  local copies, waits for them, and re-layouts  20.2 us (3%)
  between operations  14.9 us (2%)
    all_gather x1, waiting for transfers between devices, local(): lax.all_gather(gate_weight, 'rows', axis=0, tiled=True)  202 us
    all_gather x1, waiting for transfers between devices, local(): lax.all_gather(down_weight, 'rows', axis=0, tiled=True)  201 us
    pallas_call x1, Pallas kernels, panel(): pl.pallas_call(functools.partial(panel_kernel, block, share), out_shape=j...  84.1 us
    all_gather x1, waiting for transfers between devices, early(): diag_block = lax.all_gather(panel_rows[0], 'rows', axis=0, tiled=True)  65.6 us
    all_gather x1, waiting for transfers between devices, early(): panel_rows = lax.all_gather(gram_in[:, :, 0, :], 'cols', axis=2, tiled=True)  35.5 us
    psum x1, waiting for transfers between devices, local(): proj_inner, proj_outer = lax.psum((inner_part, outer_part), 'cols')  30.4 us
    all_gather x1, waiting for transfers between devices, local(): lax.all_gather(tokens, 'cols', axis=1, tiled=True)  22.6 us
    all_gather x1, blocking collectives, early(): heads = lax.all_gather(queries[:, 0, :], 'rows', axis=1, tiled=True)  22.2 us
  transfers between devices with their start and end apart: 8, of which 8 were waited for; matrix products, arithmetic and copies ran while one was open for 4% of the time, Pallas kernels for 0%

profile of v1, /device:TPU:9, one launch (start us, length us, event | category | flops | bytes accessed | tf_op | source)
XLA Modules:
  0.0 776.7 jit_solution(16424961739551716958)
XLA Ops:
  7.2 0.7 all-gather.16.cloned.1.call-update
  8.0 0.7 all-gather.18.cloned.1.call-update
  10.4 0.7 copy.42
  11.1 22.6 %all-gather.16.cloned.1.call-done = bf16[256,4096]{1,0:T(8,128)(2,1)} async-done(((bf16[256,1024]{1,0:T(8,128)(2,1)}), bf16[256,4096]{1,0:T(8,128)(2,1)}) %all-gather.16.cloned.1.call-update) | async-done | bytes 2097168 | tf_op jit(solution)/shard_map/all_gather | solution.py:248
  33.8 201.6 %all-gather.18.cloned.1.call-done = bf16[4096,1792]{1,0:T(8,128)(2,1)} async-done(((bf16[512,1792]{1,0:T(8,128)(2,1)}), bf16[4096,1792]{1,0:T(8,128)(2,1)}) %all-gather.18.cloned.1.call-update) | async-done | bytes 14680080 | tf_op jit(solution)/shard_map/all_gather | solution.py:253
  235.4 8.4 %fusion.22 = f32[256,1792]{1,0:T(8,128)S(1)} fusion(bf16[256,4096]{1,0:T(8,128)(2,1)} %all-gather.16.cloned.1.call-done, bf16[4096,1792]{1,0:T(8,128)(2,1)} %all-gather.18.cloned.1.call-done), kind=kOutput, calls=%fused_computation.68 | convolution fusion | flops 3758096384 | bytes 18612224 | tf_op jit(solution)/shard_map/dot_general | solution.py:251
  243.8 16.6 %all-gather.12.cloned.1.call-done = bf16[256,4096]{1,0:T(8,128)(2,1)} async-done(((bf16[256,1024]{1,0:T(8,128)(2,1)}), bf16[256,4096]{1,0:T(8,128)(2,1)}) %all-gather.12.cloned.1.call-update) | async-done | bytes 2097168 | tf_op jit(solution)/shard_map/all_gather | solution.py:249
  260.4 201.4 %all-gather.14.cloned.1.call-done = bf16[4096,1792]{1,0:T(8,128)(2,1)} async-done(((bf16[512,1792]{1,0:T(8,128)(2,1)}), bf16[4096,1792]{1,0:T(8,128)(2,1)}) %all-gather.14.cloned.1.call-update) | async-done | bytes 14680080 | tf_op jit(solution)/shard_map/all_gather | solution.py:258
  461.8 10.1 %fusion.1 = f32[256,64]{0,1:T(8,128)S(1)} fusion(bf16[1792,64]{0,1:T(8,128)(2,1)S(1)} %copy-done.7, bf16[256,4096]{1,0:T(8,128)(2,1)} %all-gather.12.cloned.1.call-done, bf16[4096,1792]{1,0:T(8,128)(2,1)} %all-gather.14.cloned.1.call-done, f32[256,1792]{1,0:T(8,128)S(1)} %fusion.22), kind=kOutput, calls=%fused_computation.4 | convolution fusion | flops 3819569152 | bytes 18907136 | tf_op jit(solution)/shard_map/dot_general | solution.py:262
  472.8 1.0 copy.57
  474.0 30.4 %all-reduce.3.cloned.1.call-done = (f32[4,64,64]{1,2,0:T(8,128)}, f32[4,64,128]{2,1,0:T(8,128)}) async-done(((f32[4,64,64]{1,2,0:T(8,128)}, f32[4,64,128]{2,1,0:T(8,128)}), (f32[4,64,64]{1,2,0:T(8,128)}, f32[4,64,128]{2,1,0:T(8,128)})) %all-reduce.3.cloned.1.call-update) | async-done | bytes 196624 | tf_op jit(solution)/shard_map/psum | solution.py:266
  504.5 1.6 fusion.10
  506.1 0.8 reshape.38
  506.9 35.5 %all-gather.22.cloned.1.call-done = f32[8,128,1,1024]{3,1,2,0:T(8,128)} async-done(((f32[8,128,1,256]{3,1,2,0:T(8,128)}), f32[8,128,1,1024]{3,1,2,0:T(8,128)}) %all-gather.22.cloned.1.call-update) | async-done | bytes 4194320 | tf_op jit(solution)/shard_map/all_gather | solution.py:228
  542.5 1.9 slice.50
  544.5 22.2 %all-gather.2 = f32[64,1,1024]{2,0,1:T(8,128)S(1)} all-gather(f32[64,1,128]{2,0,1:T(8,128)S(1)} %bitcast.95), channel_id=4, replica_groups=mesh['rows'=8,'cols'=4] {'rows'}, dimensions={2}, use_global_device_ids=true | all-gather | bytes 294912 | tf_op jit(solution)/shard_map/all_gather | solution.py:230
  566.7 4.3 slice.51
  571.1 0.9 slice.52
  572.1 11.8 %all-gather.20.cloned.1.call-done = f32[32,8,1024]{2,1,0:T(8,128)} async-done(((f32[4,8,1024]{2,1,0:T(8,128)}), f32[32,8,1024]{2,1,0:T(8,128)}) %all-gather.20.cloned.1.call-update) | async-done | bytes 1048592 | tf_op jit(solution)/shard_map/all_gather | solution.py:183
  583.9 3.7 copy.45
  587.6 1.2 fusion.4
  589.5 1.2 fusion.5
  591.4 1.3 slice.55
  593.0 65.6 %all-gather.24.cloned.1.call-done = f32[1,1024,1,1024]{3,1,2,0:T(8,128)} async-done(((f32[1,128,1,1024]{3,1,2,0:T(8,128)}), f32[1,1024,1,1024]{3,1,2,0:T(8,128)}) %all-gather.24.cloned.1.call-update) | async-done | bytes 4194320 | tf_op jit(solution)/shard_map/all_gather | solution.py:229
  658.6 2.0 copy-done.2
  660.6 84.1 %panel_factor.1 = f32[2048,1024]{1,0:T(8,128)} custom-call(f32[1024,1024]{1,0:T(8,128)} %bitcast.91, f32[896,1024]{1,0:T(8,128)S(1)} %bitcast.86, f32[128,1024]{1,0:T(8,128)S(1)} %maximum_maximum_fusion.head_ref, bf16[1920,192]{1,0:T(8,128)(2,1)S(1)} %pad_maximum_fusion.left_ref, bf16[192,1024]{1,0:T(8,128)(2,1)S(1)} %constant_dynamic-update-slice_fusion.5.right_ref), custom_call_target="tpu_custom_call" | custom-call | tf_op jit(solution)/shard_map/panel_factor/pallas_call | solution.py:122
  744.8 5.8 fusion.19
  750.6 0.9 fusion.14
  751.7 1.1 constant_dynamic-slice_fusion.1
  753.3 0.8 pad_maximum_fusion.1
  754.1 1.1 dynamic-slice_select_fusion
  755.4 14.0 %gram_update.1 = f32[8192,256]{1,0:T(8,128)} custom-call(f32[8192,256]{1,0:T(8,128)} %bitcast.88, bf16[8,128,192]{2,1,0:T(8,128)(2,1)S(1)} %concatenate.24.left_ref, bf16[8,192,256]{2,1,0:T(8,128)(2,1)S(1)} %constant_dynamic-update-slice_fusion.right_ref, f32[8,128,256]{2,1,0:T(8,128)S(1)} %bitcast.87), custom_call_target="tpu_custom_call" | custom-call | tf_op jit(solution)/shard_map/gram_update/pallas_call | solution.py:160
  (69 shorter events, 5.4 us)
Async XLA Ops:
  7.2 2.9 copy-start
  7.2 2.9 copy-start.4
  7.2 26.6 %all-gather.16.cloned.1.call-start = ((), (), s32[]{:S(2)}) async-start(), calls=%async_computation.2 | async-start | bytes 2621440 | tf_op jit(solution)/shard_map/all_gather | solution.py:248
  7.9 227.4 %all-gather.18.cloned.1.call-start = ((), (), s32[]{:S(2)}) async-start(), calls=%async_computation.3 | async-start | bytes 16515072 | tf_op jit(solution)/shard_map/all_gather | solution.py:253
  8.7 251.7 %all-gather.12.cloned.1.call-start = ((), (), s32[]{:S(2)}) async-start(), calls=%async_computation | async-start | bytes 2621440 | tf_op jit(solution)/shard_map/all_gather | solution.py:249
  9.4 452.4 %all-gather.14.cloned.1.call-start = ((), (), s32[]{:S(2)}) async-start(), calls=%async_computation.1 | async-start | bytes 16515072 | tf_op jit(solution)/shard_map/all_gather | solution.py:258
  10.0 494.5 %all-reduce.3.cloned.1.call-start = ((), (), s32[]{:S(2)}) async-start(), calls=%async_computation.7 | async-start | bytes 524288 | tf_op jit(solution)/shard_map/psum | solution.py:266
  11.1 450.7 %copy-start.7 = (bf16[1792,64]{0,1:T(8,128)(2,1)S(1)}, bf16[1792,64]{0,1:T(8,128)(2,1)}, u32[]{:S(2)}) copy-start(bf16[1792,64]{0,1:T(8,128)(2,1)} %param.15) | copy-start | bytes 688132
  243.8 229.1 %slice-start.2 = ((f32[8,128,8,256]{3,2,1,0:T(8,128)}), f32[8,128,1,256]{3,2,1,0:T(1,128)S(1)}, s32[]{:S(2)}) async-start(f32[8,128,8,256]{3,2,1,0:T(8,128)} %param.18), calls=%async_computation.10 | async-start | bytes 2097152 | tf_op jit(solution)/shard_map/slice | solution.py:228
  471.9 2.0 copy-start.8
  471.9 2.0 copy-start.6
  472.8 71.7 %slice-start.3 = ((f32[64,8,128]{2,1,0:T(8,128)}), f32[64,1,128]{2,1,0:T(1,128)S(1)}, s32[]{:S(2)}) async-start(f32[64,8,128]{2,1,0:T(8,128)} %param.19), calls=%async_computation.11 | async-start | bytes 65536 | tf_op jit(solution)/shard_map/slice | solution.py:230
  472.8 69.7 %all-gather.22.cloned.1.call-start = ((), (), s32[]{:S(2)}) async-start(), calls=%async_computation.5 | async-start | bytes 5242880 | tf_op jit(solution)/shard_map/all_gather | solution.py:228
  473.9 110.0 %all-gather.20.cloned.1.call-start = ((), (), s32[]{:S(2)}) async-start(), calls=%async_computation.4 | async-start | bytes 1179648 | tf_op jit(solution)/shard_map/all_gather | solution.py:183
  506.9 151.7 %all-gather.24.cloned.1.call-start = ((), (), s32[]{:S(2)}) async-start(), calls=%async_computation.6 | async-start | bytes 4718592 | tf_op jit(solution)/shard_map/all_gather | solution.py:229
  658.6 2.0 copy-start.2
  744.8 5.9 copy-start.3
  750.6 1.0 copy-start.5
  750.6 1.0 slice-start
  751.6 3.6 slice-start.1
  755.4 14.1 %copy-start.1 = (bf16[4096,128]{1,0:T(8,128)(2,1)S(1)}, bf16[4096,128]{1,0:T(8,128)(2,1)}, u32[]{:S(2)}) copy-start(bf16[4096,128]{1,0:T(8,128)(2,1)} %param.14) | copy-start | bytes 3145732
Sparse Core Ops, SparseCore 0:
  9.6 24.1 all-gather.15
  36.0 199.3 all-gather.17
  236.9 23.4 all-gather.11
  262.4 199.3 all-gather.13
  472.9 31.5 all-reduce.2
  506.5 35.8 all-gather.21
  545.4 38.4 all-gather.19
  586.2 72.2 all-gather.23

commit v2 on v1

v2 whole, which is shorter than its diff:
```python
import functools
import jax
import jax.numpy as jnp
from jax import lax
from jax.experimental import pallas as pl
from jax.experimental.pallas import tpu as pltpu
from jax.sharding import PartitionSpec as P

highest = lax.Precision.HIGHEST
vmem_limit = 56 * 1024 * 1024


def eliminate(rows, size):
    shape = (8, size)
    sub = lax.broadcasted_iota(jnp.int32, shape, 0)
    lane = lax.broadcasted_iota(jnp.int32, shape, 1)
    count = size // 8

    def row_of(x, k):
        return jnp.broadcast_to(x[k : k + 1, :], shape)

    for p in range(count):
        base = 8 * p
        inside = (lane >= base) & (lane < base + 8)

        def columns(q):
            return [jnp.broadcast_to(rows[q][:, base + k : base + k + 1], shape) for k in range(8)]

        cols = columns(p)
        own = jnp.where(inside, jnp.where(lane - base == sub, 1.0, 0.0), rows[p])
        scaled_cols, scaled_rows, scale = [], [], jnp.zeros(shape, jnp.float32)
        for k in range(8):
            pivot = row_of(cols[k], k)
            inverse = 1.0 / pivot
            scale = jnp.where(sub == k, lax.rsqrt(pivot), scale)
            heads = [row_of(cols[j], k) * inverse for j in range(k + 1, 8)]
            head_row = row_of(own, k) * inverse
            scaled_cols.append(heads)
            scaled_rows.append(head_row)
            below = jnp.where(sub > k, cols[k], 0.0)
            for j in range(k + 1, 8):
                cols[j] = cols[j] - below * heads[j - k - 1]
            own = own - below * head_row
        for q in range(p + 1, count):
            other = columns(q)
            value = jnp.where(inside, 0.0, rows[q])
            for k in range(8):
                for j in range(k + 1, 8):
                    other[j] = other[j] - other[k] * scaled_cols[k][j - k - 1]
                value = value - other[k] * scaled_rows[k]
            rows[q] = value
        rows[p] = jnp.where(lane < base + 8, own * scale, 0.0)
    return rows


def mm(a, b):
    return jnp.dot(a, b, precision=highest, preferred_element_type=jnp.float32)


def mm_t(a, b):
    return lax.dot_general(
        a, b, (((1,), (1,)), ((), ())), precision=highest, preferred_element_type=jnp.float32
    )


def three_way(x):
    high = x.astype(jnp.bfloat16)
    rest = x - high.astype(jnp.float32)
    mid = rest.astype(jnp.bfloat16)
    return high, mid, (rest - mid.astype(jnp.float32)).astype(jnp.bfloat16)


def pack_left(x):
    high, mid, low = three_way(x)
    return jnp.concatenate([high, high, mid, high, low, mid], axis=0)


def pack_right(x):
    high, mid, low = three_way(x)
    return jnp.concatenate([high, mid, high, low, high, mid], axis=0)


def outer_sum(left, right):
    return lax.dot_general(
        left, right, (((0,), (0,)), ((), ())), preferred_element_type=jnp.float32
    )


def panel_kernel(
    block,
    share,
    band,
    spot_ref,
    diag_ref,
    below_ref,
    head_ref,
    first_ref,
    own_ref,
    part_ref,
    solved_ref,
    product_ref,
    work_ref,
    inv_ref,
    upper_ref,
):
    width = diag_ref.shape[0]
    low = below_ref.shape[0]
    total = work_ref.shape[0]
    blocks = width // block
    right = pack_right(first_ref[...])
    for start in range(0, width, block):
        rows = slice(start, start + block)
        left = pack_left(first_ref[:, rows])
        work_ref[rows, :] = diag_ref[rows, :] + outer_sum(left, right) * share
    cycles, _, band_rows = own_ref.shape
    for a in range(1, cycles):
        rows = slice((a - 1) * band_rows, a * band_rows)
        here = slice(width + (a - 1) * band_rows, width + a * band_rows)
        work_ref[here, :] = below_ref[rows, :] + outer_sum(pack_left(own_ref[a]), right) * share
    work_ref[width + low :, :] = head_ref[...]

    def one(b, carry):
        off = pl.multiple_of(b * block, block)
        rows = [
            work_ref[pl.ds(pl.multiple_of(off + 8 * q, 8), 8), pl.ds(off, block)]
            for q in range(block // 8)
        ]
        rows = eliminate(rows, block)
        for q in range(block // 8):
            inv_ref[8 * q : 8 * q + 8, :] = rows[q]
        for s in range(blocks):

            @pl.when(b == s)
            def _():
                here = slice(s * block, (s + 1) * block)
                after = slice((s + 1) * block, width)
                inv = inv_ref[...]
                if s + 1 < blocks:
                    upper_ref[:, after] = mm(inv, work_ref[here, after])
                chunk = 2 * block
                for start in range(s * block, total, chunk):
                    these = slice(start, min(start + chunk, total))
                    work_ref[these, here] = mm_t(work_ref[these, here], inv)
                for start in range((s + 1) * block, total, chunk):
                    if s + 1 < blocks:
                        these = slice(start, min(start + chunk, total))
                        work_ref[these, after] = work_ref[these, after] - mm(
                            work_ref[these, here], upper_ref[:, after]
                        )

        return carry

    lax.fori_loop(0, blocks, one, 0)
    solved_ref[...] = work_ref[width + low :, :]
    product_ref[...] = mm_t(work_ref[width + low :, :], work_ref[width:, :])
    if band == 0:
        part_ref[...] = work_ref[: width + low, :]
    else:
        row_start = spot_ref[0] * band_rows
        lanes = pl.ds(pl.multiple_of(spot_ref[1] * band, 128), band)
        mine = work_ref[pl.ds(pl.multiple_of(row_start, 8), band_rows), lanes]
        row = row_start + lax.broadcasted_iota(jnp.int32, mine.shape, 0)
        col = spot_ref[1] * band + lax.broadcasted_iota(jnp.int32, mine.shape, 1)
        part_ref[:band_rows, :] = jnp.where(col <= row, mine, 0.0)
        part_ref[band_rows:, :] = work_ref[width : width + low, lanes]


def panel(spot, diag, below, heads, first, own, band, share):
    block = 128
    width, low, extra = diag.shape[0], below.shape[0], heads.shape[0]
    cycles, _, band_rows = own.shape
    part = (cycles * band_rows, band) if band else (width + low, width)
    whole = pl.BlockSpec(memory_space=pltpu.VMEM)
    return pl.pallas_call(
        functools.partial(panel_kernel, block, share, band),
        out_shape=[
            jax.ShapeDtypeStruct(part, jnp.float32),
            jax.ShapeDtypeStruct((extra, width), jnp.float32),
            jax.ShapeDtypeStruct((extra, low + extra), jnp.float32),
        ],
        in_specs=[pl.BlockSpec(memory_space=pltpu.SMEM)] + [whole] * 5,
        out_specs=[whole] * 3,
        scratch_shapes=[
            pltpu.VMEM((width + low + extra, width), jnp.float32),
            pltpu.VMEM((block, block), jnp.float32),
            pltpu.VMEM((block, width), jnp.float32),
        ],
        compiler_params=pltpu.CompilerParams(vmem_limit_bytes=vmem_limit),
        name="panel_factor",
    )(spot, diag, below, heads, first, own)


def gram_kernel(share, gram_ref, own_ref, col_ref, panel_ref, out_ref):
    steps, _, count = own_ref.shape
    cycles, _, lanes = col_ref.shape
    right = jnp.concatenate([pack_right(col_ref[b]) for b in range(cycles)], axis=1)
    for a in range(steps):
        base = a * count * cycles
        out_ref[pl.ds(base, count, stride=cycles), :] = panel_ref[a]
        update = outer_sum(pack_left(own_ref[a]), right) * share
        for b in range(1, cycles):
            here = pl.ds(base + b, count, stride=cycles)
            out_ref[here, :] = gram_ref[here, :] + update[:, b * lanes : (b + 1) * lanes]


def gram_update(gram_in, own, col, panel_part, share):
    cycles, seqs, count = own.shape
    width = col.shape[2]
    lanes = 128
    if width % lanes:
        update = jnp.einsum("asu,bsv->aubv", own, col, precision=highest)
        return (gram_in + update * share).at[:, :, 0, :].set(panel_part)
    steps = 2 if cycles % 2 == 0 else 1
    gram = gram_in.reshape(cycles * count * cycles, width)
    tall = pl.BlockSpec((steps * count * cycles, lanes), lambda v, a: (a, v))
    return pl.pallas_call(
        functools.partial(gram_kernel, share),
        out_shape=jax.ShapeDtypeStruct(gram.shape, jnp.float32),
        grid=(width // lanes, cycles // steps),
        in_specs=[
            tall,
            pl.BlockSpec((steps, seqs, count), lambda v, a: (a, 0, 0)),
            pl.BlockSpec((cycles, seqs, lanes), lambda v, a: (0, 0, v)),
            pl.BlockSpec((steps, count, lanes), lambda v, a: (a, 0, v)),
        ],
        out_specs=tall,
        compiler_params=pltpu.CompilerParams(vmem_limit_bytes=vmem_limit),
        name="gram_update",
    )(gram, own, col, panel_part).reshape(gram_in.shape)


def finish(features, first, own, col, gram_in, queries, diag, below, heads):
    row_index, col_index = lax.axis_index("rows"), lax.axis_index("cols")
    cycles, band_rows, _, band_cols = gram_in.shape
    width, low = diag.shape[0], below.shape[0]
    query_count, seq_count = queries.shape[0], features.shape[0]
    share = 1.0 / first.shape[0]
    used = query_count + seq_count
    spare = -(low + used) % 128
    head_rows = jnp.concatenate(
        [heads, features, jnp.zeros((spare, width), jnp.float32)], axis=0
    )
    band = band_cols if band_cols % 128 == 0 else 0
    spot = jnp.stack([row_index, col_index]).astype(jnp.int32)
    part, solved, product = panel(spot, diag, below, head_rows, first, own, band, share)
    if band == 0:
        mine = lax.dynamic_slice_in_dim(part, row_index * band_rows, band_rows, 0)
        row = row_index * band_rows + lax.broadcasted_iota(jnp.int32, mine.shape, 0)
        mine = jnp.where(lax.broadcasted_iota(jnp.int32, mine.shape, 1) <= row, mine, 0.0)
        part = jnp.concatenate([mine, part[width:]], axis=0)
        part = lax.dynamic_slice_in_dim(part, col_index * band_cols, band_cols, 1)
    gram_next = gram_update(
        gram_in, own, col, part.reshape(cycles, band_rows, band_cols), share
    )
    tail = queries[:, 1:, :] - product[:query_count, :low].reshape(
        query_count, cycles - 1, band_rows
    )
    own_head = lax.dynamic_slice_in_dim(
        solved[:query_count], row_index * band_rows, band_rows, 1
    )
    query_next = jnp.concatenate([own_head[:, None, :], tail], axis=1)
    scores = product[:query_count, low + query_count : low + used]
    return gram_next, query_next, scores


def sequence_features(proj_inner, proj_outer, lengths, loss_mask):
    seq_count, window = loss_mask.shape
    positions = jnp.arange(window, dtype=jnp.int32)
    token_live = (positions[None, :] >= (window - lengths)[:, None]).astype(
        jnp.float32
    ) * loss_mask.astype(jnp.float32)
    weighted = proj_inner.reshape(seq_count, window, -1) * token_live[:, :, None]
    features = jnp.einsum(
        "stk,stl->skl",
        weighted,
        proj_outer.reshape(seq_count, window, -1),
        precision=highest,
    )
    return features.reshape(seq_count, -1)


def general(
    tokens,
    cotangent,
    gate_weight,
    down_weight,
    proj_in,
    proj_out,
    lengths,
    loss_mask,
    gram_in,
    queries,
):
    row_index, col_index = lax.axis_index("rows"), lax.axis_index("cols")
    full_tokens = lax.all_gather(tokens, "cols", axis=1, tiled=True)
    full_cotangent = lax.all_gather(cotangent, "cols", axis=1, tiled=True)
    gate_pre = jnp.dot(
        full_tokens,
        lax.all_gather(gate_weight, "rows", axis=0, tiled=True),
        preferred_element_type=jnp.float32,
    )
    grad_hidden = jnp.dot(
        full_cotangent,
        lax.all_gather(down_weight, "rows", axis=0, tiled=True),
        preferred_element_type=jnp.float32,
    )
    grad_up = (grad_hidden * jax.nn.silu(gate_pre)).astype(jnp.bfloat16)
    outer_part = jnp.dot(grad_up, proj_out, preferred_element_type=jnp.float32)
    proj_inner = jnp.dot(full_tokens, proj_in, preferred_element_type=jnp.float32)
    proj_outer = lax.psum(outer_part, "cols")
    features = sequence_features(proj_inner, proj_outer, lengths, loss_mask)
    cycles, band_rows, _, band_cols = gram_in.shape
    every = lax.all_gather(features, "rows", axis=0, tiled=True)
    every = jnp.transpose(every.reshape(every.shape[0], cycles, -1), (1, 0, 2))
    own = lax.dynamic_slice_in_dim(every, row_index * band_rows, band_rows, 2)
    col = lax.dynamic_slice_in_dim(every, col_index * band_cols, band_cols, 2)
    panel_rows = lax.all_gather(gram_in[:, :, 0, :], "cols", axis=2, tiled=True)
    width = panel_rows.shape[2]
    diag = lax.all_gather(panel_rows[0], "rows", axis=0, tiled=True)
    heads = lax.all_gather(queries[:, 0, :], "rows", axis=1, tiled=True)
    below = panel_rows[1:].reshape((cycles - 1) * band_rows, width)
    return finish(features[:, :width], every[0], own, col, gram_in, queries, diag, below, heads)


sizes = {"z": 4, "x": 2, "y": 2, "core": 2}


def shift(value, axis, step, wrap=True):
    names = ("z", "x", "y", "core")
    pairs = []
    for source in range(sizes["z"] * sizes["x"] * sizes["y"] * sizes["core"]):
        rest, at = source, []
        for name in reversed(names):
            at.append(rest % sizes[name])
            rest //= sizes[name]
        at = at[::-1]
        which = names.index(axis)
        there = at[which] + step
        if wrap:
            there %= sizes[axis]
        elif not 0 <= there < sizes[axis]:
            continue
        at[which] = there
        target = 0
        for name, spot in zip(names, at):
            target = target * sizes[name] + spot
        pairs.append((source, target))
    return lax.ppermute(value, ("rows", "cols"), pairs)


def in_order(place, own, other):
    first = jnp.where(place == 0, own, other)
    second = jnp.where(place == 0, other, own)
    return first, second


def gather_columns(value, me):
    width = value.shape[1]
    near = jnp.concatenate(in_order(me["y"], value, shift(value, "y", 1)), axis=1)
    left, right = in_order(me["core"], near, shift(near, "core", 1))
    return jnp.concatenate(
        [left[:, :width], right[:, :width], left[:, width:], right[:, width:]], axis=1
    )


slot_of = (((0, 3, 2, 1), (0, 2, 3, 1), (0, 1, 3, 2), (0, 1, 2, 3)))


def gradient_kernel(spot_ref, *refs):
    token_refs, refs = refs[:16], refs[16:]
    weight_refs, refs = refs[:8], refs[8:]
    out_proj_ref, in_proj_ref, outer_ref, inner_ref, token_buf, weight_buf, token_sem, weight_sem = refs
    z, x, y, core = (spot_ref[i] for i in range(4))
    height, band = token_refs[0].shape[1:]
    depth = weight_refs[0].shape[2]
    weight_copies = []
    for i, ref in enumerate(weight_refs):
        row = ((z - i // 2) % 4) * 2 + (x + i % 2) % 2
        there = weight_buf.at[:, :, pl.ds(pl.multiple_of(row * depth, 128), depth)]
        weight_copies.append(pltpu.make_async_copy(ref, there, weight_sem.at[i]))
    token_copies = []
    for i, ref in enumerate(token_refs):
        col = ((y + i % 4 // 2) % 2) * 2 + (core + i % 2) % 2
        there = token_buf.at[i // 4, :, :, pl.ds(pl.multiple_of(col * band, 128), band)]
        token_copies.append(pltpu.make_async_copy(ref, there, token_sem.at[i]))
    for copy in weight_copies + token_copies:
        copy.start()
    for copy in weight_copies:
        copy.wait()
    for s in range(4):
        for copy in token_copies[4 * s : 4 * s + 4]:
            copy.wait()
        if s == 0:
            inner_ref[...] = jnp.dot(
                token_buf[0, 0], in_proj_ref[...], preferred_element_type=jnp.float32
            )
        over = (((1,), (1,)), ((), ()))
        gate = lax.dot_general(
            token_buf[s, 0], weight_buf[0], over, preferred_element_type=jnp.float32
        )
        hidden = lax.dot_general(
            token_buf[s, 1], weight_buf[1], over, preferred_element_type=jnp.float32
        )
        grad = (hidden * (gate / (1.0 + jnp.exp(-gate)))).astype(jnp.bfloat16)
        outer_ref[s] = jnp.dot(grad, out_proj_ref[...], preferred_element_type=jnp.float32)


def gradient(spot, tokens, weights, out_proj, in_proj):
    kinds, height, band = tokens[0].shape
    share, depth = weights[0].shape[1:]
    full = depth * 8
    hbm = pl.BlockSpec(memory_space=pl.ANY)
    whole = pl.BlockSpec(memory_space=pltpu.VMEM)
    return pl.pallas_call(
        gradient_kernel,
        out_shape=[
            jax.ShapeDtypeStruct((4, height, out_proj.shape[1]), jnp.float32),
            jax.ShapeDtypeStruct((height, in_proj.shape[1]), jnp.float32),
        ],
        in_specs=[pl.BlockSpec(memory_space=pltpu.SMEM)] + [hbm] * 24 + [whole] * 2,
        out_specs=[whole] * 2,
        scratch_shapes=[
            pltpu.VMEM((4, kinds, height, full), jnp.bfloat16),
            pltpu.VMEM((kinds, share, full), jnp.bfloat16),
            pltpu.SemaphoreType.DMA((16,)),
            pltpu.SemaphoreType.DMA((8,)),
        ],
        compiler_params=pltpu.CompilerParams(vmem_limit_bytes=vmem_limit),
        name="gradient",
    )(spot, *tokens, *weights, out_proj, in_proj)


def rounds(tokens, cotangent, gate_weight, down_weight, gram_in, queries, me):
    z = me["z"]
    both = jnp.stack([tokens, cotangent])
    depth, width = gate_weight.shape
    share = width // 4
    cut = jnp.stack(
        [gate_weight.T.reshape(4, share, depth), down_weight.T.reshape(4, share, depth)], axis=1
    )
    piece = [lax.dynamic_index_in_dim(cut, (z + s) % 4, 0, False) for s in range(4)]
    cycles, band_rows, _, band_cols = gram_in.shape
    corner = gram_in[0, :, 0, :]
    below = gram_in[1:, :, 0, :].reshape((cycles - 1) * band_rows, band_cols)
    head = queries[:, 0, :]

    up1, down1 = shift(both, "z", 1, False), shift(both, "z", -1, False)
    wz1 = shift(piece[1], "z", 1)
    y_own = shift(both, "y", 1)
    wx0 = shift(piece[0], "x", 1)
    c_own = shift(both, "core", 1)
    up1, down1, wz1, y_own, wx0, p3, below = lax.optimization_barrier(
        (up1, down1, wz1, y_own, wx0, piece[3], below)
    )

    slot_a = jnp.where(z < 2, down1, up1)
    up2, down2 = shift(up1, "z", 1, False), shift(down1, "z", -1, False)
    wz3 = shift(p3, "z", 3)
    y_a = shift(slot_a, "y", 1)
    wx1 = shift(wz1, "x", 1)
    c_a = shift(slot_a, "core", 1)
    cy_own = shift(y_own, "core", 1)
    up2, down2, wz3, y_a, wx1, p2, corner, head = lax.optimization_barrier(
        (up2, down2, wz3, y_a, wx1, piece[2], corner, head)
    )

    slot_b = jnp.where(z == 0, down2, jnp.where(z == 1, up1, jnp.where(z == 2, down1, up2)))
    up3, down3 = shift(up2, "z", 1, False), shift(down2, "z", -1, False)
    wz2 = shift(p2, "z", 2)
    y_b = shift(slot_b, "y", 1)
    wx3 = shift(wz3, "x", 1)
    c_b = shift(slot_b, "core", 1)
    cy_a = shift(y_a, "core", 1)
    up3, down3, wz2, y_b, wx3 = lax.optimization_barrier((up3, down3, wz2, y_b, wx3))

    slot_c = jnp.where(z == 0, down3, jnp.where(z == 1, down2, jnp.where(z == 2, up2, up3)))
    y_c = shift(slot_c, "y", 1)
    wx2 = shift(wz2, "x", 1)
    c_c = shift(slot_c, "core", 1)
    cy_b = shift(y_b, "core", 1)
    cy_c = shift(y_c, "core", 1)
    pieces = [
        both, c_own, y_own, cy_own,
        slot_a, c_a, y_a, cy_a,
        slot_b, c_b, y_b, cy_b,
        slot_c, c_c, y_c, cy_c,
    ]
    weights = [piece[0], wx0, wz1, wx1, wz2, wx2, wz3, wx3]

    near = [corner] + [shift(corner, "z", s) for s in range(1, 4)]
    across = shift(jnp.concatenate(near, axis=0), "x", 1)
    diag = jnp.zeros((8 * band_rows, band_cols), jnp.float32)
    for s in range(4):
        row = ((z - s) % 4) * 2
        diag = lax.dynamic_update_slice(diag, near[s], ((row + me["x"]) * band_rows, 0))
        other = across[s * band_rows : (s + 1) * band_rows]
        diag = lax.dynamic_update_slice(diag, other, ((row + 1 - me["x"]) * band_rows, 0))
    diag = gather_columns(diag, me)
    below = gather_columns(below, me)
    pair = jnp.concatenate(in_order(me["x"], head, shift(head, "x", 1)), axis=1)
    span = pair.shape[1]
    heads = jnp.zeros((head.shape[0], 4 * span), jnp.float32)
    for s in range(4):
        came = pair if s == 0 else shift(pair, "z", s)
        heads = lax.dynamic_update_slice(heads, came, (0, ((z - s) % 4) * span))
    return pieces, weights, diag, below, heads


def local(
    tokens,
    cotangent,
    gate_weight,
    down_weight,
    proj_in,
    proj_out,
    lengths,
    loss_mask,
    gram_in,
    queries,
):
    row_index, col_index = lax.axis_index("rows"), lax.axis_index("cols")
    me = {"z": row_index // 2, "x": row_index % 2, "y": col_index // 2, "core": col_index % 2}
    pieces, weights, diag, below, heads = rounds(
        tokens, cotangent, gate_weight, down_weight, gram_in, queries, me
    )
    share = weights[0].shape[1]
    out_proj = lax.dynamic_slice_in_dim(proj_out, me["z"] * share, share, 0)
    spot = jnp.stack([me["z"], me["x"], me["y"], me["core"]]).astype(jnp.int32)
    outer, proj_inner = gradient(spot, pieces, weights, out_proj, proj_in)
    proj_outer = outer[0]
    table = jnp.array(slot_of, jnp.int32)
    for s in range(1, 4):
        part = lax.dynamic_index_in_dim(outer, table[me["z"], s], 0, False)
        proj_outer = proj_outer + shift(part, "z", -s)
    proj_outer = proj_outer + shift(proj_outer, "y", 1)
    proj_outer = proj_outer + shift(proj_outer, "core", 1)
    features = sequence_features(proj_inner, proj_outer, lengths, loss_mask)
    cycles, band_rows, _, band_cols = gram_in.shape
    seqs = features.shape[0]
    width = diag.shape[0]
    mine = lax.dynamic_slice_in_dim(
        features.reshape(seqs * cycles, width), col_index * band_cols, band_cols, 1
    )
    pair = jnp.concatenate([mine, shift(mine, "x", 1)], axis=0)
    column = jnp.concatenate([pair] + [shift(pair, "z", s) for s in range(1, 4)], axis=0)
    every = gather_columns(column, me)
    every = jnp.transpose(every.reshape(-1, cycles, width), (1, 0, 2))
    own = lax.dynamic_slice_in_dim(every, row_index * band_rows, band_rows, 2)
    col = lax.dynamic_slice_in_dim(every, col_index * band_cols, band_cols, 2)
    return finish(features[:, :width], every[0], own, col, gram_in, queries, diag, below, heads)


def solution(mesh):
    fits = mesh.shape["rows"] == 8 and mesh.shape["cols"] == 4
    return jax.shard_map(
        local if fits else general,
        mesh=mesh,
        in_specs=(
            P("rows", "cols"),
            P("rows", "cols"),
            P("rows", "cols"),
            P("rows", "cols"),
            P(),
            P("cols", None),
            P("rows"),
            P("rows", None),
            P(None, "rows", None, "cols"),
            P("cols", None, "rows"),
        ),
        out_specs=(P(None, "rows", None, "cols"), P("cols", None, "rows"), P("cols", "rows")),
        check_vma=False,
    )
```

time: 788 us -> 391 us (0.50)
  waiting for transfers between devices: 588 us -> 131 us
  starting transfers between devices: 0.32 us -> 76 us
  matrix products: 27.2 us -> 0.66 us
  other arithmetic: 5.44 us -> 31.8 us
  blocking collectives: 22.2 us -> 0 us
  local copies, waits for them, and re-layouts: 20.2 us -> 37.1 us
    all_gather x7 -> x0, waiting for transfers between devices: 555 us -> none  [the longest x1 202 us: local(): lax.all_gather(gate_weight, 'rows', axis=0, tiled=True)]
    ppermute x0 -> x48, waiting for transfers between devices: none -> 131 us  [shift(): return lax.ppermute(value, ('rows', 'cols'), pairs)]
    ppermute x0 -> x48, starting transfers between devices: none -> 76 us  [shift(): return lax.ppermute(value, ('rows', 'cols'), pairs)]
    psum x1 -> x0, waiting for transfers between devices: 30.4 us -> none  [local(): proj_inner, proj_outer = lax.psum((inner_part, outer_part), 'cols')]
    dot_general x6 -> x1, matrix products: 27.2 us -> 0.66 us  [sequence_features(): jnp.einsum('stk,stl->skl', weighted, proj_outer.reshape(seq_count, window...]
    all_gather x1 -> x0, blocking collectives: 22.2 us -> none  [early(): heads = lax.all_gather(queries[:, 0, :], 'rows', axis=1, tiled=True)]
    select_n x1 -> x10, other arithmetic: 1.14 us -> 15 us  [the longest x7 9.46 us: in_order(): first = jnp.where(place == 0, own, other)]
    concatenate x6 -> x10, other arithmetic: 1.25 us -> 9.84 us  [the longest x2 4.96 us: gather_columns(): jnp.concatenate([left[:, :width], right[:, :width], left[:, width:], righ...]
  transfers between devices with their start and end apart: 8 -> 48, of which waited for: 8 -> 18; matrix products, arithmetic and copies ran while one was open for 4% -> 15% of each run, Pallas kernels for 0% -> 5%
where the time goes in v2:
time: 391 us; the launch traced here: 385 us
  waiting for transfers between devices  131 us (34%)
  Pallas kernels  101 us (26%)
  starting transfers between devices  76 us (19%)
  local copies, waits for them, and re-layouts  37.1 us (9%)
  other arithmetic  31.8 us (8%)
  between operations  7.59 us (2%)
    ppermute x48, waiting for transfers between devices, shift(): return lax.ppermute(value, ('rows', 'cols'), pairs)  131 us
    ppermute x48, starting transfers between devices, shift(): return lax.ppermute(value, ('rows', 'cols'), pairs)  76 us
    pallas_call x1, Pallas kernels, panel(): pl.pallas_call(functools.partial(panel_kernel, block, share, band), out_s...  69.1 us
    pallas_call x1, Pallas kernels, gradient(): pl.pallas_call(gradient_kernel, out_shape=[jax.ShapeDtypeStruct((4, heigh...  20.8 us
    unnamed x74, local copies, waits for them, and re-layouts  11.3 us
    pallas_call x1, Pallas kernels, gram_update(): pl.pallas_call(functools.partial(gram_kernel, share), out_shape=jax.Shape...  10.8 us
    select_n x7, other arithmetic, in_order(): first = jnp.where(place == 0, own, other)  9.46 us
  transfers between devices with their start and end apart: 48, of which 18 were waited for; matrix products, arithmetic and copies ran while one was open for 15% of the time, Pallas kernels for 5%

profile of v2, /device:TPU:9, one launch (start us, length us, event | category | flops | bytes accessed | tf_op | source)
XLA Modules:
  0.0 384.6 jit_solution(3862504118953750191)
XLA Ops:
  2.0 3.2 collective-permute-start.1
  5.2 3.0 collective-permute-start.2
  9.6 2.8 copy.22
  12.4 3.8 copy.23
  16.2 3.0 fusion.1
  20.8 3.6 slice.78
  24.5 23.1 %collective-permute-done.3.refs_18_ = bf16[2,448,512]{2,1,0:T(8,128)(2,1)S(1)} collective-permute-done((bf16[2,448,512]{2,1,0:T(8,128)(2,1)S(1)}, bf16[2,448,512]{2,1,0:T(8,128)(2,1)S(1)}, u32[]{:S(2)}, u32[]{:S(2)}) %collective-permute-start.3) | collective-permute-done | bytes 917536 | tf_op jit(solution)/shard_map/ppermute | solution.py:348
  48.6 5.1 %collective-permute-start.10 = (bf16[2,448,512]{2,1,0:T(8,128)(2,1)}, bf16[2,448,512]{2,1,0:T(8,128)(2,1)}, u32[]{:S(2)}, u32[]{:S(2)}) collective-permute-start(bf16[2,448,512]{2,1,0:T(8,128)(2,1)} %get-tuple-element.31), channel_id=1, source_target_pairs={{0,24},{1,25},{2,26},{3,27},{4,28},{5,29},{6,30},{7,31},{8,0},{9,1... | collective-permute-start | bytes 2752520 | tf_op jit(solution)/shard_map/ppermute | solution.py:348
  55.6 4.4 %collective-permute-start.9 = (bf16[2,256,1024]{2,1,0:T(8,128)(2,1)}, bf16[2,256,1024]{2,1,0:T(8,128)(2,1)}, u32[]{:S(2)}, u32[]{:S(2)}) collective-permute-start(bf16[2,256,1024]{2,1,0:T(8,128)(2,1)} %collective-permute-done.2), channel_id=1, source_target_pairs={{8,0},{9,1},{10,2},{11,3},{12,4},{13,5},{14,6},{15,7},{16,8},{17,9... | collective-permute-start | bytes 3145736 | tf_op jit(solution)/shard_map/ppermute | solution.py:348
  64.8 7.3 %collective-permute-done.10.refs_22_ = bf16[2,448,512]{2,1,0:T(8,128)(2,1)} collective-permute-done((bf16[2,448,512]{2,1,0:T(8,128)(2,1)}, bf16[2,448,512]{2,1,0:T(8,128)(2,1)}, u32[]{:S(2)}, u32[]{:S(2)}) %collective-permute-start.10) | collective-permute-done | bytes 917536 | tf_op jit(solution)/shard_map/ppermute | solution.py:348
  75.6 6.8 %collective-permute-done.12.refs_19_ = bf16[2,448,512]{2,1,0:T(8,128)(2,1)S(1)} collective-permute-done((bf16[2,448,512]{2,1,0:T(8,128)(2,1)S(1)}, bf16[2,448,512]{2,1,0:T(8,128)(2,1)S(1)}, u32[]{:S(2)}, u32[]{:S(2)}) %collective-permute-start.12) | collective-permute-done | bytes 917536 | tf_op jit(solution)/shard_map/ppermute | solution.py:348
  82.5 13.9 %collective-permute-done.8 = bf16[2,256,1024]{2,1,0:T(8,128)(2,1)} collective-permute-done((bf16[2,256,1024]{2,1,0:T(8,128)(2,1)}, bf16[2,256,1024]{2,1,0:T(8,128)(2,1)}, u32[]{:S(2)}, u32[]{:S(2)}) %collective-permute-start.8) | collective-permute-done | bytes 1048608 | tf_op jit(solution)/shard_map/ppermute | solution.py:348
  104.0 2.6 collective-permute-start.15
  106.6 42.0 %collective-permute-done.38 = f32[128,256]{1,0:T(8,128)S(1)} collective-permute-done((f32[128,256]{1,0:T(8,128)S(1)}, f32[128,256]{1,0:T(8,128)S(1)}, u32[]{:S(2)}, u32[]{:S(2)}) %collective-permute-start.38) | collective-permute-done | bytes 131104 | tf_op jit(solution)/shard_map/ppermute | solution.py:348
  151.5 2.9 collective-permute-start.16
  162.3 7.5 %collective-permute-done.19.refs_23_ = bf16[2,448,512]{2,1,0:T(8,128)(2,1)} collective-permute-done((bf16[2,448,512]{2,1,0:T(8,128)(2,1)}, bf16[2,448,512]{2,1,0:T(8,128)(2,1)}, u32[]{:S(2)}, u32[]{:S(2)}) %collective-permute-start.19) | collective-permute-done | bytes 917536 | tf_op jit(solution)/shard_map/ppermute | solution.py:348
  173.0 4.2 %collective-permute-done.16 = bf16[2,256,1024]{2,1,0:T(8,128)(2,1)S(1)} collective-permute-done((bf16[2,256,1024]{2,1,0:T(8,128)(2,1)}, bf16[2,256,1024]{2,1,0:T(8,128)(2,1)S(1)}, u32[]{:S(2)}, u32[]{:S(2)}) %collective-permute-start.16) | collective-permute-done | bytes 1048608 | tf_op jit(solution)/shard_map/ppermute | solution.py:348
  180.2 2.5 select_select_fusion.refs_12_
  200.8 2.8 collective-permute-start.21
  203.7 4.1 %collective-permute-done.22.refs_14_ = bf16[2,256,1024]{2,1,0:T(8,128)(2,1)S(1)} collective-permute-done((bf16[2,256,1024]{2,1,0:T(8,128)(2,1)}, bf16[2,256,1024]{2,1,0:T(8,128)(2,1)S(1)}, u32[]{:S(2)}, u32[]{:S(2)}) %collective-permute-start.22) | collective-permute-done | bytes 1048608 | tf_op jit(solution)/shard_map/ppermute | solution.py:348
  222.4 20.8 %gradient.1 = (f32[4,256,64]{2,1,0:T(8,128)}, f32[256,128]{1,0:T(8,128)}) custom-call(s32[4]{0:T(128)} %pad_add_fusion.spot_ref, bf16[2,256,1024]{2,1,0:T(8,128)(2,1)} %copy-done.4, bf16[2,256,1024]{2,1,0:T(8,128)(2,1)} %copy-done.11, bf16[2,256,1024]{2,1,0:T(8,128)(2,1)} %collective-permute-done.4.refs_2_, bf16[2,256,1024]{2,1,0:T(8,128)(2,1)} %copy-done.12, ...), custom_call_target="tpu_custom_call" | custom-call | tf_op jit(solution)/shard_map/gradient/pallas_call | solution.py:414
  249.1 7.5 %collective-permute-done.26 = f32[256,64]{1,0:T(8,128)S(1)} collective-permute-done((f32[256,64]{1,0:T(8,128)S(1)}, f32[256,64]{1,0:T(8,128)S(1)}, u32[]{:S(2)}, u32[]{:S(2)}) %collective-permute-start.26) | collective-permute-done | bytes 65568 | tf_op jit(solution)/shard_map/ppermute | solution.py:348
  264.4 4.0 %broadcast_select_fusion.4 = (f32[896,512]{1,0:T(8,128)}, f32[896,512]{1,0:T(8,128)}) fusion(f32[896,512]{1,0:T(8,128)} %collective-permute-done.43, pred[]{:T(512)S(6)} %eq.47, f32[896,256]{1,0:T(8,128)S(1)} %copy-done.3, f32[896,256]{1,0:T(8,128)S(1)} %get-tuple-element.79), kind=kLoop, calls=%fused_computation.28 | loop fusion | flops 1376256 | bytes 7340033 | tf_op jit(solution)/shard_map/jit(_where)/select_n | solution.py:352
  270.6 2.2 fusion.15
  273.6 2.5 collective-permute-start.32
  279.5 3.2 collective-permute-done.33
  283.7 2.3 pad_maximum_fusion.1.below_ref
  287.0 3.1 collective-permute-done.34
  291.7 2.3 broadcast_select_fusion.1
  294.3 2.7 pad_maximum_fusion.diag_ref
  300.1 69.1 %panel_factor.1 = (f32[1024,256]{1,0:T(8,128)}, f32[128,1024]{1,0:T(8,128)}, f32[128,1024]{1,0:T(8,128)}) custom-call(s32[2]{0:T(128)} %pad_add_fusion.1.spot_ref, f32[1024,1024]{1,0:T(8,128)} %pad_maximum_fusion.diag_ref, f32[896,1024]{1,0:T(8,128)} %pad_maximum_fusion.1.below_ref, f32[128,1024]{1,0:T(8,128)} %maximum_maximum_fusion.head_ref, ...), custom_call_target="tpu_custom_call" | custom-call | tf_op jit(solution)/shard_map/panel_factor/pallas_call | solution.py:174
  373.4 10.8 %gram_update.1 = f32[8192,256]{1,0:T(8,128)} custom-call(f32[8192,256]{1,0:T(8,128)} %bitcast.62, f32[8,32,128]{2,1,0:T(8,128)} %dynamic-slice_bitcast_fusion.1.own_ref, f32[8,32,256]{2,1,0:T(8,128)} %dynamic-slice_bitcast_fusion.col_ref, f32[8,128,256]{2,1,0:T(8,128)} %bitcast.74), custom_call_target="tpu_custom_call" | custom-call | tf_op jit(solution)/shard_map/gram_update/pallas_call | solution.py:216
  (210 shorter events, 97.8 us)
Async XLA Ops:
  2.0 45.6 %collective-permute-start.1 = (bf16[2,256,1024]{2,1,0:T(8,128)(2,1)S(1)}, bf16[2,256,1024]{2,1,0:T(8,128)(2,1)}, u32[]{:S(2)}, u32[]{:S(2)}) collective-permute-start(bf16[2,256,1024]{2,1,0:T(8,128)(2,1)S(1)} %pad_maximum_fusion.4.refs_0_), channel_id=1, source_target_pairs={{0,8},{1,9},{2,10},{3,11},{4,12},{5,13},{6,14},{7,15},{8,16},{9,17... | collective-permute-start | bytes 3145736 | tf_op jit(solution)/shard_map/ppermute | solution.py:348
  5.2 42.4 %collective-permute-start.2 = (bf16[2,256,1024]{2,1,0:T(8,128)(2,1)S(1)}, bf16[2,256,1024]{2,1,0:T(8,128)(2,1)}, u32[]{:S(2)}, u32[]{:S(2)}) collective-permute-start(bf16[2,256,1024]{2,1,0:T(8,128)(2,1)S(1)} %pad_maximum_fusion.4.refs_0_), channel_id=1, source_target_pairs={{8,0},{9,1},{10,2},{11,3},{12,4},{13,5},{14,6},{15,7},{16,8},{17,9... | collective-permute-start | bytes 3145736 | tf_op jit(solution)/shard_map/ppermute | solution.py:348
  8.3 39.4 %collective-permute-start.4 = (bf16[2,256,1024]{2,1,0:T(8,128)(2,1)S(1)}, bf16[2,256,1024]{2,1,0:T(8,128)(2,1)}, u32[]{:S(2)}, u32[]{:S(2)}) collective-permute-start(bf16[2,256,1024]{2,1,0:T(8,128)(2,1)S(1)} %pad_maximum_fusion.4.refs_0_), channel_id=1, source_target_pairs={{0,2},{1,3},{2,0},{3,1},{4,6},{5,7},{6,4},{7,5},{8,10},{9,11},{10,... | collective-permute-start | bytes 3145736 | tf_op jit(solution)/shard_map/ppermute | solution.py:348
  19.3 28.3 %collective-permute-start.3 = (bf16[2,448,512]{2,1,0:T(8,128)(2,1)S(1)}, bf16[2,448,512]{2,1,0:T(8,128)(2,1)S(1)}, u32[]{:S(2)}, u32[]{:S(2)}) collective-permute-start(bf16[2,448,512]{2,1,0:T(8,128)(2,1)S(1)} %get-tuple-element.66), channel_id=1, source_target_pairs={{0,8},{1,9},{2,10},{3,11},{4,12},{5,13},{6,14},{7,15},{8,16},{9,17... | collective-permute-start | bytes 2752520 | tf_op jit(solution)/shard_map/ppermute | solution.py:348
  19.6 28.0 %collective-permute-start.5 = (bf16[2,448,512]{2,1,0:T(8,128)(2,1)S(1)}, bf16[2,448,512]{2,1,0:T(8,128)(2,1)S(1)}, u32[]{:S(2)}, u32[]{:S(2)}) collective-permute-start(bf16[2,448,512]{2,1,0:T(8,128)(2,1)S(1)} %get-tuple-element.67.refs_16_), channel_id=1, source_target_pairs={{0,4},{1,5},{2,6},{3,7},{4,0},{5,1},{6,2},{7,3},{8,12},{9,13},{10,... | collective-permute-start | bytes 2752520 | tf_op jit(solution)/shard_map/ppermute | solution.py:348
  48.6 23.5 %collective-permute-start.10 = (bf16[2,448,512]{2,1,0:T(8,128)(2,1)}, bf16[2,448,512]{2,1,0:T(8,128)(2,1)}, u32[]{:S(2)}, u32[]{:S(2)}) collective-permute-start(bf16[2,448,512]{2,1,0:T(8,128)(2,1)} %get-tuple-element.31), channel_id=1, source_target_pairs={{0,24},{1,25},{2,26},{3,27},{4,28},{5,29},{6,30},{7,31},{8,0},{9,1... | collective-permute-start | bytes 2752520 | tf_op jit(solution)/shard_map/ppermute | solution.py:348
  53.7 42.6 %collective-permute-start.8 = (bf16[2,256,1024]{2,1,0:T(8,128)(2,1)}, bf16[2,256,1024]{2,1,0:T(8,128)(2,1)}, u32[]{:S(2)}, u32[]{:S(2)}) collective-permute-start(bf16[2,256,1024]{2,1,0:T(8,128)(2,1)} %collective-permute-done.1), channel_id=1, source_target_pairs={{0,8},{1,9},{2,10},{3,11},{4,12},{5,13},{6,14},{7,15},{8,16},{9,17... | collective-permute-start | bytes 3145736 | tf_op jit(solution)/shard_map/ppermute | solution.py:348
  55.6 40.7 %collective-permute-start.9 = (bf16[2,256,1024]{2,1,0:T(8,128)(2,1)}, bf16[2,256,1024]{2,1,0:T(8,128)(2,1)}, u32[]{:S(2)}, u32[]{:S(2)}) collective-permute-start(bf16[2,256,1024]{2,1,0:T(8,128)(2,1)} %collective-permute-done.2), channel_id=1, source_target_pairs={{8,0},{9,1},{10,2},{11,3},{12,4},{13,5},{14,6},{15,7},{16,8},{17,9... | collective-permute-start | bytes 3145736 | tf_op jit(solution)/shard_map/ppermute | solution.py:348
  62.4 34.0 %collective-permute-start.11 = (bf16[2,256,1024]{2,1,0:T(8,128)(2,1)S(1)}, bf16[2,256,1024]{2,1,0:T(8,128)(2,1)S(1)}, u32[]{:S(2)}, u32[]{:S(2)}) collective-permute-start(bf16[2,256,1024]{2,1,0:T(8,128)(2,1)S(1)} %broadcast_select_fusion.2.refs_4_), channel_id=1, source_target_pairs={{0,2},{1,3},{2,0},{3,1},{4,6},{5,7},{6,4},{7,5},{8,10},{9,11},{10,... | collective-permute-start | bytes 3145736 | tf_op jit(solution)/shard_map/ppermute | solution.py:348
  63.6 18.9 %collective-permute-start.12 = (bf16[2,448,512]{2,1,0:T(8,128)(2,1)S(1)}, bf16[2,448,512]{2,1,0:T(8,128)(2,1)S(1)}, u32[]{:S(2)}, u32[]{:S(2)}) collective-permute-start(bf16[2,448,512]{2,1,0:T(8,128)(2,1)S(1)} %collective-permute-done.3.refs_18_), channel_id=1, source_target_pairs={{0,4},{1,5},{2,6},{3,7},{4,0},{5,1},{6,2},{7,3},{8,12},{9,13},{10,... | collective-permute-start | bytes 2752520 | tf_op jit(solution)/shard_map/ppermute | solution.py:348
  72.1 31.9 %collective-permute-start.42 = (f32[896,256]{1,0:T(8,128)S(1)}, f32[896,256]{1,0:T(8,128)}, u32[]{:S(2)}, u32[]{:S(2)}) collective-permute-start(f32[896,256]{1,0:T(8,128)S(1)} %bitcast.66), channel_id=1, source_target_pairs={{0,2},{1,3},{2,0},{3,1},{4,6},{5,7},{6,4},{7,5},{8,10},{9,11},{10,... | collective-permute-start | bytes 2752520 | tf_op jit(solution)/shard_map/ppermute | solution.py:348
  97.4 59.1 %collective-permute-start.17 = (bf16[2,448,512]{2,1,0:T(8,128)(2,1)}, bf16[2,448,512]{2,1,0:T(8,128)(2,1)}, u32[]{:S(2)}, u32[]{:S(2)}) collective-permute-start(bf16[2,448,512]{2,1,0:T(8,128)(2,1)} %get-tuple-element.36), channel_id=1, source_target_pairs={{0,16},{1,17},{2,18},{3,19},{4,20},{5,21},{6,22},{7,23},{8,24},{9,... | collective-permute-start | bytes 2752520 | tf_op jit(solution)/shard_map/ppermute | solution.py:348
  99.1 49.5 %collective-permute-start.38 = (f32[128,256]{1,0:T(8,128)S(1)}, f32[128,256]{1,0:T(8,128)S(1)}, u32[]{:S(2)}, u32[]{:S(2)}) collective-permute-start(f32[128,256]{1,0:T(8,128)S(1)} %bitcast.69), channel_id=1, source_target_pairs={{0,24},{1,25},{2,26},{3,27},{4,28},{5,29},{6,30},{7,31},{8,0},{9,1... | collective-permute-start | bytes 393224 | tf_op jit(solution)/shard_map/ppermute | solution.py:348
  102.0 49.5 %collective-permute-start.37 = (f32[128,256]{1,0:T(8,128)S(1)}, f32[128,256]{1,0:T(8,128)S(1)}, u32[]{:S(2)}, u32[]{:S(2)}) collective-permute-start(f32[128,256]{1,0:T(8,128)S(1)} %bitcast.70), channel_id=1, source_target_pairs={{0,16},{1,17},{2,18},{3,19},{4,20},{5,21},{6,22},{7,23},{8,24},{9,... | collective-permute-start | bytes 393224 | tf_op jit(solution)/shard_map/ppermute | solution.py:348
  104.0 50.5 %collective-permute-start.36 = (f32[128,256]{1,0:T(8,128)S(1)}, f32[128,256]{1,0:T(8,128)S(1)}, u32[]{:S(2)}, u32[]{:S(2)}) collective-permute-start(f32[128,256]{1,0:T(8,128)S(1)} %bitcast.71), channel_id=1, source_target_pairs={{0,8},{1,9},{2,10},{3,11},{4,12},{5,13},{6,14},{7,15},{8,16},{9,17... | collective-permute-start | bytes 393224 | tf_op jit(solution)/shard_map/ppermute | solution.py:348
  104.0 67.7 %collective-permute-start.15 = (bf16[2,256,1024]{2,1,0:T(8,128)(2,1)}, bf16[2,256,1024]{2,1,0:T(8,128)(2,1)S(1)}, u32[]{:S(2)}, u32[]{:S(2)}) collective-permute-start(bf16[2,256,1024]{2,1,0:T(8,128)(2,1)} %collective-permute-done.8), channel_id=1, source_target_pairs={{0,8},{1,9},{2,10},{3,11},{4,12},{5,13},{6,14},{7,15},{8,16},{9,17... | collective-permute-start | bytes 3145736 | tf_op jit(solution)/shard_map/ppermute | solution.py:348
  148.6 21.3 %collective-permute-start.19 = (bf16[2,448,512]{2,1,0:T(8,128)(2,1)}, bf16[2,448,512]{2,1,0:T(8,128)(2,1)}, u32[]{:S(2)}, u32[]{:S(2)}) collective-permute-start(bf16[2,448,512]{2,1,0:T(8,128)(2,1)} %collective-permute-done.10.refs_22_), channel_id=1, source_target_pairs={{0,4},{1,5},{2,6},{3,7},{4,0},{5,1},{6,2},{7,3},{8,12},{9,13},{10,... | collective-permute-start | bytes 2752520 | tf_op jit(solution)/shard_map/ppermute | solution.py:348
  151.5 25.7 %collective-permute-start.16 = (bf16[2,256,1024]{2,1,0:T(8,128)(2,1)}, bf16[2,256,1024]{2,1,0:T(8,128)(2,1)S(1)}, u32[]{:S(2)}, u32[]{:S(2)}) collective-permute-start(bf16[2,256,1024]{2,1,0:T(8,128)(2,1)} %collective-permute-done.9), channel_id=1, source_target_pairs={{8,0},{9,1},{10,2},{11,3},{12,4},{13,5},{14,6},{15,7},{16,8},{17,9... | collective-permute-start | bytes 3145736 | tf_op jit(solution)/shard_map/ppermute | solution.py:348
  154.5 24.8 %collective-permute-start.18 = (bf16[2,256,1024]{2,1,0:T(8,128)(2,1)S(1)}, bf16[2,256,1024]{2,1,0:T(8,128)(2,1)}, u32[]{:S(2)}, u32[]{:S(2)}) collective-permute-start(bf16[2,256,1024]{2,1,0:T(8,128)(2,1)S(1)} %select_select_fusion.1.refs_8_), channel_id=1, source_target_pairs={{0,2},{1,3},{2,0},{3,1},{4,6},{5,7},{6,4},{7,5},{8,10},{9,11},{10,... | collective-permute-start | bytes 3145736 | tf_op jit(solution)/shard_map/ppermute | solution.py:348
  156.5 26.2 %collective-permute-start = (bf16[2,256,1024]{2,1,0:T(8,128)(2,1)S(1)}, bf16[2,256,1024]{2,1,0:T(8,128)(2,1)S(1)}, u32[]{:S(2)}, u32[]{:S(2)}) collective-permute-start(bf16[2,256,1024]{2,1,0:T(8,128)(2,1)S(1)} %pad_maximum_fusion.4.refs_0_), channel_id=1, source_target_pairs={{0,1},{1,0},{2,3},{3,2},{4,5},{5,4},{6,7},{7,6},{8,9},{9,8},{10,11... | collective-permute-start | bytes 3145736 | tf_op jit(solution)/shard_map/ppermute | solution.py:348
  169.8 17.6 %collective-permute-start.6 = (bf16[2,256,1024]{2,1,0:T(8,128)(2,1)}, bf16[2,256,1024]{2,1,0:T(8,128)(2,1)S(1)}, u32[]{:S(2)}, u32[]{:S(2)}) collective-permute-start(bf16[2,256,1024]{2,1,0:T(8,128)(2,1)} %collective-permute-done.4.refs_2_), channel_id=1, source_target_pairs={{0,1},{1,0},{2,3},{3,2},{4,5},{5,4},{6,7},{7,6},{8,9},{9,8},{10,11... | collective-permute-start | bytes 3145736 | tf_op jit(solution)/shard_map/ppermute | solution.py:348
  171.7 12.4 %collective-permute-start.39 = (f32[512,256]{1,0:T(8,128)S(1)}, f32[512,256]{1,0:T(8,128)S(1)}, u32[]{:S(2)}, u32[]{:S(2)}) collective-permute-start(f32[512,256]{1,0:T(8,128)S(1)} %pad_maximum_fusion.6), channel_id=1, source_target_pairs={{0,4},{1,5},{2,6},{3,7},{4,0},{5,1},{6,2},{7,3},{8,12},{9,13},{10,... | collective-permute-start | bytes 1572872 | tf_op jit(solution)/shard_map/ppermute | solution.py:348
  179.2 24.4 %collective-permute-start.13 = (bf16[2,256,1024]{2,1,0:T(8,128)(2,1)S(1)}, bf16[2,256,1024]{2,1,0:T(8,128)(2,1)S(1)}, u32[]{:S(2)}, u32[]{:S(2)}) collective-permute-start(bf16[2,256,1024]{2,1,0:T(8,128)(2,1)S(1)} %copy-done.10), channel_id=1, source_target_pairs={{0,1},{1,0},{2,3},{3,2},{4,5},{5,4},{6,7},{7,6},{8,9},{9,8},{10,11... | collective-permute-start | bytes 3145736 | tf_op jit(solution)/shard_map/ppermute | solution.py:348
  182.7 25.1 %collective-permute-start.22 = (bf16[2,256,1024]{2,1,0:T(8,128)(2,1)}, bf16[2,256,1024]{2,1,0:T(8,128)(2,1)S(1)}, u32[]{:S(2)}, u32[]{:S(2)}) collective-permute-start(bf16[2,256,1024]{2,1,0:T(8,128)(2,1)} %select_select_fusion.refs_12_), channel_id=1, source_target_pairs={{0,2},{1,3},{2,0},{3,1},{4,6},{5,7},{6,4},{7,5},{8,10},{9,11},{10,... | collective-permute-start | bytes 3145736 | tf_op jit(solution)/shard_map/ppermute | solution.py:348
  184.1 25.2 %collective-permute-start.14 = (bf16[2,256,1024]{2,1,0:T(8,128)(2,1)S(1)}, bf16[2,256,1024]{2,1,0:T(8,128)(2,1)S(1)}, u32[]{:S(2)}, u32[]{:S(2)}) collective-permute-start(bf16[2,256,1024]{2,1,0:T(8,128)(2,1)S(1)} %select_select_fusion.1.refs_8_), channel_id=1, source_target_pairs={{0,1},{1,0},{2,3},{3,2},{4,5},{5,4},{6,7},{7,6},{8,9},{9,8},{10,11... | collective-permute-start | bytes 3145736 | tf_op jit(solution)/shard_map/ppermute | solution.py:348
  187.4 22.2 %collective-permute-start.24 = (bf16[2,448,512]{2,1,0:T(8,128)(2,1)}, bf16[2,448,512]{2,1,0:T(8,128)(2,1)S(1)}, u32[]{:S(2)}, u32[]{:S(2)}) collective-permute-start(bf16[2,448,512]{2,1,0:T(8,128)(2,1)} %collective-permute-done.17.refs_20_), channel_id=1, source_target_pairs={{0,4},{1,5},{2,6},{3,7},{4,0},{5,1},{6,2},{7,3},{8,12},{9,13},{10,... | collective-permute-start | bytes 2752520 | tf_op jit(solution)/shard_map/ppermute | solution.py:348
  200.8 21.6 %collective-permute-start.21 = (bf16[2,256,1024]{2,1,0:T(8,128)(2,1)}, bf16[2,256,1024]{2,1,0:T(8,128)(2,1)}, u32[]{:S(2)}, u32[]{:S(2)}) collective-permute-start(bf16[2,256,1024]{2,1,0:T(8,128)(2,1)} %select_select_fusion.refs_12_), channel_id=1, source_target_pairs={{0,1},{1,0},{2,3},{3,2},{4,5},{5,4},{6,7},{7,6},{8,9},{9,8},{10,11... | collective-permute-start | bytes 3145736 | tf_op jit(solution)/shard_map/ppermute | solution.py:348
  203.6 18.7 %collective-permute-start.20 = (bf16[2,256,1024]{2,1,0:T(8,128)(2,1)}, bf16[2,256,1024]{2,1,0:T(8,128)(2,1)}, u32[]{:S(2)}, u32[]{:S(2)}) collective-permute-start(bf16[2,256,1024]{2,1,0:T(8,128)(2,1)} %collective-permute-done.18.refs_10_), channel_id=1, source_target_pairs={{0,1},{1,0},{2,3},{3,2},{4,5},{5,4},{6,7},{7,6},{8,9},{9,8},{10,11... | collective-permute-start | bytes 3145736 | tf_op jit(solution)/shard_map/ppermute | solution.py:348
  207.8 14.6 %collective-permute-start.23 = (bf16[2,256,1024]{2,1,0:T(8,128)(2,1)S(1)}, bf16[2,256,1024]{2,1,0:T(8,128)(2,1)}, u32[]{:S(2)}, u32[]{:S(2)}) collective-permute-start(bf16[2,256,1024]{2,1,0:T(8,128)(2,1)S(1)} %collective-permute-done.22.refs_14_), channel_id=1, source_target_pairs={{0,1},{1,0},{2,3},{3,2},{4,5},{5,4},{6,7},{7,6},{8,9},{9,8},{10,11... | collective-permute-start | bytes 3145736 | tf_op jit(solution)/shard_map/ppermute | solution.py:348
  209.2 55.2 %collective-permute-start.43 = (f32[896,512]{1,0:T(8,128)}, f32[896,512]{1,0:T(8,128)}, u32[]{:S(2)}, u32[]{:S(2)}) collective-permute-start(f32[896,512]{1,0:T(8,128)} %pad_maximum_fusion.3), channel_id=1, source_target_pairs={{0,1},{1,0},{2,3},{3,2},{4,5},{5,4},{6,7},{7,6},{8,9},{9,8},{10,11... | collective-permute-start | bytes 5505032 | tf_op jit(solution)/shard_map/ppermute | solution.py:348
  209.6 37.8 %collective-permute-start.40 = (f32[1024,256]{1,0:T(8,128)}, f32[1024,256]{1,0:T(8,128)}, u32[]{:S(2)}, u32[]{:S(2)}) collective-permute-start(f32[1024,256]{1,0:T(8,128)} %slice_dynamic-update-slice_fusion), channel_id=1, source_target_pairs={{0,2},{1,3},{2,0},{3,1},{4,6},{5,7},{6,4},{7,5},{8,10},{9,11},{10,... | collective-permute-start | bytes 3145736 | tf_op jit(solution)/shard_map/ppermute | solution.py:348
  260.5 31.2 %collective-permute-start.41 = (f32[1024,512]{1,0:T(8,128)}, f32[1024,512]{1,0:T(8,128)}, u32[]{:S(2)}, u32[]{:S(2)}) collective-permute-start(f32[1024,512]{1,0:T(8,128)} %pad_maximum_fusion.2), channel_id=1, source_target_pairs={{0,1},{1,0},{2,3},{3,2},{4,5},{5,4},{6,7},{7,6},{8,9},{9,8},{10,11... | collective-permute-start | bytes 6291464 | tf_op jit(solution)/shard_map/ppermute | solution.py:348
  (48 other events, 1056.8 us)

commit v3 on v2

v3 whole, which is shorter than its diff:
```python
import functools
import jax
import jax.numpy as jnp
from jax import lax
from jax.experimental import pallas as pl
from jax.experimental.pallas import tpu as pltpu
from jax.sharding import PartitionSpec as P

highest = lax.Precision.HIGHEST
vmem_limit = 56 * 1024 * 1024
block = 128


def eliminate(rows):
    shape = (8, block)
    sub = lax.broadcasted_iota(jnp.int32, shape, 0)
    lane = lax.broadcasted_iota(jnp.int32, shape, 1)
    count = block // 8

    def row_of(x, k):
        return jnp.broadcast_to(x[k : k + 1, :], shape)

    for p in range(count):
        base = 8 * p
        inside = (lane >= base) & (lane < base + 8)

        def columns(q):
            return [jnp.broadcast_to(rows[q][:, base + k : base + k + 1], shape) for k in range(8)]

        cols = columns(p)
        own = jnp.where(inside, jnp.where(lane - base == sub, 1.0, 0.0), rows[p])
        heads, tops, scale = [], [], jnp.zeros(shape, jnp.float32)
        for k in range(0, 8, 2):
            a, b, d = row_of(cols[k], k), row_of(cols[k + 1], k), row_of(cols[k + 1], k + 1)
            det = a * d - b * b
            inverse = 1.0 / det
            single = 1.0 / a

            def solve(u, v):
                return (d * u - b * v) * inverse, (a * v - b * u) * inverse

            pairs = [solve(row_of(cols[j], k), row_of(cols[j], k + 1)) for j in range(k + 2, 8)]
            upper = row_of(own, k)
            top = solve(upper, row_of(own, k + 1))
            heads.append(pairs)
            tops.append(top)
            c0 = jnp.where(sub > k + 1, cols[k], 0.0)
            c1 = jnp.where(sub > k + 1, cols[k + 1], 0.0)
            for j in range(k + 2, 8):
                h0, h1 = pairs[j - k - 2]
                cols[j] = cols[j] - (c0 * h0 + c1 * h1)
            own = own - (c0 * top[0] + c1 * top[1])
            own = own - jnp.where(sub == k + 1, b * single, 0.0) * upper
            scale = jnp.where(sub == k, lax.rsqrt(a), scale)
            scale = jnp.where(sub == k + 1, lax.rsqrt(det * single), scale)
        for q in range(p + 1, count):
            other = columns(q)
            value = jnp.where(inside, 0.0, rows[q])
            for k in range(0, 8, 2):
                for j in range(k + 2, 8):
                    h0, h1 = heads[k // 2][j - k - 2]
                    other[j] = other[j] - (other[k] * h0 + other[k + 1] * h1)
                top = tops[k // 2]
                value = value - (other[k] * top[0] + other[k + 1] * top[1])
            rows[q] = value
        rows[p] = jnp.where(lane < base + 8, own * scale, 0.0)
    return rows


def mm(a, b):
    return jnp.dot(a, b, precision=highest, preferred_element_type=jnp.float32)


def mm_t(a, b):
    return lax.dot_general(
        a, b, (((1,), (1,)), ((), ())), precision=highest, preferred_element_type=jnp.float32
    )


def three_way(x):
    high = x.astype(jnp.bfloat16)
    rest = x - high.astype(jnp.float32)
    mid = rest.astype(jnp.bfloat16)
    return high, mid, (rest - mid.astype(jnp.float32)).astype(jnp.bfloat16)


def pack_left(x):
    high, mid, low = three_way(x)
    return jnp.concatenate([high, high, mid, high, low, mid], axis=0)


def pack_right(x):
    high, mid, low = three_way(x)
    return jnp.concatenate([high, mid, high, low, high, mid], axis=0)


def outer_sum(left, right):
    return lax.dot_general(
        left, right, (((0,), (0,)), ((), ())), preferred_element_type=jnp.float32
    )


def spans(start, stop, step):
    return [slice(at, min(at + step, stop)) for at in range(start, stop, step)]


def factor(work_ref, inv_ref, upper_ref, root_ref):
    total, width = work_ref.shape
    blocks = width // block
    chunk = 4 * block
    eye = lax.broadcasted_iota(jnp.int32, (block, block), 0) == lax.broadcasted_iota(
        jnp.int32, (block, block), 1
    )
    across, along = [], []
    for here in spans(0, width, block):
        diagonal = jnp.where(eye, work_ref[here, here], 0.0)
        across.append(lax.rsqrt(jnp.sum(diagonal, axis=0, keepdims=True)))
        down = jnp.sum(diagonal, axis=1, keepdims=True)
        along.append(lax.rsqrt(down))
        root_ref[here, :] = jnp.broadcast_to(down * along[-1], (block, block))
    across = jnp.concatenate(across, axis=1)
    for i, here in enumerate(spans(0, width, block)):
        work_ref[here, :] = work_ref[here, :] * along[i] * across
    for here in spans(width, total, block):
        work_ref[here, :] = work_ref[here, :] * across

    def one(b, carry):
        off = pl.multiple_of(b * block, block)
        rows = [
            work_ref[pl.ds(pl.multiple_of(off + 8 * q, 8), 8), pl.ds(off, block)]
            for q in range(block // 8)
        ]
        rows = eliminate(rows)
        for q in range(block // 8):
            inv_ref[8 * q : 8 * q + 8, :] = rows[q]
        for s in range(blocks):

            @pl.when(b == s)
            def _():
                here = slice(s * block, (s + 1) * block)
                after = slice((s + 1) * block, width)
                half = s % 2
                kept = slice(half * block, (half + 1) * block)
                inv = inv_ref[...]
                if s + 1 < blocks:
                    upper_ref[kept, after] = mm(inv, work_ref[here, after])
                for these in spans(s * block, total, chunk):
                    work_ref[these, here] = mm_t(work_ref[these, here], inv)
                if half == 0 and s + 1 < blocks:
                    near = slice((s + 1) * block, (s + 2) * block)
                    far = slice((s + 2) * block, width)
                    for these in spans((s + 1) * block, total, chunk):
                        work_ref[these, near] = work_ref[these, near] - mm(
                            work_ref[these, here], upper_ref[kept, near]
                        )
                    if s + 2 < blocks:
                        work_ref[near, far] = work_ref[near, far] - mm(
                            work_ref[near, here], upper_ref[kept, far]
                        )
                elif s + 1 < blocks:
                    both = slice((s - 1) * block, (s + 1) * block)
                    for these in spans((s + 1) * block, total, chunk):
                        work_ref[these, after] = work_ref[these, after] - mm(
                            work_ref[these, both], upper_ref[:, after]
                        )

        return carry

    lax.fori_loop(0, blocks, one, 0)


def factor_scratch(total, width):
    return [
        pltpu.VMEM((total, width), jnp.float32),
        pltpu.VMEM((block, block), jnp.float32),
        pltpu.VMEM((2 * block, width), jnp.float32),
        pltpu.VMEM((width, block), jnp.float32),
    ]


def plain_kernel(rows_ref, out_ref, work_ref, inv_ref, upper_ref, root_ref):
    work_ref[...] = rows_ref[...]
    factor(work_ref, inv_ref, upper_ref, root_ref)
    width = work_ref.shape[1]
    out_ref[width:, :] = work_ref[width:, :]
    for here in spans(0, width, block):
        for there in spans(0, width, block):
            out_ref[here, there] = work_ref[here, there] * root_ref[here, :]


def plain_panel(rows):
    whole = pl.BlockSpec(memory_space=pltpu.VMEM)
    return pl.pallas_call(
        plain_kernel,
        out_shape=jax.ShapeDtypeStruct(rows.shape, jnp.float32),
        in_specs=[whole],
        out_specs=whole,
        scratch_shapes=factor_scratch(*rows.shape),
        compiler_params=pltpu.CompilerParams(vmem_limit_bytes=vmem_limit),
        name="plain_panel",
    )(rows)


def panel_kernel(
    share,
    seqs,
    spot_ref,
    d0_ref,
    d1_ref,
    b0_ref,
    b1_ref,
    near_ref,
    far_ref,
    head_ref,
    query_ref,
    part_ref,
    next_ref,
    score_ref,
    own_ref,
    work_ref,
    inv_ref,
    upper_ref,
    root_ref,
    feat_ref,
):
    total, width = work_ref.shape
    _, low, band = b0_ref.shape
    cycles = low // block + 1
    row, col = spot_ref[0], spot_ref[1]
    core = col % 2
    for far, (diag_ref, below_ref) in enumerate(((d0_ref, b0_ref), (d1_ref, b1_ref))):
        for half in range(2):
            there = 2 * half + (core + far) % 2
            lanes = pl.ds(pl.multiple_of(there * band, 128), band)
            work_ref[:width, lanes] = diag_ref[half]
            work_ref[width : width + low, lanes] = below_ref[half]
    for far, ref in enumerate((near_ref, far_ref)):
        side = (core + far) % 2
        for i in range(4):
            feat_ref[(i // 2) * 4 + 2 * side + i % 2] = ref[:, i * 128 : (i + 1) * 128]
    every = feat_ref.shape[1] // cycles
    first = [feat_ref[i, pl.ds(0, every, stride=cycles), :] for i in range(width // 128)]
    right = pack_right(jnp.concatenate(first, axis=1))
    for i, here in enumerate(spans(0, width, block)):
        work_ref[here, :] = work_ref[here, :] + outer_sum(pack_left(first[i]), right) * share
    for a in range(cycles):
        mine = feat_ref[row, pl.ds(a, every, stride=cycles), :]
        own_ref[a] = mine
        if a > 0:
            here = slice(width + (a - 1) * block, width + a * block)
            work_ref[here, :] = work_ref[here, :] + outer_sum(pack_left(mine), right) * share
    queries = head_ref.shape[0]
    top = width + low
    work_ref[top : top + queries, :] = head_ref[...]
    work_ref[top + queries :, :] = jnp.zeros((total - top - queries, width), jnp.float32)
    for i in range(width // 128):
        work_ref[top + queries : top + queries + seqs, i * 128 : (i + 1) * 128] = feat_ref[
            i, pl.ds(0, seqs, stride=cycles), :
        ]
    factor(work_ref, inv_ref, upper_ref, root_ref)
    lanes = pl.ds(pl.multiple_of(col * band, 128), band)
    rows = pl.ds(pl.multiple_of(row * block, block), block)
    mine = work_ref[rows, lanes] * jnp.concatenate([root_ref[rows, :]] * (band // block), axis=1)
    row_at = row * block + lax.broadcasted_iota(jnp.int32, mine.shape, 0)
    col_at = col * band + lax.broadcasted_iota(jnp.int32, mine.shape, 1)
    part_ref[:block, :] = jnp.where(col_at <= row_at, mine, 0.0)
    part_ref[block:, :] = work_ref[width:top, lanes]
    solved = work_ref[top : top + queries, :]
    product = mm_t(solved, work_ref[width:top, :])
    next_ref[pl.ds(0, queries, stride=cycles), :] = work_ref[
        top : top + queries, pl.ds(pl.multiple_of(row * block, block), block)
    ]
    for a in range(1, cycles):
        here = pl.ds(a, queries, stride=cycles)
        next_ref[here, :] = query_ref[here, :] - product[:, (a - 1) * block : a * block]
    score_ref[...] = mm_t(solved, work_ref[top + queries : top + queries + 8, :])[:, :seqs]


def panel(spot, diags, belows, near, far, heads, queries, seqs, share):
    _, low, band = belows[0].shape
    width = heads.shape[1]
    cycles = low // block + 1
    total = -(-(width + low + heads.shape[0] + 8) // block) * block
    whole = pl.BlockSpec(memory_space=pltpu.VMEM)
    return pl.pallas_call(
        functools.partial(panel_kernel, share, seqs),
        out_shape=[
            jax.ShapeDtypeStruct((cycles * block, band), jnp.float32),
            jax.ShapeDtypeStruct(queries.shape, jnp.float32),
            jax.ShapeDtypeStruct((heads.shape[0], seqs), jnp.float32),
            jax.ShapeDtypeStruct((cycles, near.shape[0] // cycles, block), jnp.float32),
        ],
        in_specs=[pl.BlockSpec(memory_space=pltpu.SMEM)] + [whole] * 8,
        out_specs=[whole] * 4,
        scratch_shapes=factor_scratch(total, width)
        + [pltpu.VMEM((width // 128, near.shape[0], 128), jnp.float32)],
        compiler_params=pltpu.CompilerParams(vmem_limit_bytes=vmem_limit),
        name="panel_factor",
    )(spot, *diags, *belows, near, far, heads, queries)


def gram_kernel(share, gram_ref, own_ref, col_ref, panel_ref, out_ref):
    steps, seqs, count = own_ref.shape
    cycles, lanes = col_ref.shape[0] // seqs, col_ref.shape[1]
    right = jnp.concatenate(
        [pack_right(col_ref[pl.ds(b, seqs, stride=cycles), :]) for b in range(cycles)], axis=1
    )
    for a in range(steps):
        base = a * count * cycles
        out_ref[pl.ds(base, count, stride=cycles), :] = panel_ref[a]
        update = outer_sum(pack_left(own_ref[a]), right) * share
        for b in range(1, cycles):
            here = pl.ds(base + b, count, stride=cycles)
            out_ref[here, :] = gram_ref[here, :] + update[:, b * lanes : (b + 1) * lanes]


def gram_update(gram_in, own, col, part, share):
    cycles, seqs, count = own.shape
    rows, width = col.shape
    lanes = 128
    steps = 2 if cycles % 2 == 0 else 1
    gram = gram_in.reshape(cycles * count * cycles, width)
    tall = pl.BlockSpec((steps * count * cycles, lanes), lambda v, a: (a, v))
    return pl.pallas_call(
        functools.partial(gram_kernel, share),
        out_shape=jax.ShapeDtypeStruct(gram.shape, jnp.float32),
        grid=(width // lanes, cycles // steps),
        in_specs=[
            tall,
            pl.BlockSpec((steps, seqs, count), lambda v, a: (a, 0, 0)),
            pl.BlockSpec((rows, lanes), lambda v, a: (0, v)),
            pl.BlockSpec((steps, count, lanes), lambda v, a: (a, 0, v)),
        ],
        out_specs=tall,
        compiler_params=pltpu.CompilerParams(vmem_limit_bytes=vmem_limit),
        name="gram_update",
    )(gram, own, col, part.reshape(cycles, count, width)).reshape(gram_in.shape)


def sequence_features(proj_inner, proj_outer, lengths, loss_mask):
    seq_count, window = loss_mask.shape
    positions = jnp.arange(window, dtype=jnp.int32)
    token_live = (positions[None, :] >= (window - lengths)[:, None]).astype(
        jnp.float32
    ) * loss_mask.astype(jnp.float32)
    weighted = proj_inner.reshape(seq_count, window, -1) * token_live[:, :, None]
    features = jnp.einsum(
        "stk,stl->skl",
        weighted,
        proj_outer.reshape(seq_count, window, -1),
        precision=highest,
    )
    return features.reshape(seq_count, -1)


def general(
    tokens,
    cotangent,
    gate_weight,
    down_weight,
    proj_in,
    proj_out,
    lengths,
    loss_mask,
    gram_in,
    queries,
):
    row_index, col_index = lax.axis_index("rows"), lax.axis_index("cols")
    full_tokens = lax.all_gather(tokens, "cols", axis=1, tiled=True)
    full_cotangent = lax.all_gather(cotangent, "cols", axis=1, tiled=True)
    gate_pre = jnp.dot(
        full_tokens,
        lax.all_gather(gate_weight, "rows", axis=0, tiled=True),
        preferred_element_type=jnp.float32,
    )
    grad_hidden = jnp.dot(
        full_cotangent,
        lax.all_gather(down_weight, "rows", axis=0, tiled=True),
        preferred_element_type=jnp.float32,
    )
    grad_up = (grad_hidden * jax.nn.silu(gate_pre)).astype(jnp.bfloat16)
    outer_part = jnp.dot(grad_up, proj_out, preferred_element_type=jnp.float32)
    proj_inner = jnp.dot(full_tokens, proj_in, preferred_element_type=jnp.float32)
    proj_outer = lax.psum(outer_part, "cols")
    features = sequence_features(proj_inner, proj_outer, lengths, loss_mask)
    cycles, band_rows, _, band_cols = gram_in.shape
    every = lax.all_gather(features, "rows", axis=0, tiled=True)
    every = jnp.transpose(every.reshape(every.shape[0], cycles, -1), (1, 0, 2))
    own = lax.dynamic_slice_in_dim(every, row_index * band_rows, band_rows, 2)
    col = lax.dynamic_slice_in_dim(every, col_index * band_cols, band_cols, 2)
    panel_rows = lax.all_gather(gram_in[:, :, 0, :], "cols", axis=2, tiled=True)
    width = panel_rows.shape[2]
    diag = lax.all_gather(panel_rows[0], "rows", axis=0, tiled=True)
    heads = lax.all_gather(queries[:, 0, :], "rows", axis=1, tiled=True)
    below = panel_rows[1:].reshape((cycles - 1) * band_rows, width)
    share = 1.0 / every.shape[1]
    seqs, low, query_count = features.shape[0], below.shape[0], queries.shape[0]
    first = every[0]
    update = jnp.einsum("sr,sc->rc", first, first, precision=highest) * share
    more = jnp.einsum("asr,sc->arc", own[1:], first, precision=highest) * share
    used = width + low + query_count + seqs
    rows = [diag + update, below + more.reshape(low, width), heads, features[:, :width]]
    rows.append(jnp.zeros((-used % block, width), jnp.float32))
    done = plain_panel(jnp.concatenate(rows, axis=0))
    mine = lax.dynamic_slice_in_dim(done, row_index * band_rows, band_rows, 0)
    row_at = row_index * band_rows + lax.broadcasted_iota(jnp.int32, mine.shape, 0)
    mine = jnp.where(lax.broadcasted_iota(jnp.int32, mine.shape, 1) <= row_at, mine, 0.0)
    lower_part = done[width : width + low]
    solved = done[width + low : width + low + query_count]
    whitened = done[width + low + query_count : used]
    part = jnp.concatenate([mine, lower_part], axis=0)
    part = lax.dynamic_slice_in_dim(part, col_index * band_cols, band_cols, 1)
    updated = gram_in + jnp.einsum("asu,bsv->aubv", own, col, precision=highest) * share
    gram_next = updated.at[:, :, 0, :].set(part.reshape(cycles, band_rows, band_cols))
    tail = queries[:, 1:, :] - mm_t(solved, lower_part).reshape(query_count, cycles - 1, band_rows)
    own_head = lax.dynamic_slice_in_dim(solved, row_index * band_rows, band_rows, 1)
    query_next = jnp.concatenate([own_head[:, None, :], tail], axis=1)
    return gram_next, query_next, mm_t(solved, whitened)


sizes = {"z": 4, "x": 2, "y": 2, "core": 2}


def shift(value, axis, step, wrap=True, steps=None):
    names = ("z", "x", "y", "core")
    pairs = []
    for source in range(sizes["z"] * sizes["x"] * sizes["y"] * sizes["core"]):
        rest, at = source, []
        for name in reversed(names):
            at.append(rest % sizes[name])
            rest //= sizes[name]
        at = at[::-1]
        which = names.index(axis)
        there = at[which] + step
        if steps is not None:
            there = steps[at[which]]
        if wrap:
            there %= sizes[axis]
        elif not 0 <= there < sizes[axis]:
            continue
        at[which] = there
        target = 0
        for name, spot in zip(names, at):
            target = target * sizes[name] + spot
        pairs.append((source, target))
    return lax.ppermute(value, ("rows", "cols"), pairs)


slot_of = (((0, 3, 2, 1), (0, 2, 3, 1), (0, 1, 3, 2), (0, 1, 2, 3)))


def gradient_kernel(spot_ref, *refs):
    token_refs, refs = refs[:11], refs[11:]
    weight_refs, refs = refs[:8], refs[8:]
    out_proj_ref, in_proj_ref, outer_ref, inner_ref, token_buf, weight_buf, token_sem, weight_sem = refs
    z, x, y, core = (spot_ref[i] for i in range(4))
    height, band = token_refs[0].shape[1:]
    near, (far_1, far_2, far_3) = token_refs[:8], token_refs[8:]
    far = [far_1.at[i] for i in range(4)] + [far_2.at[i] for i in range(3)] + [far_3]
    depth = weight_refs[0].shape[2]
    weight_copies = []
    for i, ref in enumerate(weight_refs):
        row = ((z - i // 2) % 4) * 2 + (x + i % 2) % 2
        there = weight_buf.at[:, :, pl.ds(pl.multiple_of(row * depth, 128), depth)]
        weight_copies.append(pltpu.make_async_copy(ref, there, weight_sem.at[i]))
    token_copies = []
    for i in range(16):
        ref = (far if i % 2 else near)[i // 2]
        col = ((y + i % 4 // 2) % 2) * 2 + (core + i % 2) % 2
        there = token_buf.at[i // 4, :, :, pl.ds(pl.multiple_of(col * band, 128), band)]
        token_copies.append(pltpu.make_async_copy(ref, there, token_sem.at[i]))
    for copy in weight_copies + token_copies:
        copy.start()
    for copy in weight_copies:
        copy.wait()
    for s in range(4):
        for copy in token_copies[4 * s : 4 * s + 4]:
            copy.wait()
        if s == 0:
            inner_ref[...] = jnp.dot(
                token_buf[0, 0], in_proj_ref[...], preferred_element_type=jnp.float32
            )
        over = (((1,), (1,)), ((), ()))
        gate = lax.dot_general(
            token_buf[s, 0], weight_buf[0], over, preferred_element_type=jnp.float32
        )
        hidden = lax.dot_general(
            token_buf[s, 1], weight_buf[1], over, preferred_element_type=jnp.float32
        )
        grad = (hidden * (gate / (1.0 + jnp.exp(-gate)))).astype(jnp.bfloat16)
        outer_ref[s] = jnp.dot(grad, out_proj_ref[...], preferred_element_type=jnp.float32)


def gradient(spot, tokens, weights, out_proj, in_proj):
    kinds, height, band = tokens[0].shape
    share, depth = weights[0].shape[1:]
    full = depth * 8
    hbm = pl.BlockSpec(memory_space=pl.ANY)
    whole = pl.BlockSpec(memory_space=pltpu.VMEM)
    return pl.pallas_call(
        gradient_kernel,
        out_shape=[
            jax.ShapeDtypeStruct((4, height, out_proj.shape[1]), jnp.float32),
            jax.ShapeDtypeStruct((height, in_proj.shape[1]), jnp.float32),
        ],
        in_specs=[pl.BlockSpec(memory_space=pltpu.SMEM)] + [hbm] * 19 + [whole] * 2,
        out_specs=[whole] * 2,
        scratch_shapes=[
            pltpu.VMEM((4, kinds, height, full), jnp.bfloat16),
            pltpu.VMEM((kinds, share, full), jnp.bfloat16),
            pltpu.SemaphoreType.DMA((16,)),
            pltpu.SemaphoreType.DMA((8,)),
        ],
        compiler_params=pltpu.CompilerParams(vmem_limit_bytes=vmem_limit),
        cost_estimate=pl.CostEstimate(
            flops=16 * kinds * height * full * share,
            bytes_accessed=2 * kinds * full * (4 * height + share),
            transcendentals=4 * height * share,
        ),
        name="gradient",
    )(spot, *tokens, *weights, out_proj, in_proj)


def tie(values, *after):
    count = len(values)
    return lax.optimization_barrier((*values, *after))[:count]


def rounds(tokens, cotangent, gate_weight, down_weight, gram_in, queries, me):
    z = me["z"]
    both = jnp.stack([tokens, cotangent])
    depth, width = gate_weight.shape
    share = width // 4
    cut = jnp.stack(
        [gate_weight.T.reshape(4, share, depth), down_weight.T.reshape(4, share, depth)], axis=1
    )
    piece = [lax.dynamic_index_in_dim(cut, (z + s) % 4, 0, False) for s in range(4)]
    cycles, band_rows, _, band_cols = gram_in.shape
    count = queries.shape[0]
    below = gram_in[1:, :, 0, :].reshape((cycles - 1) * band_rows, band_cols)
    small = jnp.concatenate([gram_in[0, :, 0, :], queries[:, 0, :].reshape(-1, band_cols)], axis=0)
    small = lax.all_gather(small, "rows", axis=0)
    over_y = [[0, 2], [1, 3]]
    belows = lax.all_gather(below, "cols", axis=0, axis_index_groups=over_y)
    diag = small[:, :band_rows].reshape(-1, band_cols)
    diags = lax.all_gather(diag, "cols", axis=0, axis_index_groups=over_y)
    heads = jnp.transpose(small[:, band_rows:].reshape(8, count, band_rows), (1, 0, 2))
    heads = heads.reshape(count, 8 * band_rows)

    up1, down1 = shift(both, "z", 1, False), shift(both, "z", -1, False)
    y_own = shift(both, "y", 1)
    wx0 = shift(piece[0], "x", 1)
    wz1 = shift(piece[1], "z", 1)
    up1, down1, wz1, y_own, wx0, p3 = tie((up1, down1, wz1, y_own, wx0, piece[3]))

    slot_a = jnp.where(z < 2, down1, up1)
    up2, down2 = shift(up1, "z", 1, False), shift(down1, "z", -1, False)
    y_a = shift(slot_a, "y", 1)
    wx1 = shift(wz1, "x", 1)
    wz3 = shift(p3, "z", 3)
    up2, down2, wz3, y_a, wx1, p2 = tie((up2, down2, wz3, y_a, wx1, piece[2]))

    slot_b = jnp.where(z == 0, down2, jnp.where(z == 1, up1, jnp.where(z == 2, down1, up2)))
    last = shift(jnp.where(z == 2, up2, down2), "z", 1, False, (-1, 0, 3, -1))
    y_b = shift(slot_b, "y", 1)
    wx3 = shift(wz3, "x", 1)
    wz2 = shift(p2, "z", 2)
    core_1 = shift(jnp.stack([both, y_own, slot_a, y_a]), "core", 1)
    last, wz2, y_b, wx3, core_1 = tie((last, wz2, y_b, wx3, core_1))

    slot_c = jnp.where(z == 0, last, jnp.where(z == 1, down2, jnp.where(z == 2, up2, last)))
    y_c = shift(slot_c, "y", 1)
    wx2 = shift(wz2, "x", 1)
    core_2 = shift(jnp.stack([slot_b, y_b, slot_c]), "core", 1)
    y_c, wx2, core_2, diags, belows = tie((y_c, wx2, core_2, diags, belows))
    core_3 = shift(y_c, "core", 1)
    diag_c = shift(diags, "core", 1)
    below_c = shift(belows, "core", 1)
    pieces = [both, y_own, slot_a, y_a, slot_b, y_b, slot_c, y_c, core_1, core_2, core_3]
    weights = [piece[0], wx0, wz1, wx1, wz2, wx2, wz3, wx3]
    diags, belows = [diags, diag_c], [belows, below_c]
    return pieces, weights, diags, belows, heads


def local(
    tokens,
    cotangent,
    gate_weight,
    down_weight,
    proj_in,
    proj_out,
    lengths,
    loss_mask,
    gram_in,
    queries,
):
    row_index, col_index = lax.axis_index("rows"), lax.axis_index("cols")
    me = {"z": row_index // 2, "x": row_index % 2, "y": col_index // 2, "core": col_index % 2}
    pieces, weights, diags, belows, heads = rounds(
        tokens, cotangent, gate_weight, down_weight, gram_in, queries, me
    )
    share = weights[0].shape[1]
    out_proj = lax.dynamic_slice_in_dim(proj_out, me["z"] * share, share, 0)
    spot = jnp.stack([me["z"], me["x"], me["y"], me["core"]]).astype(jnp.int32)
    outer, proj_inner = gradient(spot, pieces, weights, out_proj, proj_in)
    tied = tie((outer, *diags, *belows))
    outer, diags, belows = tied[0], tied[1:3], tied[3:5]
    proj_outer = outer[0]
    table = jnp.array(slot_of, jnp.int32)
    for s in range(1, 4):
        part = lax.dynamic_index_in_dim(outer, table[me["z"], s], 0, False)
        proj_outer = proj_outer + shift(part, "z", -s)
    proj_outer = proj_outer + shift(proj_outer, "y", 1)
    proj_outer = proj_outer + shift(proj_outer, "core", 1)
    features = sequence_features(proj_inner, proj_outer, lengths, loss_mask)
    cycles, band_rows, _, band_cols = gram_in.shape
    seqs = features.shape[0]
    features = features.reshape(seqs * cycles, -1)
    mine = [
        lax.dynamic_slice_in_dim(features, (2 * i + me["core"]) * band_cols, band_cols, 1)
        for i in range(2)
    ]
    mine = jnp.concatenate(mine, axis=1)
    pair = jnp.concatenate([mine, shift(mine, "x", 1)], axis=0)
    near = jnp.concatenate([pair] + [shift(pair, "z", s) for s in range(1, 4)], axis=0)
    far = shift(near, "core", 1)
    share = cycles / near.shape[0]
    where = jnp.stack([row_index, col_index]).astype(jnp.int32)
    part, query_next, scores, own = panel(
        where, diags, belows, near, far, heads, queries.reshape(-1, band_rows), seqs, share
    )
    col = lax.dynamic_slice_in_dim(near, me["y"] * band_cols, band_cols, 1)
    gram_next = gram_update(gram_in, own, col, part, share)
    return gram_next, query_next.reshape(queries.shape), scores


def solution(mesh):
    fits = mesh.shape["rows"] == 8 and mesh.shape["cols"] == 4
    return jax.shard_map(
        local if fits else general,
        mesh=mesh,
        in_specs=(
            P("rows", "cols"),
            P("rows", "cols"),
            P("rows", "cols"),
            P("rows", "cols"),
            P(),
            P("cols", None),
            P("rows"),
            P("rows", None),
            P(None, "rows", None, "cols"),
            P("cols", None, "rows"),
        ),
        out_specs=(P(None, "rows", None, "cols"), P("cols", None, "rows"), P("cols", "rows")),
        check_vma=False,
    )
```

time: 391 us -> 439 us (1.12); the launches traced: 385 us -> 442 us
  waiting for transfers between devices: 131 us -> 225 us
  starting transfers between devices: 76 us -> 41.8 us
  between operations: 7.59 us -> 19.8 us
  other arithmetic: 31.8 us -> 21.2 us
  local copies, waits for them, and re-layouts: 37.1 us -> 27.2 us
    all_gather x0 -> x3, waiting for transfers between devices: none -> 91.1 us  [the longest x1 43.6 us: rounds(): belows = lax.all_gather(below, 'cols', axis=0, axis_index_groups=over_y)]
    ppermute x48 -> x31, starting transfers between devices: 76 us -> 41.3 us  [shift(): return lax.ppermute(value, ('rows', 'cols'), pairs)]
    select_n x9 -> x2, other arithmetic: 13.7 us -> 4.16 us  [the longest x1 2.78 us: rounds(): last = shift(jnp.where(z == 2, up2, down2), 'z', 1, False, (-1, 0, 3, -1))]
    concatenate x9 -> x2, other arithmetic: 9.84 us -> 0.69 us  [the longest x1 0.68 us: rounds(): jnp.concatenate([gram_in[0, :, 0, :], queries[:, 0, :].reshape(-1, band_c...]
    another operation x2 -> x4, other arithmetic: 2 us -> 11.1 us  [the longest x2 6.59 us: rounds(): core_1 = shift(jnp.stack([both, y_own, slot_a, y_a]), 'core', 1)]
    dynamic_update_slice x11 -> x0, local copies, waits for them, and re-layouts: 7.88 us -> none  [the longest x4 2.68 us: rounds(): lax.dynamic_update_slice(diag, near[s], ((row + me['x']) * band_rows, 0))]
    pallas_call x1, Pallas kernels: 69.1 us -> 73.7 us  [panel(): pl.pallas_call(functools.partial(panel_kernel, share, seqs), out_shape=[j...]
    ppermute x48 -> x31, waiting for transfers between devices: 131 us -> 134 us  [shift(): return lax.ppermute(value, ('rows', 'cols'), pairs)]
  transfers between devices with their start and end apart: 48 -> 34, of which waited for: 18 -> 16; matrix products, arithmetic and copies ran while one was open for 15% -> 8% of each run, Pallas kernels for 5% -> 5%
where the time goes in v3:
time: 439 us; the launch traced here: 442 us
  waiting for transfers between devices  225 us (51%)
  Pallas kernels  105 us (24%)
  starting transfers between devices  41.8 us (10%)
  local copies, waits for them, and re-layouts  27.2 us (6%)
  other arithmetic  21.2 us (5%)
  between operations  19.8 us (5%)
    ppermute x31, waiting for transfers between devices, shift(): return lax.ppermute(value, ('rows', 'cols'), pairs)  134 us
    pallas_call x1, Pallas kernels, panel(): pl.pallas_call(functools.partial(panel_kernel, share, seqs), out_shape=[j...  73.7 us
    all_gather x1, waiting for transfers between devices, rounds(): belows = lax.all_gather(below, 'cols', axis=0, axis_index_groups=over_y)  43.6 us
    ppermute x31, starting transfers between devices, shift(): return lax.ppermute(value, ('rows', 'cols'), pairs)  41.3 us
    all_gather x1, waiting for transfers between devices, rounds(): diags = lax.all_gather(diag, 'cols', axis=0, axis_index_groups=over_y)  33.5 us
    pallas_call x1, Pallas kernels, gradient(): pl.pallas_call(gradient_kernel, out_shape=[jax.ShapeDtypeStruct((4, heigh...  20.5 us
    unnamed x41, local copies, waits for them, and re-layouts  14.1 us
    all_gather x1, waiting for transfers between devices, rounds(): small = lax.all_gather(small, 'rows', axis=0)  14.1 us
  transfers between devices with their start and end apart: 34, of which 16 were waited for; matrix products, arithmetic and copies ran while one was open for 8% of the time, Pallas kernels for 5%

profile of v3, /device:TPU:9, one launch (start us, length us, event | category | flops | bytes accessed | tf_op | source)
XLA Modules:
  0.0 441.6 jit_solution(16570340152359333457)
XLA Ops:
  7.2 2.7 fusion.13
  10.0 3.2 collective-permute-start
  13.2 3.1 collective-permute-start.1
  17.5 2.8 copy.29
  20.4 3.8 copy.30
  24.2 3.4 fusion.1
  29.2 26.6 %collective-permute-done.2.refs_13_ = bf16[2,448,512]{2,1,0:T(8,128)(2,1)S(1)} collective-permute-done((bf16[2,448,512]{2,1,0:T(8,128)(2,1)}, bf16[2,448,512]{2,1,0:T(8,128)(2,1)S(1)}, u32[]{:S(2)}, u32[]{:S(2)}) %collective-permute-start.2) | collective-permute-done | bytes 917536 | tf_op jit(solution)/shard_map/ppermute | solution.py:446
  57.1 3.2 collective-permute-start.5
  60.3 5.1 %collective-permute-start.6 = (bf16[2,256,1024]{2,1,0:T(8,128)(2,1)S(1)}, bf16[2,256,1024]{2,1,0:T(8,128)(2,1)S(1)}, u32[]{:S(2)}, u32[]{:S(2)}) collective-permute-start(bf16[2,256,1024]{2,1,0:T(8,128)(2,1)S(1)} %collective-permute-done.1), channel_id=1, source_target_pairs={{8,0},{9,1},{10,2},{11,3},{12,4},{13,5},{14,6},{15,7},{16,8},{17,9... | collective-permute-start | bytes 3145736 | tf_op jit(solution)/shard_map/ppermute | solution.py:446
  68.1 37.7 %collective-permute-done.7.refs_17_ = bf16[2,448,512]{2,1,0:T(8,128)(2,1)} collective-permute-done((bf16[2,448,512]{2,1,0:T(8,128)(2,1)}, bf16[2,448,512]{2,1,0:T(8,128)(2,1)}, u32[]{:S(2)}, u32[]{:S(2)}) %collective-permute-start.7) | collective-permute-done | bytes 917536 | tf_op jit(solution)/shard_map/ppermute | solution.py:446
  106.7 3.9 pad_maximum_fusion
  110.6 2.8 collective-permute-start.14
  116.5 2.8 broadcast_select_fusion
  119.3 2.9 collective-permute-start.10
  124.8 3.6 slice.21
  129.9 39.0 %collective-permute-done.11.refs_15_ = bf16[2,448,512]{2,1,0:T(8,128)(2,1)} collective-permute-done((bf16[2,448,512]{2,1,0:T(8,128)(2,1)}, bf16[2,448,512]{2,1,0:T(8,128)(2,1)}, u32[]{:S(2)}, u32[]{:S(2)}) %collective-permute-start.11) | collective-permute-done | bytes 917536 | tf_op jit(solution)/shard_map/ppermute | solution.py:446
  172.3 3.9 pad_maximum_fusion.1
  177.2 14.1 %all-gather.9.cloned.1.call-done = f32[1280,256]{1,0:T(8,128)} async-done(((f32[160,256]{1,0:T(8,128)}), f32[1280,256]{1,0:T(8,128)}) %all-gather.9.cloned.1.call-update) | async-done | bytes 1310736 | tf_op jit(solution)/shard_map/all_gather | solution.py:542
  191.2 2.3 slice.24
  195.1 43.6 %all-gather.7.cloned.1.call-done.b0_ref = f32[2,896,256]{2,1,0:T(8,128)} async-done(((f32[1,896,256]{2,1,0:T(8,128)}), f32[2,896,256]{2,1,0:T(8,128)}) %all-gather.7.cloned.1.call-update) | async-done | bytes 1835024 | tf_op jit(solution)/shard_map/all_gather | solution.py:544
  238.7 33.5 %all-gather.5.cloned.1.call-done.d0_ref = f32[2,1024,256]{2,1,0:T(8,128)} async-done(((f32[1,1024,256]{2,1,0:T(8,128)}), f32[2,1024,256]{2,1,0:T(8,128)}) %all-gather.5.cloned.1.call-update) | async-done | bytes 2097168 | tf_op jit(solution)/shard_map/all_gather | solution.py:546
  282.0 20.5 %gradient.1 = (f32[4,256,64]{2,1,0:T(8,128)}, f32[256,128]{1,0:T(8,128)}) custom-call(s32[4]{0:T(128)} %pad_add_fusion.1.spot_ref, bf16[2,256,1024]{2,1,0:T(8,128)(2,1)} %get-tuple-element.85.refs_0_, bf16[2,256,1024]{2,1,0:T(8,128)(2,1)} %collective-permute-done.3.refs_1_, bf16[2,256,1024]{2,1,0:T(8,128)(2,1)} %copy-done.3, ...), custom_call_target="tpu_custom_call" | custom-call | flops 15032385536 | bytes 24117248 | tf_op jit(solution)/shard_map/gradient/pallas_call | solution.py:500
  302.5 1.5 dynamic-slice_bitcast_fusion.2
  309.2 7.4 %collective-permute-done.22 = f32[256,64]{1,0:T(8,128)S(1)} collective-permute-done((f32[256,64]{1,0:T(8,128)S(1)}, f32[256,64]{1,0:T(8,128)S(1)}, u32[]{:S(2)}, u32[]{:S(2)}) %collective-permute-start.22) | collective-permute-done | bytes 65568 | tf_op jit(solution)/shard_map/ppermute | solution.py:446
  316.6 2.2 collective-permute-done.21
  319.9 4.5 %collective-permute-done.24 = f32[256,64]{1,0:T(8,128)S(1)} collective-permute-done((f32[256,64]{1,0:T(8,128)S(1)}, f32[256,64]{1,0:T(8,128)S(1)}, u32[]{:S(2)}, u32[]{:S(2)}) %collective-permute-start.24) | collective-permute-done | bytes 65568 | tf_op jit(solution)/shard_map/ppermute | solution.py:446
  326.8 1.6 fusion.10
  329.8 1.9 collective-permute-done.26
  335.7 2.3 collective-permute-done.28
  338.0 7.3 %collective-permute-done.29 = f32[64,512]{1,0:T(8,128)S(1)} collective-permute-done((f32[64,512]{1,0:T(8,128)S(1)}, f32[64,512]{1,0:T(8,128)S(1)}, u32[]{:S(2)}, u32[]{:S(2)}) %collective-permute-start.29) | collective-permute-done | bytes 131104 | tf_op jit(solution)/shard_map/ppermute | solution.py:446
  348.9 73.7 %panel_factor.1 = (f32[1024,256]{1,0:T(8,128)}, f32[512,128]{1,0:T(8,128)}, f32[64,4]{1,0:T(8,128)}, f32[8,32,128]{2,1,0:T(8,128)}) custom-call(s32[2]{0:T(128)} %pad_add_fusion.spot_ref, f32[2,1024,256]{2,1,0:T(8,128)} %all-gather.5.cloned.1.call-done.d0_ref, f32[2,1024,256]{2,1,0:T(8,128)} %copy-done.4, ...), custom_call_target="tpu_custom_call" | custom-call | tf_op jit(solution)/shard_map/panel_factor/pallas_call | solution.py:285
  424.0 10.8 %gram_update.1 = f32[8192,256]{1,0:T(8,128)} custom-call(f32[8192,256]{1,0:T(8,128)} %bitcast.65, f32[8,32,128]{2,1,0:T(8,128)} %get-tuple-element.65.own_ref, f32[256,256]{1,0:T(8,128)} %constant_dynamic-slice_fusion.col_ref, f32[8,128,256]{2,1,0:T(8,128)} %bitcast.75), custom_call_target="tpu_custom_call" | custom-call | tf_op jit(solution)/shard_map/gram_update/pallas_call | solution.py:324
  (116 shorter events, 43.9 us)
Async XLA Ops:
  7.2 184.0 %all-gather.9.cloned.1.call-start = ((), (), s32[]{:S(2)}) async-start(), calls=%async_computation.2 | async-start | bytes 1474560 | tf_op jit(solution)/shard_map/all_gather | solution.py:542
  10.0 45.8 %collective-permute-start = (bf16[2,256,1024]{2,1,0:T(8,128)(2,1)}, bf16[2,256,1024]{2,1,0:T(8,128)(2,1)}, u32[]{:S(2)}, u32[]{:S(2)}) collective-permute-start(bf16[2,256,1024]{2,1,0:T(8,128)(2,1)} %get-tuple-element.85.refs_0_), channel_id=1, source_target_pairs={{0,8},{1,9},{2,10},{3,11},{4,12},{5,13},{6,14},{7,15},{8,16},{9,17... | collective-permute-start | bytes 3145736 | tf_op jit(solution)/shard_map/ppermute | solution.py:446
  13.2 42.6 %collective-permute-start.1 = (bf16[2,256,1024]{2,1,0:T(8,128)(2,1)}, bf16[2,256,1024]{2,1,0:T(8,128)(2,1)S(1)}, u32[]{:S(2)}, u32[]{:S(2)}) collective-permute-start(bf16[2,256,1024]{2,1,0:T(8,128)(2,1)} %get-tuple-element.85.refs_0_), channel_id=1, source_target_pairs={{8,0},{9,1},{10,2},{11,3},{12,4},{13,5},{14,6},{15,7},{16,8},{17,9... | collective-permute-start | bytes 3145736 | tf_op jit(solution)/shard_map/ppermute | solution.py:446
  16.2 39.5 %collective-permute-start.3 = (bf16[2,256,1024]{2,1,0:T(8,128)(2,1)}, bf16[2,256,1024]{2,1,0:T(8,128)(2,1)}, u32[]{:S(2)}, u32[]{:S(2)}) collective-permute-start(bf16[2,256,1024]{2,1,0:T(8,128)(2,1)} %get-tuple-element.85.refs_0_), channel_id=1, source_target_pairs={{0,2},{1,3},{2,0},{3,1},{4,6},{5,7},{6,4},{7,5},{8,10},{9,11},{10,... | collective-permute-start | bytes 3145736 | tf_op jit(solution)/shard_map/ppermute | solution.py:446
  27.6 28.1 %collective-permute-start.2 = (bf16[2,448,512]{2,1,0:T(8,128)(2,1)}, bf16[2,448,512]{2,1,0:T(8,128)(2,1)S(1)}, u32[]{:S(2)}, u32[]{:S(2)}) collective-permute-start(bf16[2,448,512]{2,1,0:T(8,128)(2,1)} %get-tuple-element.79), channel_id=1, source_target_pairs={{0,8},{1,9},{2,10},{3,11},{4,12},{5,13},{6,14},{7,15},{8,16},{9,17... | collective-permute-start | bytes 2752520 | tf_op jit(solution)/shard_map/ppermute | solution.py:446
  28.0 27.8 %collective-permute-start.4 = (bf16[2,448,512]{2,1,0:T(8,128)(2,1)}, bf16[2,448,512]{2,1,0:T(8,128)(2,1)S(1)}, u32[]{:S(2)}, u32[]{:S(2)}) collective-permute-start(bf16[2,448,512]{2,1,0:T(8,128)(2,1)} %get-tuple-element.80.refs_11_), channel_id=1, source_target_pairs={{0,4},{1,5},{2,6},{3,7},{4,0},{5,1},{6,2},{7,3},{8,12},{9,13},{10,... | collective-permute-start | bytes 2752520 | tf_op jit(solution)/shard_map/ppermute | solution.py:446
  57.1 48.7 %collective-permute-start.5 = (bf16[2,256,1024]{2,1,0:T(8,128)(2,1)}, bf16[2,256,1024]{2,1,0:T(8,128)(2,1)S(1)}, u32[]{:S(2)}, u32[]{:S(2)}) collective-permute-start(bf16[2,256,1024]{2,1,0:T(8,128)(2,1)} %collective-permute-done), channel_id=1, source_target_pairs={{0,8},{1,9},{2,10},{3,11},{4,12},{5,13},{6,14},{7,15},{8,16},{9,17... | collective-permute-start | bytes 3145736 | tf_op jit(solution)/shard_map/ppermute | solution.py:446
  60.3 45.5 %collective-permute-start.6 = (bf16[2,256,1024]{2,1,0:T(8,128)(2,1)S(1)}, bf16[2,256,1024]{2,1,0:T(8,128)(2,1)S(1)}, u32[]{:S(2)}, u32[]{:S(2)}) collective-permute-start(bf16[2,256,1024]{2,1,0:T(8,128)(2,1)S(1)} %collective-permute-done.1), channel_id=1, source_target_pairs={{8,0},{9,1},{10,2},{11,3},{12,4},{13,5},{14,6},{15,7},{16,8},{17,9... | collective-permute-start | bytes 3145736 | tf_op jit(solution)/shard_map/ppermute | solution.py:446
  65.5 40.2 %collective-permute-start.8 = (bf16[2,256,1024]{2,1,0:T(8,128)(2,1)S(1)}, bf16[2,256,1024]{2,1,0:T(8,128)(2,1)S(1)}, u32[]{:S(2)}, u32[]{:S(2)}) collective-permute-start(bf16[2,256,1024]{2,1,0:T(8,128)(2,1)S(1)} %broadcast_select_fusion.1.refs_2_), channel_id=1, source_target_pairs={{0,2},{1,3},{2,0},{3,1},{4,6},{5,7},{6,4},{7,5},{8,10},{9,11},{10,... | collective-permute-start | bytes 3145736 | tf_op jit(solution)/shard_map/ppermute | solution.py:446
  66.9 38.9 %collective-permute-start.7 = (bf16[2,448,512]{2,1,0:T(8,128)(2,1)}, bf16[2,448,512]{2,1,0:T(8,128)(2,1)}, u32[]{:S(2)}, u32[]{:S(2)}) collective-permute-start(bf16[2,448,512]{2,1,0:T(8,128)(2,1)} %get-tuple-element.39), channel_id=1, source_target_pairs={{0,24},{1,25},{2,26},{3,27},{4,28},{5,29},{6,30},{7,31},{8,0},{9,1... | collective-permute-start | bytes 2752520 | tf_op jit(solution)/shard_map/ppermute | solution.py:446
  66.9 38.9 %collective-permute-start.9 = (bf16[2,448,512]{2,1,0:T(8,128)(2,1)}, bf16[2,448,512]{2,1,0:T(8,128)(2,1)S(1)}, u32[]{:S(2)}, u32[]{:S(2)}) collective-permute-start(bf16[2,448,512]{2,1,0:T(8,128)(2,1)} %copy-done.11), channel_id=1, source_target_pairs={{0,4},{1,5},{2,6},{3,7},{4,0},{5,1},{6,2},{7,3},{8,12},{9,13},{10,... | collective-permute-start | bytes 2752520 | tf_op jit(solution)/shard_map/ppermute | solution.py:446
  110.6 60.3 %collective-permute-start.14 = (bf16[4,2,256,1024]{3,2,1,0:T(8,128)(2,1)}, bf16[4,2,256,1024]{3,2,1,0:T(8,128)(2,1)}, u32[]{:S(2)}, u32[]{:S(2)}) collective-permute-start(bf16[4,2,256,1024]{3,2,1,0:T(8,128)(2,1)} %pad_maximum_fusion), channel_id=1, source_target_pairs={{0,1},{1,0},{2,3},{3,2},{4,5},{5,4},{6,7},{7,6},{8,9},{9,8},{10,11... | collective-permute-start | bytes 12582920 | tf_op jit(solution)/shard_map/ppermute | solution.py:446
  116.5 122.2 %all-gather.7.cloned.1.call-start = ((), (), s32[]{:S(2)}) async-start(), calls=%async_computation.1 | async-start | bytes 2752512 | tf_op jit(solution)/shard_map/all_gather | solution.py:544
  119.3 50.5 %collective-permute-start.10 = (bf16[2,256,1024]{2,1,0:T(8,128)(2,1)}, bf16[2,256,1024]{2,1,0:T(8,128)(2,1)S(1)}, u32[]{:S(2)}, u32[]{:S(2)}) collective-permute-start(bf16[2,256,1024]{2,1,0:T(8,128)(2,1)} %get-tuple-element.82), channel_id=1, source_target_pairs={{8,0},{9,1},{10,2},{11,3},{12,4},{13,5},{14,6},{15,7},{16,24},{17,... | collective-permute-start | bytes 3145736 | tf_op jit(solution)/shard_map/ppermute | solution.py:446
  122.3 47.6 %collective-permute-start.12 = (bf16[2,256,1024]{2,1,0:T(8,128)(2,1)}, bf16[2,256,1024]{2,1,0:T(8,128)(2,1)}, u32[]{:S(2)}, u32[]{:S(2)}) collective-permute-start(bf16[2,256,1024]{2,1,0:T(8,128)(2,1)} %get-tuple-element.83.refs_4_), channel_id=1, source_target_pairs={{0,2},{1,3},{2,0},{3,1},{4,6},{5,7},{6,4},{7,5},{8,10},{9,11},{10,... | collective-permute-start | bytes 3145736 | tf_op jit(solution)/shard_map/ppermute | solution.py:446
  123.6 45.3 %collective-permute-start.11 = (bf16[2,448,512]{2,1,0:T(8,128)(2,1)}, bf16[2,448,512]{2,1,0:T(8,128)(2,1)}, u32[]{:S(2)}, u32[]{:S(2)}) collective-permute-start(bf16[2,448,512]{2,1,0:T(8,128)(2,1)} %get-tuple-element.44), channel_id=1, source_target_pairs={{0,16},{1,17},{2,18},{3,19},{4,20},{5,21},{6,22},{7,23},{8,24},{9,... | collective-permute-start | bytes 2752520 | tf_op jit(solution)/shard_map/ppermute | solution.py:446
  123.6 45.3 %collective-permute-start.13 = (bf16[2,448,512]{2,1,0:T(8,128)(2,1)}, bf16[2,448,512]{2,1,0:T(8,128)(2,1)}, u32[]{:S(2)}, u32[]{:S(2)}) collective-permute-start(bf16[2,448,512]{2,1,0:T(8,128)(2,1)} %collective-permute-done.7.refs_17_), channel_id=1, source_target_pairs={{0,4},{1,5},{2,6},{3,7},{4,0},{5,1},{6,2},{7,3},{8,12},{9,13},{10,... | collective-permute-start | bytes 2752520 | tf_op jit(solution)/shard_map/ppermute | solution.py:446
  129.5 142.7 %all-gather.5.cloned.1.call-start = ((), (), s32[]{:S(2)}) async-start(), calls=%async_computation | async-start | bytes 3145728 | tf_op jit(solution)/shard_map/all_gather | solution.py:546
  176.2 95.9 %collective-permute-start.17 = (bf16[3,2,256,1024]{3,2,1,0:T(8,128)(2,1)}, bf16[3,2,256,1024]{3,2,1,0:T(8,128)(2,1)}, u32[]{:S(2)}, u32[]{:S(2)}) collective-permute-start(bf16[3,2,256,1024]{3,2,1,0:T(8,128)(2,1)} %pad_maximum_fusion.1), channel_id=1, source_target_pairs={{0,1},{1,0},{2,3},{3,2},{4,5},{5,4},{6,7},{7,6},{8,9},{9,8},{10,11... | collective-permute-start | bytes 9437192 | tf_op jit(solution)/shard_map/ppermute | solution.py:446
  193.6 78.6 %collective-permute-start.15 = (bf16[2,256,1024]{2,1,0:T(8,128)(2,1)S(1)}, bf16[2,256,1024]{2,1,0:T(8,128)(2,1)S(1)}, u32[]{:S(2)}, u32[]{:S(2)}) collective-permute-start(bf16[2,256,1024]{2,1,0:T(8,128)(2,1)S(1)} %select_select_fusion.refs_6_), channel_id=1, source_target_pairs={{0,2},{1,3},{2,0},{3,1},{4,6},{5,7},{6,4},{7,5},{8,10},{9,11},{10,... | collective-permute-start | bytes 3145736 | tf_op jit(solution)/shard_map/ppermute | solution.py:446
  194.8 77.3 %collective-permute-start.16 = (bf16[2,448,512]{2,1,0:T(8,128)(2,1)}, bf16[2,448,512]{2,1,0:T(8,128)(2,1)S(1)}, u32[]{:S(2)}, u32[]{:S(2)}) collective-permute-start(bf16[2,448,512]{2,1,0:T(8,128)(2,1)} %collective-permute-done.11.refs_15_), channel_id=1, source_target_pairs={{0,4},{1,5},{2,6},{3,7},{4,0},{5,1},{6,2},{7,3},{8,12},{9,13},{10,... | collective-permute-start | bytes 2752520 | tf_op jit(solution)/shard_map/ppermute | solution.py:446
  273.1 8.9 %collective-permute-start.18 = (bf16[2,256,1024]{2,1,0:T(8,128)(2,1)S(1)}, bf16[2,256,1024]{2,1,0:T(8,128)(2,1)}, u32[]{:S(2)}, u32[]{:S(2)}) collective-permute-start(bf16[2,256,1024]{2,1,0:T(8,128)(2,1)S(1)} %collective-permute-done.15.refs_7_), channel_id=1, source_target_pairs={{0,1},{1,0},{2,3},{3,2},{4,5},{5,4},{6,7},{7,6},{8,9},{9,8},{10,11... | collective-permute-start | bytes 3145736 | tf_op jit(solution)/shard_map/ppermute | solution.py:446
  273.8 28.7 %collective-permute-start.19 = (f32[2,1024,256]{2,1,0:T(8,128)}, f32[2,1024,256]{2,1,0:T(8,128)S(1)}, u32[]{:S(2)}, u32[]{:S(2)}) collective-permute-start(f32[2,1024,256]{2,1,0:T(8,128)} %all-gather.5.cloned.1.call-done.d0_ref), channel_id=1, source_target_pairs={{0,1},{1,0},{2,3},{3,2},{4,5},{5,4},{6,7},{7,6},{8,9},{9,8},{10,11... | collective-permute-start | bytes 6291464 | tf_op jit(solution)/shard_map/ppermute | solution.py:446
  273.8 28.7 %collective-permute-start.20 = (f32[2,896,256]{2,1,0:T(8,128)}, f32[2,896,256]{2,1,0:T(8,128)}, u32[]{:S(2)}, u32[]{:S(2)}) collective-permute-start(f32[2,896,256]{2,1,0:T(8,128)} %all-gather.7.cloned.1.call-done.b0_ref), channel_id=1, source_target_pairs={{0,1},{1,0},{2,3},{3,2},{4,5},{5,4},{6,7},{7,6},{8,9},{9,8},{10,11... | collective-permute-start | bytes 5505032 | tf_op jit(solution)/shard_map/ppermute | solution.py:446
  304.0 5.2 %collective-permute-start.23 = (f32[256,64]{1,0:T(8,128)S(1)}, f32[256,64]{1,0:T(8,128)S(1)}, u32[]{:S(2)}, u32[]{:S(2)}) collective-permute-start(f32[256,64]{1,0:T(8,128)S(1)} %get-tuple-element.87), channel_id=1, source_target_pairs={{0,8},{1,9},{2,10},{3,11},{4,12},{5,13},{6,14},{7,15},{8,16},{9,17... | collective-permute-start | bytes 196616 | tf_op jit(solution)/shard_map/ppermute | solution.py:446
  305.3 11.4 %collective-permute-start.22 = (f32[256,64]{1,0:T(8,128)S(1)}, f32[256,64]{1,0:T(8,128)S(1)}, u32[]{:S(2)}, u32[]{:S(2)}) collective-permute-start(f32[256,64]{1,0:T(8,128)S(1)} %get-tuple-element.88), channel_id=1, source_target_pairs={{0,16},{1,17},{2,18},{3,19},{4,20},{5,21},{6,22},{7,23},{8,24},{9,... | collective-permute-start | bytes 196616 | tf_op jit(solution)/shard_map/ppermute | solution.py:446
  306.4 12.4 %collective-permute-start.21 = (f32[256,64]{1,0:T(8,128)S(1)}, f32[256,64]{1,0:T(8,128)S(1)}, u32[]{:S(2)}, u32[]{:S(2)}) collective-permute-start(f32[256,64]{1,0:T(8,128)S(1)} %get-tuple-element.86), channel_id=1, source_target_pairs={{0,24},{1,25},{2,26},{3,27},{4,28},{5,29},{6,30},{7,31},{8,0},{9,1... | collective-permute-start | bytes 196616 | tf_op jit(solution)/shard_map/ppermute | solution.py:446
  319.8 4.7 %collective-permute-start.24 = (f32[256,64]{1,0:T(8,128)S(1)}, f32[256,64]{1,0:T(8,128)S(1)}, u32[]{:S(2)}, u32[]{:S(2)}) collective-permute-start(f32[256,64]{1,0:T(8,128)S(1)} %fusion.9), channel_id=1, source_target_pairs={{0,2},{1,3},{2,0},{3,1},{4,6},{5,7},{6,4},{7,5},{8,10},{9,11},{10,... | collective-permute-start | bytes 196616 | tf_op jit(solution)/shard_map/ppermute | solution.py:446
  331.8 3.9 collective-permute-start.27
  331.8 6.1 %collective-permute-start.28 = (f32[64,512]{1,0:T(8,128)S(1)}, f32[64,512]{1,0:T(8,128)S(1)}, u32[]{:S(2)}, u32[]{:S(2)}) collective-permute-start(f32[64,512]{1,0:T(8,128)S(1)} %pad_maximum_fusion.4), channel_id=1, source_target_pairs={{0,16},{1,17},{2,18},{3,19},{4,20},{5,21},{6,22},{7,23},{8,24},{9,... | collective-permute-start | bytes 393224 | tf_op jit(solution)/shard_map/ppermute | solution.py:446
  332.8 12.4 %collective-permute-start.29 = (f32[64,512]{1,0:T(8,128)S(1)}, f32[64,512]{1,0:T(8,128)S(1)}, u32[]{:S(2)}, u32[]{:S(2)}) collective-permute-start(f32[64,512]{1,0:T(8,128)S(1)} %pad_maximum_fusion.4), channel_id=1, source_target_pairs={{0,24},{1,25},{2,26},{3,27},{4,28},{5,29},{6,30},{7,31},{8,0},{9,1... | collective-permute-start | bytes 393224 | tf_op jit(solution)/shard_map/ppermute | solution.py:446
  345.3 3.6 collective-permute-start.30
  (18 other events, 606.8 us)
Sparse Core Ops, SparseCore 0:
  116.6 74.5 all-gather.8
  192.8 45.8 all-gather.6
  240.2 31.8 all-gather.4

commit v4 on v3

--- a/solution.py
+++ b/solution.py
@@ -131,48 +131,56 @@
             for q in range(block // 8)
         ]
         rows = eliminate(rows)
-        for q in range(block // 8):
-            inv_ref[8 * q : 8 * q + 8, :] = rows[q]
+        for half in range(2):
+
+            @pl.when(b % 2 == half)
+            def _():
+                kept = slice(half * block, (half + 1) * block)
+                for q in range(block // 8):
+                    at = half * block + 8 * q
+                    inv_ref[at : at + 8, kept] = rows[q]
+
         for s in range(blocks):
 
             @pl.when(b == s)
             def _():
+                half = s % 2
                 here = slice(s * block, (s + 1) * block)
+                kept = slice(half * block, (half + 1) * block)
+                inv = inv_ref[kept, kept]
+                work_ref[here, here] = mm_t(work_ref[here, here], inv)
+                if half == 0:
+                    near = slice((s + 1) * block, (s + 2) * block)
+                    across = mm_t(work_ref[near, here], inv)
+                    work_ref[near, here] = across
+                    work_ref[near, near] = work_ref[near, near] - mm_t(across, across)
+                    return
+                both = slice((s - 1) * block, (s + 1) * block)
                 after = slice((s + 1) * block, width)
-                half = s % 2
-                kept = slice(half * block, (half + 1) * block)
+                old = slice(0, block)
+                across = work_ref[here, (s - 1) * block : s * block]
+                inv_ref[kept, old] = -mm(inv, mm(across, inv_ref[old, old]))
                 inv = inv_ref[...]
                 if s + 1 < blocks:
-                    upper_ref[kept, after] = mm(inv, work_ref[here, after])
-                for these in spans(s * block, total, chunk):
-                    work_ref[these, here] = mm_t(work_ref[these, here], inv)
-                if half == 0 and s + 1 < blocks:
-                    near = slice((s + 1) * block, (s + 2) * block)
-                    far = slice((s + 2) * block, width)
-                    for these in spans((s + 1) * block, total, chunk):
-                        work_ref[these, near] = work_ref[these, near] - mm(
-                            work_ref[these, here], upper_ref[kept, near]
+                    upper_ref[:, after] = mm(inv, work_ref[both, after])
+                for these in spans((s + 1) * block, total, chunk):
+                    solved = mm_t(work_ref[these, both], inv)
+                    work_ref[these, both] = solved
+                    if s + 1 < blocks:
+                        work_ref[these, after] = work_ref[these, after] - mm(
+                            solved, upper_ref[:, after]
                         )
-                    if s + 2 < blocks:
-                        work_ref[near, far] = work_ref[near, far] - mm(
-                            work_ref[near, here], upper_ref[kept, far]
-                        )
-                elif s + 1 < blocks:
-                    both = slice((s - 1) * block, (s + 1) * block)
-                    for these in spans((s + 1) * block, total, chunk):
-                        work_ref[these, after] = work_ref[these, after] - mm(
-                            work_ref[these, both], upper_ref[:, after]
-                        )
 
         return carry
 
+    inv_ref[:block, block:] = jnp.zeros((block, block), jnp.float32)
     lax.fori_loop(0, blocks, one, 0)
 
 
 def factor_scratch(total, width):
     return [
         pltpu.VMEM((total, width), jnp.float32),
-        pltpu.VMEM((block, block), jnp.float32),
+        pltpu.VMEM((2 * block, 2 * block), jnp.float32),
         pltpu.VMEM((2 * block, width), jnp.float32),
         pltpu.VMEM((width, block), jnp.float32),
     ]
@@ -201,14 +209,25 @@
     )(rows)
 
 
+def band_of(row, k):
+    z, x = row // 2, row % 2
+    step = k // 2
+    near = (z // 2) * 2 + (z + step % 2) % 2
+    return ((near + 2 * (step // 2)) % 4) * 2 + (x + k % 2) % 2
+
+
 def panel_kernel(
     share,
     seqs,
     spot_ref,
     d0_ref,
     d1_ref,
+    d2_ref,
+    d3_ref,
     b0_ref,
     b1_ref,
+    b2_ref,
+    b3_ref,
     near_ref,
     far_ref,
     head_ref,
@@ -224,16 +243,28 @@
     feat_ref,
 ):
     total, width = work_ref.shape
-    _, low, band = b0_ref.shape
+    low, band = b0_ref.shape
     cycles = low // block + 1
     row, col = spot_ref[0], spot_ref[1]
-    core = col % 2
-    for far, (diag_ref, below_ref) in enumerate(((d0_ref, b0_ref), (d1_ref, b1_ref))):
-        for half in range(2):
-            there = 2 * half + (core + far) % 2
-            lanes = pl.ds(pl.multiple_of(there * band, 128), band)
-            work_ref[:width, lanes] = diag_ref[half]
-            work_ref[width : width + low, lanes] = below_ref[half]
+    y, core = col // 2, col % 2
+    queries = query_ref.shape[0] // cycles
+    top = width + low
+    diag_refs, below_refs = (d0_ref, d1_ref, d2_ref, d3_ref), (b0_ref, b1_ref, b2_ref, b3_ref)
+    for i, (diag_ref, below_ref) in enumerate(zip(diag_refs, below_refs)):
+        there = ((y + i // 2) % 2) * 2 + (core + i % 2) % 2
+        lanes = pl.ds(pl.multiple_of(there * band, 128), band)
+        work_ref[width:top, lanes] = below_ref[...]
+        for k in range(8):
+            at = band_of(row, k) * block
+            work_ref[pl.ds(pl.multiple_of(at, block), block), lanes] = diag_ref[
+                k * block : (k + 1) * block, :
+            ]
+    half = queries // 2
+    for k in range(8):
+        lanes = pl.ds(pl.multiple_of(band_of(row, k) * block, block), block)
+        rows = slice(k * half, (k + 1) * half)
+        work_ref[top : top + half, lanes] = head_ref[rows, :block]
+        work_ref[top + half : top + queries, lanes] = head_ref[rows, block:]
     for far, ref in enumerate((near_ref, far_ref)):
         side = (core + far) % 2
         for i in range(4):
@@ -249,9 +280,6 @@
         if a > 0:
             here = slice(width + (a - 1) * block, width + a * block)
             work_ref[here, :] = work_ref[here, :] + outer_sum(pack_left(mine), right) * share
-    queries = head_ref.shape[0]
-    top = width + low
-    work_ref[top : top + queries, :] = head_ref[...]
     work_ref[top + queries :, :] = jnp.zeros((total - top - queries, width), jnp.float32)
     for i in range(width // 128):
         work_ref[top + queries : top + queries + seqs, i * 128 : (i + 1) * 128] = feat_ref[
@@ -277,20 +305,21 @@
 
 
 def panel(spot, diags, belows, near, far, heads, queries, seqs, share):
-    _, low, band = belows[0].shape
-    width = heads.shape[1]
+    low, band = belows[0].shape
+    width = diags[0].shape[0]
     cycles = low // block + 1
-    total = -(-(width + low + heads.shape[0] + 8) // block) * block
+    count = queries.shape[0] // cycles
+    total = -(-(width + low + count + 8) // block) * block
     whole = pl.BlockSpec(memory_space=pltpu.VMEM)
     return pl.pallas_call(
         functools.partial(panel_kernel, share, seqs),
         out_shape=[
             jax.ShapeDtypeStruct((cycles * block, band), jnp.float32),
             jax.ShapeDtypeStruct(queries.shape, jnp.float32),
-            jax.ShapeDtypeStruct((heads.shape[0], seqs), jnp.float32),
+            jax.ShapeDtypeStruct((count, seqs), jnp.float32),
             jax.ShapeDtypeStruct((cycles, near.shape[0] // cycles, block), jnp.float32),
         ],
-        in_specs=[pl.BlockSpec(memory_space=pltpu.SMEM)] + [whole] * 8,
+        in_specs=[pl.BlockSpec(memory_space=pltpu.SMEM)] + [whole] * 12,
         out_specs=[whole] * 4,
         scratch_shapes=factor_scratch(total, width)
         + [pltpu.VMEM((width // 128, near.shape[0], 128), jnp.float32)],
@@ -430,6 +459,9 @@
             at.append(rest % sizes[name])
             rest //= sizes[name]
         at = at[::-1]
+        if axis == "both":
+            pairs.append((source, source ^ 3))
+            continue
         which = names.index(axis)
         there = at[which] + step
         if steps is not None:
@@ -450,13 +482,13 @@
 
 
 def gradient_kernel(spot_ref, *refs):
-    token_refs, refs = refs[:11], refs[11:]
+    token_refs, refs = refs[:13], refs[13:]
     weight_refs, refs = refs[:8], refs[8:]
     out_proj_ref, in_proj_ref, outer_ref, inner_ref, token_buf, weight_buf, token_sem, weight_sem = refs
     z, x, y, core = (spot_ref[i] for i in range(4))
     height, band = token_refs[0].shape[1:]
-    near, (far_1, far_2, far_3) = token_refs[:8], token_refs[8:]
-    far = [far_1.at[i] for i in range(4)] + [far_2.at[i] for i in range(3)] + [far_3]
+    near, group = token_refs[:8], token_refs[8]
+    far = [group.at[i] for i in range(4)] + list(token_refs[9:])
     depth = weight_refs[0].shape[2]
     weight_copies = []
     for i, ref in enumerate(weight_refs):
@@ -503,7 +535,7 @@
             jax.ShapeDtypeStruct((4, height, out_proj.shape[1]), jnp.float32),
             jax.ShapeDtypeStruct((height, in_proj.shape[1]), jnp.float32),
         ],
-        in_specs=[pl.BlockSpec(memory_space=pltpu.SMEM)] + [hbm] * 19 + [whole] * 2,
+        in_specs=[pl.BlockSpec(memory_space=pltpu.SMEM)] + [hbm] * 21 + [whole] * 2,
         out_specs=[whole] * 2,
         scratch_shapes=[
             pltpu.VMEM((4, kinds, height, full), jnp.bfloat16),
@@ -538,14 +570,9 @@
     cycles, band_rows, _, band_cols = gram_in.shape
     count = queries.shape[0]
     below = gram_in[1:, :, 0, :].reshape((cycles - 1) * band_rows, band_cols)
-    small = jnp.concatenate([gram_in[0, :, 0, :], queries[:, 0, :].reshape(-1, band_cols)], axis=0)
-    small = lax.all_gather(small, "rows", axis=0)
-    over_y = [[0, 2], [1, 3]]
-    belows = lax.all_gather(below, "cols", axis=0, axis_index_groups=over_y)
-    diag = small[:, :band_rows].reshape(-1, band_cols)
-    diags = lax.all_gather(diag, "cols", axis=0, axis_index_groups=over_y)
-    heads = jnp.transpose(small[:, band_rows:].reshape(8, count, band_rows), (1, 0, 2))
-    heads = heads.reshape(count, 8 * band_rows)
+    head = queries[:, 0, :]
+    head = jnp.concatenate([head[: count // 2], head[count // 2 :]], axis=1)
+    small = jnp.concatenate([gram_in[0, :, 0, :], head], axis=0)
 
     up1, down1 = shift(both, "z", 1, False), shift(both, "z", -1, False)
     y_own = shift(both, "y", 1)
@@ -565,21 +592,32 @@
     y_b = shift(slot_b, "y", 1)
     wx3 = shift(wz3, "x", 1)
     wz2 = shift(p2, "z", 2)
-    core_1 = shift(jnp.stack([both, y_own, slot_a, y_a]), "core", 1)
-    last, wz2, y_b, wx3, core_1 = tie((last, wz2, y_b, wx3, core_1))
+    below_y = shift(below, "y", 1)
+    group = jnp.stack([both, y_own, slot_a, y_a])
+    last, wz2, y_b, wx3, below_y, group, small = tie(
+        (last, wz2, y_b, wx3, below_y, group, small)
+    )
 
     slot_c = jnp.where(z == 0, last, jnp.where(z == 1, down2, jnp.where(z == 2, up2, last)))
     y_c = shift(slot_c, "y", 1)
     wx2 = shift(wz2, "x", 1)
-    core_2 = shift(jnp.stack([slot_b, y_b, slot_c]), "core", 1)
-    y_c, wx2, core_2, diags, belows = tie((y_c, wx2, core_2, diags, belows))
-    core_3 = shift(y_c, "core", 1)
-    diag_c = shift(diags, "core", 1)
-    below_c = shift(belows, "core", 1)
-    pieces = [both, y_own, slot_a, y_a, slot_b, y_b, slot_c, y_c, core_1, core_2, core_3]
+    core_1 = shift(group, "core", 1)
+    small = jnp.concatenate([small, shift(small, "z", 0, False, (1, 0, 3, 2))], axis=0)
+    small = jnp.concatenate([small, shift(small, "z", 0, False, (2, 3, 0, 1))], axis=0)
+    c_b = shift(slot_b, "core", 1)
+    y_c, wx2, core_1, c_b, small = tie((y_c, wx2, core_1, c_b, small))
+
+    cy_b = shift(y_b, "core", 1)
+    c_c = shift(slot_c, "core", 1)
+    cy_c = shift(y_c, "core", 1)
+    cy_b, c_c, cy_c, small, below, below_y = tie((cy_b, c_c, cy_c, small, below, below_y))
+    across = shift(small, "x", 1)
+    below_c = shift(below, "core", 1)
+    below_cy = shift(below_y, "core", 1)
+    belows = [below, below_c, below_y, below_cy]
+    pieces = [both, y_own, slot_a, y_a, slot_b, y_b, slot_c, y_c, core_1, c_b, cy_b, c_c, cy_c]
     weights = [piece[0], wx0, wz1, wx1, wz2, wx2, wz3, wx3]
-    diags, belows = [diags, diag_c], [belows, below_c]
-    return pieces, weights, diags, belows, heads
+    return pieces, weights, small, across, belows
 
 
 def local(
@@ -596,22 +634,28 @@
 ):
     row_index, col_index = lax.axis_index("rows"), lax.axis_index("cols")
     me = {"z": row_index // 2, "x": row_index % 2, "y": col_index // 2, "core": col_index % 2}
-    pieces, weights, diags, belows, heads = rounds(
+    pieces, weights, small, across, belows = rounds(
         tokens, cotangent, gate_weight, down_weight, gram_in, queries, me
     )
     share = weights[0].shape[1]
     out_proj = lax.dynamic_slice_in_dim(proj_out, me["z"] * share, share, 0)
     spot = jnp.stack([me["z"], me["x"], me["y"], me["core"]]).astype(jnp.int32)
     outer, proj_inner = gradient(spot, pieces, weights, out_proj, proj_in)
-    tied = tie((outer, *diags, *belows))
-    outer, diags, belows = tied[0], tied[1:3], tied[3:5]
+    tied = tie((outer, small, across, *belows))
+    outer, small, across, belows = tied[0], tied[1], tied[2], tied[3:]
+    band_rows, count = gram_in.shape[1], queries.shape[0]
+    rows = band_rows + count // 2
+    parts = [side[i * rows : (i + 1) * rows] for i in range(4) for side in (small, across)]
+    diag = jnp.concatenate([part[:band_rows] for part in parts], axis=0)
+    heads = jnp.concatenate([part[band_rows:] for part in parts], axis=0)
+    diag_y = shift(diag, "y", 1)
     proj_outer = outer[0]
     table = jnp.array(slot_of, jnp.int32)
     for s in range(1, 4):
         part = lax.dynamic_index_in_dim(outer, table[me["z"], s], 0, False)
         proj_outer = proj_outer + shift(part, "z", -s)
-    proj_outer = proj_outer + shift(proj_outer, "y", 1)
-    proj_outer = proj_outer + shift(proj_outer, "core", 1)
+    over_y, over_core = shift(proj_outer, "y", 1), shift(proj_outer, "core", 1)
+    proj_outer = (proj_outer + over_core) + (over_y + shift(proj_outer, "both", 1))
     features = sequence_features(proj_inner, proj_outer, lengths, loss_mask)
     cycles, band_rows, _, band_cols = gram_in.shape
     seqs = features.shape[0]
@@ -622,6 +666,8 @@
     ]
     mine = jnp.concatenate(mine, axis=1)
     pair = jnp.concatenate([mine, shift(mine, "x", 1)], axis=0)
+    diag, diag_y, pair = tie((diag, diag_y, pair))
+    diags = [diag, shift(diag, "core", 1), diag_y, shift(diag_y, "core", 1)]
     near = jnp.concatenate([pair] + [shift(pair, "z", s) for s in range(1, 4)], axis=0)
     far = shift(near, "core", 1)
     share = cycles / near.shape[0]

time: 439 us -> 345 us (0.79); the launches traced: 442 us -> 341 us
  waiting for transfers between devices: 225 us -> 147 us
  Pallas kernels: 105 us -> 92.4 us
  between operations: 19.8 us -> 7.34 us
  starting transfers between devices: 41.8 us -> 53.3 us
  other arithmetic: 21.2 us -> 14.3 us
    all_gather x3 -> x0, waiting for transfers between devices: 91.1 us -> none  [the longest x1 43.6 us: rounds(): belows = lax.all_gather(below, 'cols', axis=0, axis_index_groups=over_y)]
    ppermute x31 -> x41, waiting for transfers between devices: 134 us -> 147 us  [shift(): return lax.ppermute(value, ('rows', 'cols'), pairs)]
    pallas_call x1, Pallas kernels: 73.7 us -> 61 us  [panel(): pl.pallas_call(functools.partial(panel_kernel, share, seqs), out_shape=[j...]
    ppermute x31 -> x41, starting transfers between devices: 41.3 us -> 53.3 us  [shift(): return lax.ppermute(value, ('rows', 'cols'), pairs)]
    another operation x3 -> x2, other arithmetic: 10.5 us -> 4.86 us  [rounds(): group = jnp.stack([both, y_own, slot_a, y_a])]
    unnamed x41 -> x81, local copies, waits for them, and re-layouts: 14.1 us -> 16.6 us
  transfers between devices with their start and end apart: 34 -> 41, of which waited for: 16 -> 15; matrix products, arithmetic and copies ran while one was open for 8% -> 9% of each run, Pallas kernels for 5% -> 6%
where the time goes in v4:
time: 345 us; the launch traced here: 341 us
  waiting for transfers between devices  147 us (43%)
  Pallas kernels  92.4 us (27%)
  starting transfers between devices  53.3 us (15%)
  local copies, waits for them, and re-layouts  26 us (8%)
  other arithmetic  14.3 us (4%)
  between operations  7.34 us (2%)
    ppermute x41, waiting for transfers between devices, shift(): return lax.ppermute(value, ('rows', 'cols'), pairs)  147 us
    pallas_call x1, Pallas kernels, panel(): pl.pallas_call(functools.partial(panel_kernel, share, seqs), out_shape=[j...  61 us
    ppermute x41, starting transfers between devices, shift(): return lax.ppermute(value, ('rows', 'cols'), pairs)  53.3 us
    pallas_call x1, Pallas kernels, gradient(): pl.pallas_call(gradient_kernel, out_shape=[jax.ShapeDtypeStruct((4, heigh...  20.5 us
    unnamed x81, local copies, waits for them, and re-layouts  16.6 us
    pallas_call x1, Pallas kernels, gram_update(): pl.pallas_call(functools.partial(gram_kernel, share), out_shape=jax.Shape...  10.8 us
  transfers between devices with their start and end apart: 41, of which 15 were waited for; matrix products, arithmetic and copies ran while one was open for 9% of the time, Pallas kernels for 6%

profile of v4, /device:TPU:9, one launch (start us, length us, event | category | flops | bytes accessed | tf_op | source)
XLA Modules:
  0.0 341.3 jit_solution(14226483415691262553)
XLA Ops:
  0.6 2.7 fusion.13
  3.4 3.2 collective-permute-start
  6.6 2.1 collective-permute-start.1
  10.0 2.8 copy.23
  12.9 3.8 %copy.24 = bf16[512,1792]{0,1:T(8,128)(2,1)} copy(bf16[512,1792]{1,0:T(8,128)(2,1)} %param.14) | data formatting | bytes 3670016 | tf_op args[3]
  16.7 3.3 fusion.1
  22.4 26.7 %collective-permute-done.2.refs_15_ = bf16[2,448,512]{2,1,0:T(8,128)(2,1)S(1)} collective-permute-done((bf16[2,448,512]{2,1,0:T(8,128)(2,1)}, bf16[2,448,512]{2,1,0:T(8,128)(2,1)S(1)}, u32[]{:S(2)}, u32[]{:S(2)}) %collective-permute-start.2) | collective-permute-done | bytes 917536 | tf_op jit(solution)/shard_map/ppermute | solution.py:478
  50.4 3.2 collective-permute-start.5
  53.6 5.1 %collective-permute-start.6 = (bf16[2,256,1024]{2,1,0:T(8,128)(2,1)}, bf16[2,256,1024]{2,1,0:T(8,128)(2,1)S(1)}, u32[]{:S(2)}, u32[]{:S(2)}) collective-permute-start(bf16[2,256,1024]{2,1,0:T(8,128)(2,1)} %collective-permute-done.1), channel_id=1, source_target_pairs={{8,0},{9,1},{10,2},{11,3},{12,4},{13,5},{14,6},{15,7},{16,8},{17,9... | collective-permute-start | bytes 3145736 | tf_op jit(solution)/shard_map/ppermute | solution.py:478
  58.7 2.3 broadcast_select_fusion.1.refs_2_
  63.5 35.8 %collective-permute-done.7.refs_19_ = bf16[2,448,512]{2,1,0:T(8,128)(2,1)} collective-permute-done((bf16[2,448,512]{2,1,0:T(8,128)(2,1)}, bf16[2,448,512]{2,1,0:T(8,128)(2,1)}, u32[]{:S(2)}, u32[]{:S(2)}) %collective-permute-start.7) | collective-permute-done | bytes 917536 | tf_op jit(solution)/shard_map/ppermute | solution.py:478
  99.6 4.5 %collective-permute-start.10 = (bf16[2,256,1024]{2,1,0:T(8,128)(2,1)S(1)}, bf16[2,256,1024]{2,1,0:T(8,128)(2,1)S(1)}, u32[]{:S(2)}, u32[]{:S(2)}) collective-permute-start(bf16[2,256,1024]{2,1,0:T(8,128)(2,1)S(1)} %get-tuple-element.105), channel_id=1, source_target_pairs={{8,0},{9,1},{10,2},{11,3},{12,4},{13,5},{14,6},{15,7},{16,24},{17,... | collective-permute-start | bytes 3145736 | tf_op jit(solution)/shard_map/ppermute | solution.py:478
  105.4 3.6 %slice.96 = f32[7,128,1,256]{3,2,1,0:T(1,128)S(1)} slice(f32[8,128,8,256]{3,2,1,0:T(8,128)} %param.19), slice={[1:8], [0:128], [0:1], [0:256]} | slice | bytes 1835008 | tf_op jit(solution)/shard_map/slice | solution.py:572
  112.9 2.1 pad_maximum_fusion
  115.0 30.3 %collective-permute-done.14.b2_ref = f32[896,256]{1,0:T(8,128)S(1)} collective-permute-done((f32[896,256]{1,0:T(8,128)S(1)}, f32[896,256]{1,0:T(8,128)S(1)}, u32[]{:S(2)}, u32[]{:S(2)}) %collective-permute-start.14) | collective-permute-done | bytes 917536 | tf_op jit(solution)/shard_map/ppermute | solution.py:478
  145.4 3.3 collective-permute-done.11.refs_17_
  153.4 2.5 collective-permute-start.19
  155.9 3.6 %collective-permute-done.19 = f32[160,256]{1,0:T(8,128)S(1)} collective-permute-done((f32[160,256]{1,0:T(8,128)S(1)}, f32[160,256]{1,0:T(8,128)S(1)}, u32[]{:S(2)}, u32[]{:S(2)}) %collective-permute-start.19) | collective-permute-done | bytes 163872 | tf_op jit(solution)/shard_map/ppermute | solution.py:478
  161.3 14.4 %collective-permute-done.20 = f32[320,256]{1,0:T(8,128)S(1)} collective-permute-done((f32[320,256]{1,0:T(8,128)S(1)}, f32[320,256]{1,0:T(8,128)S(1)}, u32[]{:S(2)}, u32[]{:S(2)}) %collective-permute-start.20) | collective-permute-done | bytes 327712 | tf_op jit(solution)/shard_map/ppermute | solution.py:478
  189.4 20.5 %gradient.1 = (f32[4,256,64]{2,1,0:T(8,128)}, f32[256,128]{1,0:T(8,128)}) custom-call(s32[4]{0:T(128)} %pad_add_fusion.1.spot_ref, bf16[2,256,1024]{2,1,0:T(8,128)(2,1)} %get-tuple-element.108.refs_0_, bf16[2,256,1024]{2,1,0:T(8,128)(2,1)} %collective-permute-done.3.refs_1_, bf16[2,256,1024]{2,1,0:T(8,128)(2,1)} %broadcast_select_fusion.1.refs_2_, ...), custom_call_target="tpu_custom_call" | custom-call | flops 15032385536 | bytes 24117248 | tf_op jit(solution)/shard_map/gradient/pallas_call | solution.py:532
  214.0 4.0 %collective-permute-start.29 = (f32[256,64]{1,0:T(8,128)S(1)}, f32[256,64]{1,0:T(8,128)S(1)}, u32[]{:S(2)}, u32[]{:S(2)}) collective-permute-start(f32[256,64]{1,0:T(8,128)S(1)} %get-tuple-element.111), channel_id=1, source_target_pairs={{0,16},{1,17},{2,18},{3,19},{4,20},{5,21},{6,22},{7,23},{8,24},{9,... | collective-permute-start | bytes 196616 | tf_op jit(solution)/shard_map/ppermute | solution.py:478
  219.2 6.8 %collective-permute-done.29 = f32[256,64]{1,0:T(8,128)S(1)} collective-permute-done((f32[256,64]{1,0:T(8,128)S(1)}, f32[256,64]{1,0:T(8,128)S(1)}, u32[]{:S(2)}, u32[]{:S(2)}) %collective-permute-start.29) | collective-permute-done | bytes 65568 | tf_op jit(solution)/shard_map/ppermute | solution.py:478
  226.1 2.6 collective-permute-done.28
  230.1 2.5 collective-permute-start.33
  232.7 5.6 %collective-permute-done.32 = f32[256,64]{1,0:T(8,128)S(1)} collective-permute-done((f32[256,64]{1,0:T(8,128)S(1)}, f32[256,64]{1,0:T(8,128)S(1)}, u32[]{:S(2)}, u32[]{:S(2)}) %collective-permute-start.32) | collective-permute-done | bytes 65568 | tf_op jit(solution)/shard_map/ppermute | solution.py:478
  238.3 3.4 collective-permute-done.33
  243.8 2.7 collective-permute-done.34
  248.7 4.0 %collective-permute-start.38 = (f32[64,512]{1,0:T(8,128)S(1)}, f32[64,512]{1,0:T(8,128)S(1)}, u32[]{:S(2)}, u32[]{:S(2)}) collective-permute-start(f32[64,512]{1,0:T(8,128)S(1)} %pad_maximum_fusion.4), channel_id=1, source_target_pairs={{0,16},{1,17},{2,18},{3,19},{4,20},{5,21},{6,22},{7,23},{8,24},{9,... | collective-permute-start | bytes 393224 | tf_op jit(solution)/shard_map/ppermute | solution.py:478
  253.3 7.9 %collective-permute-done.38 = f32[64,512]{1,0:T(8,128)S(1)} collective-permute-done((f32[64,512]{1,0:T(8,128)S(1)}, f32[64,512]{1,0:T(8,128)S(1)}, u32[]{:S(2)}, u32[]{:S(2)}) %collective-permute-start.38) | collective-permute-done | bytes 131104 | tf_op jit(solution)/shard_map/ppermute | solution.py:478
  261.3 2.8 collective-permute-done.39
  267.8 61.0 %panel_factor.1 = (f32[1024,256]{1,0:T(8,128)}, f32[512,128]{1,0:T(8,128)}, f32[64,4]{1,0:T(8,128)}, f32[8,32,128]{2,1,0:T(8,128)}) custom-call(s32[2]{0:T(128)} %pad_add_fusion.spot_ref, f32[1024,256]{1,0:T(8,128)} %copy-done.5, f32[1024,256]{1,0:T(8,128)} %copy-done.7, f32[1024,256]{1,0:T(8,128)} %copy-done.6, f32[1024,256]{1,0:T(8,128)} %copy-done.8, ...), custom_call_target="tpu_custom_call" | custom-call | tf_op jit(solution)/shard_map/panel_factor/pallas_call | solution.py:314
  330.2 10.8 %gram_update.1 = f32[8192,256]{1,0:T(8,128)} custom-call(f32[8192,256]{1,0:T(8,128)} %bitcast.60, f32[8,32,128]{2,1,0:T(8,128)} %get-tuple-element.91.own_ref, f32[256,256]{1,0:T(8,128)} %constant_dynamic-slice_fusion.col_ref, f32[8,128,256]{2,1,0:T(8,128)} %bitcast.67), custom_call_target="tpu_custom_call" | custom-call | tf_op jit(solution)/shard_map/gram_update/pallas_call | solution.py:353
  (164 shorter events, 43.8 us)
Async XLA Ops:
  3.4 45.8 %collective-permute-start = (bf16[2,256,1024]{2,1,0:T(8,128)(2,1)}, bf16[2,256,1024]{2,1,0:T(8,128)(2,1)S(1)}, u32[]{:S(2)}, u32[]{:S(2)}) collective-permute-start(bf16[2,256,1024]{2,1,0:T(8,128)(2,1)} %get-tuple-element.108.refs_0_), channel_id=1, source_target_pairs={{0,8},{1,9},{2,10},{3,11},{4,12},{5,13},{6,14},{7,15},{8,16},{9,17... | collective-permute-start | bytes 3145736 | tf_op jit(solution)/shard_map/ppermute | solution.py:478
  6.6 42.6 %collective-permute-start.1 = (bf16[2,256,1024]{2,1,0:T(8,128)(2,1)}, bf16[2,256,1024]{2,1,0:T(8,128)(2,1)}, u32[]{:S(2)}, u32[]{:S(2)}) collective-permute-start(bf16[2,256,1024]{2,1,0:T(8,128)(2,1)} %get-tuple-element.108.refs_0_), channel_id=1, source_target_pairs={{8,0},{9,1},{10,2},{11,3},{12,4},{13,5},{14,6},{15,7},{16,8},{17,9... | collective-permute-start | bytes 3145736 | tf_op jit(solution)/shard_map/ppermute | solution.py:478
  8.7 40.5 %collective-permute-start.3 = (bf16[2,256,1024]{2,1,0:T(8,128)(2,1)}, bf16[2,256,1024]{2,1,0:T(8,128)(2,1)}, u32[]{:S(2)}, u32[]{:S(2)}) collective-permute-start(bf16[2,256,1024]{2,1,0:T(8,128)(2,1)} %get-tuple-element.108.refs_0_), channel_id=1, source_target_pairs={{0,2},{1,3},{2,0},{3,1},{4,6},{5,7},{6,4},{7,5},{8,10},{9,11},{10,... | collective-permute-start | bytes 3145736 | tf_op jit(solution)/shard_map/ppermute | solution.py:478
  20.0 29.2 %collective-permute-start.2 = (bf16[2,448,512]{2,1,0:T(8,128)(2,1)}, bf16[2,448,512]{2,1,0:T(8,128)(2,1)S(1)}, u32[]{:S(2)}, u32[]{:S(2)}) collective-permute-start(bf16[2,448,512]{2,1,0:T(8,128)(2,1)} %get-tuple-element.102), channel_id=1, source_target_pairs={{0,8},{1,9},{2,10},{3,11},{4,12},{5,13},{6,14},{7,15},{8,16},{9,17... | collective-permute-start | bytes 2752520 | tf_op jit(solution)/shard_map/ppermute | solution.py:478
  21.2 27.9 %collective-permute-start.4 = (bf16[2,448,512]{2,1,0:T(8,128)(2,1)}, bf16[2,448,512]{2,1,0:T(8,128)(2,1)S(1)}, u32[]{:S(2)}, u32[]{:S(2)}) collective-permute-start(bf16[2,448,512]{2,1,0:T(8,128)(2,1)} %get-tuple-element.103.refs_13_), channel_id=1, source_target_pairs={{0,4},{1,5},{2,6},{3,7},{4,0},{5,1},{6,2},{7,3},{8,12},{9,13},{10,... | collective-permute-start | bytes 2752520 | tf_op jit(solution)/shard_map/ppermute | solution.py:478
  50.4 48.9 %collective-permute-start.5 = (bf16[2,256,1024]{2,1,0:T(8,128)(2,1)S(1)}, bf16[2,256,1024]{2,1,0:T(8,128)(2,1)S(1)}, u32[]{:S(2)}, u32[]{:S(2)}) collective-permute-start(bf16[2,256,1024]{2,1,0:T(8,128)(2,1)S(1)} %collective-permute-done), channel_id=1, source_target_pairs={{0,8},{1,9},{2,10},{3,11},{4,12},{5,13},{6,14},{7,15},{8,16},{9,17... | collective-permute-start | bytes 3145736 | tf_op jit(solution)/shard_map/ppermute | solution.py:478
  53.6 45.7 %collective-permute-start.6 = (bf16[2,256,1024]{2,1,0:T(8,128)(2,1)}, bf16[2,256,1024]{2,1,0:T(8,128)(2,1)S(1)}, u32[]{:S(2)}, u32[]{:S(2)}) collective-permute-start(bf16[2,256,1024]{2,1,0:T(8,128)(2,1)} %collective-permute-done.1), channel_id=1, source_target_pairs={{8,0},{9,1},{10,2},{11,3},{12,4},{13,5},{14,6},{15,7},{16,8},{17,9... | collective-permute-start | bytes 3145736 | tf_op jit(solution)/shard_map/ppermute | solution.py:478
  61.1 38.2 %collective-permute-start.8 = (bf16[2,256,1024]{2,1,0:T(8,128)(2,1)}, bf16[2,256,1024]{2,1,0:T(8,128)(2,1)}, u32[]{:S(2)}, u32[]{:S(2)}) collective-permute-start(bf16[2,256,1024]{2,1,0:T(8,128)(2,1)} %broadcast_select_fusion.1.refs_2_), channel_id=1, source_target_pairs={{0,2},{1,3},{2,0},{3,1},{4,6},{5,7},{6,4},{7,5},{8,10},{9,11},{10,... | collective-permute-start | bytes 3145736 | tf_op jit(solution)/shard_map/ppermute | solution.py:478
  62.3 37.0 %collective-permute-start.7 = (bf16[2,448,512]{2,1,0:T(8,128)(2,1)}, bf16[2,448,512]{2,1,0:T(8,128)(2,1)}, u32[]{:S(2)}, u32[]{:S(2)}) collective-permute-start(bf16[2,448,512]{2,1,0:T(8,128)(2,1)} %get-tuple-element.52), channel_id=1, source_target_pairs={{0,24},{1,25},{2,26},{3,27},{4,28},{5,29},{6,30},{7,31},{8,0},{9,1... | collective-permute-start | bytes 2752520 | tf_op jit(solution)/shard_map/ppermute | solution.py:478
  62.3 37.0 %collective-permute-start.9 = (bf16[2,448,512]{2,1,0:T(8,128)(2,1)}, bf16[2,448,512]{2,1,0:T(8,128)(2,1)}, u32[]{:S(2)}, u32[]{:S(2)}) collective-permute-start(bf16[2,448,512]{2,1,0:T(8,128)(2,1)} %copy-done.23), channel_id=1, source_target_pairs={{0,4},{1,5},{2,6},{3,7},{4,0},{5,1},{6,2},{7,3},{8,12},{9,13},{10,... | collective-permute-start | bytes 2752520 | tf_op jit(solution)/shard_map/ppermute | solution.py:478
  99.6 49.1 %collective-permute-start.10 = (bf16[2,256,1024]{2,1,0:T(8,128)(2,1)S(1)}, bf16[2,256,1024]{2,1,0:T(8,128)(2,1)S(1)}, u32[]{:S(2)}, u32[]{:S(2)}) collective-permute-start(bf16[2,256,1024]{2,1,0:T(8,128)(2,1)S(1)} %get-tuple-element.105), channel_id=1, source_target_pairs={{8,0},{9,1},{10,2},{11,3},{12,4},{13,5},{14,6},{15,7},{16,24},{17,... | collective-permute-start | bytes 3145736 | tf_op jit(solution)/shard_map/ppermute | solution.py:478
  104.1 44.6 %collective-permute-start.12 = (bf16[2,256,1024]{2,1,0:T(8,128)(2,1)S(1)}, bf16[2,256,1024]{2,1,0:T(8,128)(2,1)}, u32[]{:S(2)}, u32[]{:S(2)}) collective-permute-start(bf16[2,256,1024]{2,1,0:T(8,128)(2,1)S(1)} %get-tuple-element.106.refs_4_), channel_id=1, source_target_pairs={{0,2},{1,3},{2,0},{3,1},{4,6},{5,7},{6,4},{7,5},{8,10},{9,11},{10,... | collective-permute-start | bytes 3145736 | tf_op jit(solution)/shard_map/ppermute | solution.py:478
  109.0 36.3 %collective-permute-start.14 = (f32[896,256]{1,0:T(8,128)S(1)}, f32[896,256]{1,0:T(8,128)S(1)}, u32[]{:S(2)}, u32[]{:S(2)}) collective-permute-start(f32[896,256]{1,0:T(8,128)S(1)} %bitcast.64), channel_id=1, source_target_pairs={{0,2},{1,3},{2,0},{3,1},{4,6},{5,7},{6,4},{7,5},{8,10},{9,11},{10,... | collective-permute-start | bytes 2752520 | tf_op jit(solution)/shard_map/ppermute | solution.py:478
  109.3 39.3 %collective-permute-start.11 = (bf16[2,448,512]{2,1,0:T(8,128)(2,1)S(1)}, bf16[2,448,512]{2,1,0:T(8,128)(2,1)S(1)}, u32[]{:S(2)}, u32[]{:S(2)}) collective-permute-start(bf16[2,448,512]{2,1,0:T(8,128)(2,1)S(1)} %copy-done.13), channel_id=1, source_target_pairs={{0,16},{1,17},{2,18},{3,19},{4,20},{5,21},{6,22},{7,23},{8,24},{9,... | collective-permute-start | bytes 2752520 | tf_op jit(solution)/shard_map/ppermute | solution.py:478
  109.3 39.3 %collective-permute-start.13 = (bf16[2,448,512]{2,1,0:T(8,128)(2,1)}, bf16[2,448,512]{2,1,0:T(8,128)(2,1)S(1)}, u32[]{:S(2)}, u32[]{:S(2)}) collective-permute-start(bf16[2,448,512]{2,1,0:T(8,128)(2,1)} %collective-permute-done.7.refs_19_), channel_id=1, source_target_pairs={{0,4},{1,5},{2,6},{3,7},{4,0},{5,1},{6,2},{7,3},{8,12},{9,13},{10,... | collective-permute-start | bytes 2752520 | tf_op jit(solution)/shard_map/ppermute | solution.py:478
  148.7 27.8 %collective-permute-start.17 = (bf16[4,2,256,1024]{3,2,1,0:T(8,128)(2,1)S(1)}, bf16[4,2,256,1024]{3,2,1,0:T(8,128)(2,1)S(1)}, u32[]{:S(2)}, u32[]{:S(2)}) collective-permute-start(bf16[4,2,256,1024]{3,2,1,0:T(8,128)(2,1)S(1)} %pad_maximum_fusion), channel_id=1, source_target_pairs={{0,1},{1,0},{2,3},{3,2},{4,5},{5,4},{6,7},{7,6},{8,9},{9,8},{10,11... | collective-permute-start | bytes 12582920 | tf_op jit(solution)/shard_map/ppermute | solution.py:478
  149.6 26.7 %collective-permute-start.18 = (bf16[2,256,1024]{2,1,0:T(8,128)(2,1)S(1)}, bf16[2,256,1024]{2,1,0:T(8,128)(2,1)S(1)}, u32[]{:S(2)}, u32[]{:S(2)}) collective-permute-start(bf16[2,256,1024]{2,1,0:T(8,128)(2,1)S(1)} %get-tuple-element.106.refs_4_), channel_id=1, source_target_pairs={{0,1},{1,0},{2,3},{3,2},{4,5},{5,4},{6,7},{7,6},{8,9},{9,8},{10,11... | collective-permute-start | bytes 3145736 | tf_op jit(solution)/shard_map/ppermute | solution.py:478
  151.0 25.5 %collective-permute-start.15 = (bf16[2,256,1024]{2,1,0:T(8,128)(2,1)}, bf16[2,256,1024]{2,1,0:T(8,128)(2,1)S(1)}, u32[]{:S(2)}, u32[]{:S(2)}) collective-permute-start(bf16[2,256,1024]{2,1,0:T(8,128)(2,1)} %select_select_fusion.refs_6_), channel_id=1, source_target_pairs={{0,2},{1,3},{2,0},{3,1},{4,6},{5,7},{6,4},{7,5},{8,10},{9,11},{10,... | collective-permute-start | bytes 3145736 | tf_op jit(solution)/shard_map/ppermute | solution.py:478
  152.2 24.2 %collective-permute-start.16 = (bf16[2,448,512]{2,1,0:T(8,128)(2,1)S(1)}, bf16[2,448,512]{2,1,0:T(8,128)(2,1)S(1)}, u32[]{:S(2)}, u32[]{:S(2)}) collective-permute-start(bf16[2,448,512]{2,1,0:T(8,128)(2,1)S(1)} %collective-permute-done.11.refs_17_), channel_id=1, source_target_pairs={{0,4},{1,5},{2,6},{3,7},{4,0},{5,1},{6,2},{7,3},{8,12},{9,13},{10,... | collective-permute-start | bytes 2752520 | tf_op jit(solution)/shard_map/ppermute | solution.py:478
  159.5 16.3 %collective-permute-start.20 = (f32[320,256]{1,0:T(8,128)S(1)}, f32[320,256]{1,0:T(8,128)S(1)}, u32[]{:S(2)}, u32[]{:S(2)}) collective-permute-start(f32[320,256]{1,0:T(8,128)S(1)} %pad_maximum_fusion.3), channel_id=1, source_target_pairs={{0,16},{1,17},{2,18},{3,19},{4,20},{5,21},{6,22},{7,23},{8,24},{9,... | collective-permute-start | bytes 983048 | tf_op jit(solution)/shard_map/ppermute | solution.py:478
  175.7 12.8 %collective-permute-start.22 = (bf16[2,256,1024]{2,1,0:T(8,128)(2,1)}, bf16[2,256,1024]{2,1,0:T(8,128)(2,1)}, u32[]{:S(2)}, u32[]{:S(2)}) collective-permute-start(bf16[2,256,1024]{2,1,0:T(8,128)(2,1)} %select_select_fusion.refs_6_), channel_id=1, source_target_pairs={{0,1},{1,0},{2,3},{3,2},{4,5},{5,4},{6,7},{7,6},{8,9},{9,8},{10,11... | collective-permute-start | bytes 3145736 | tf_op jit(solution)/shard_map/ppermute | solution.py:478
  176.3 12.2 %collective-permute-start.21 = (bf16[2,256,1024]{2,1,0:T(8,128)(2,1)}, bf16[2,256,1024]{2,1,0:T(8,128)(2,1)}, u32[]{:S(2)}, u32[]{:S(2)}) collective-permute-start(bf16[2,256,1024]{2,1,0:T(8,128)(2,1)} %collective-permute-done.12.refs_5_), channel_id=1, source_target_pairs={{0,1},{1,0},{2,3},{3,2},{4,5},{5,4},{6,7},{7,6},{8,9},{9,8},{10,11... | collective-permute-start | bytes 3145736 | tf_op jit(solution)/shard_map/ppermute | solution.py:478
  188.5 21.5 %collective-permute-start.24 = (f32[640,256]{1,0:T(8,128)S(1)}, f32[640,256]{1,0:T(8,128)S(1)}, u32[]{:S(2)}, u32[]{:S(2)}) collective-permute-start(f32[640,256]{1,0:T(8,128)S(1)} %pad_maximum_fusion.2), channel_id=1, source_target_pairs={{0,4},{1,5},{2,6},{3,7},{4,0},{5,1},{6,2},{7,3},{8,12},{9,13},{10,... | collective-permute-start | bytes 1966088 | tf_op jit(solution)/shard_map/ppermute | solution.py:478
  188.9 21.1 %collective-permute-start.25 = (f32[896,256]{1,0:T(8,128)S(1)}, f32[896,256]{1,0:T(8,128)S(1)}, u32[]{:S(2)}, u32[]{:S(2)}) collective-permute-start(f32[896,256]{1,0:T(8,128)S(1)} %bitcast.65), channel_id=1, source_target_pairs={{0,1},{1,0},{2,3},{3,2},{4,5},{5,4},{6,7},{7,6},{8,9},{9,8},{10,11... | collective-permute-start | bytes 2752520 | tf_op jit(solution)/shard_map/ppermute | solution.py:478
  189.4 20.7 %collective-permute-start.26 = (f32[896,256]{1,0:T(8,128)}, f32[896,256]{1,0:T(8,128)S(1)}, u32[]{:S(2)}, u32[]{:S(2)}) collective-permute-start(f32[896,256]{1,0:T(8,128)} %copy-done.10), channel_id=1, source_target_pairs={{0,1},{1,0},{2,3},{3,2},{4,5},{5,4},{6,7},{7,6},{8,9},{9,8},{10,11... | collective-permute-start | bytes 2752520 | tf_op jit(solution)/shard_map/ppermute | solution.py:478
  211.1 35.4 %collective-permute-start.27 = (f32[1024,256]{1,0:T(8,128)S(1)}, f32[1024,256]{1,0:T(8,128)S(1)}, u32[]{:S(2)}, u32[]{:S(2)}) collective-permute-start(f32[1024,256]{1,0:T(8,128)S(1)} %slice_dynamic-update-slice_fusion.d0_ref), channel_id=1, source_target_pairs={{0,2},{1,3},{2,0},{3,1},{4,6},{5,7},{6,4},{7,5},{8,10},{9,11},{10,... | collective-permute-start | bytes 3145736 | tf_op jit(solution)/shard_map/ppermute | solution.py:478
  214.0 12.1 %collective-permute-start.29 = (f32[256,64]{1,0:T(8,128)S(1)}, f32[256,64]{1,0:T(8,128)S(1)}, u32[]{:S(2)}, u32[]{:S(2)}) collective-permute-start(f32[256,64]{1,0:T(8,128)S(1)} %get-tuple-element.111), channel_id=1, source_target_pairs={{0,16},{1,17},{2,18},{3,19},{4,20},{5,21},{6,22},{7,23},{8,24},{9,... | collective-permute-start | bytes 196616 | tf_op jit(solution)/shard_map/ppermute | solution.py:478
  230.1 11.6 %collective-permute-start.33 = (f32[256,64]{1,0:T(8,128)S(1)}, f32[256,64]{1,0:T(8,128)S(1)}, u32[]{:S(2)}, u32[]{:S(2)}) collective-permute-start(f32[256,64]{1,0:T(8,128)S(1)} %fusion.9), channel_id=1, source_target_pairs={{0,3},{1,2},{2,1},{3,0},{4,7},{5,6},{6,5},{7,4},{8,11},{9,10},{10,... | collective-permute-start | bytes 196616 | tf_op jit(solution)/shard_map/ppermute | solution.py:478
  246.6 19.7 %collective-permute-start.35 = (f32[1024,256]{1,0:T(8,128)S(1)}, f32[1024,256]{1,0:T(8,128)S(1)}, u32[]{:S(2)}, u32[]{:S(2)}) collective-permute-start(f32[1024,256]{1,0:T(8,128)S(1)} %slice_dynamic-update-slice_fusion.d0_ref), channel_id=1, source_target_pairs={{0,1},{1,0},{2,3},{3,2},{4,5},{5,4},{6,7},{7,6},{8,9},{9,8},{10,11... | collective-permute-start | bytes 3145736 | tf_op jit(solution)/shard_map/ppermute | solution.py:478
  247.3 19.0 %collective-permute-start.36 = (f32[1024,256]{1,0:T(8,128)S(1)}, f32[1024,256]{1,0:T(8,128)S(1)}, u32[]{:S(2)}, u32[]{:S(2)}) collective-permute-start(f32[1024,256]{1,0:T(8,128)S(1)} %collective-permute-done.27.d2_ref), channel_id=1, source_target_pairs={{0,1},{1,0},{2,3},{3,2},{4,5},{5,4},{6,7},{7,6},{8,9},{9,8},{10,11... | collective-permute-start | bytes 3145736 | tf_op jit(solution)/shard_map/ppermute | solution.py:478
  248.7 12.6 %collective-permute-start.38 = (f32[64,512]{1,0:T(8,128)S(1)}, f32[64,512]{1,0:T(8,128)S(1)}, u32[]{:S(2)}, u32[]{:S(2)}) collective-permute-start(f32[64,512]{1,0:T(8,128)S(1)} %pad_maximum_fusion.4), channel_id=1, source_target_pairs={{0,16},{1,17},{2,18},{3,19},{4,20},{5,21},{6,22},{7,23},{8,24},{9,... | collective-permute-start | bytes 393224 | tf_op jit(solution)/shard_map/ppermute | solution.py:478
  252.7 11.3 %collective-permute-start.39 = (f32[64,512]{1,0:T(8,128)S(1)}, f32[64,512]{1,0:T(8,128)S(1)}, u32[]{:S(2)}, u32[]{:S(2)}) collective-permute-start(f32[64,512]{1,0:T(8,128)S(1)} %pad_maximum_fusion.4), channel_id=1, source_target_pairs={{0,24},{1,25},{2,26},{3,27},{4,28},{5,29},{6,30},{7,31},{8,0},{9,1... | collective-permute-start | bytes 393224 | tf_op jit(solution)/shard_map/ppermute | solution.py:478
  (38 other events, 902.8 us)

commit v5 on v4

--- a/solution.py
+++ b/solution.py
@@ -104,7 +104,7 @@
     return [slice(at, min(at + step, stop)) for at in range(start, stop, step)]
 
 
-def factor(work_ref, inv_ref, upper_ref, root_ref):
+def factor(work_ref, inv_ref, upper_ref, root_ref, beside=None):
     total, width = work_ref.shape
     blocks = width // block
     chunk = 4 * block
@@ -130,6 +130,8 @@
             work_ref[pl.ds(pl.multiple_of(off + 8 * q, 8), 8), pl.ds(off, block)]
             for q in range(block // 8)
         ]
+        if beside is not None:
+            beside(b)
         rows = eliminate(rows)
         for half in range(2):
 
@@ -232,20 +234,30 @@
     far_ref,
     head_ref,
     query_ref,
-    part_ref,
+    gram_ref,
     next_ref,
     score_ref,
-    own_ref,
+    done_ref,
     work_ref,
     inv_ref,
     upper_ref,
     root_ref,
     feat_ref,
+    slab_ref,
+    left_ref,
+    right_ref,
+    slab_sem,
 ):
     total, width = work_ref.shape
     low, band = b0_ref.shape
     cycles = low // block + 1
     row, col = spot_ref[0], spot_ref[1]
+    loads = []
+    for h in range(band // block):
+        there = gram_ref.at[:, h * block : (h + 1) * block]
+        loads.append(pltpu.make_async_copy(there, slab_ref.at[h], slab_sem.at[h]))
+    for copy in loads:
+        copy.start()
     y, core = col // 2, col % 2
     queries = query_ref.shape[0] // cycles
     top = width + low
@@ -276,23 +288,55 @@
         work_ref[here, :] = work_ref[here, :] + outer_sum(pack_left(first[i]), right) * share
     for a in range(cycles):
         mine = feat_ref[row, pl.ds(a, every, stride=cycles), :]
-        own_ref[a] = mine
+        left = pack_left(mine)
+        left_ref[a] = left
         if a > 0:
             here = slice(width + (a - 1) * block, width + a * block)
-            work_ref[here, :] = work_ref[here, :] + outer_sum(pack_left(mine), right) * share
+            work_ref[here, :] = work_ref[here, :] + outer_sum(left, right) * share
+    sides = band // block
+    for h in range(sides):
+        for k in range(cycles):
+            other = feat_ref[sides * col + h, pl.ds(k, every, stride=cycles), :]
+            at = (h * cycles + k) * block
+            right_ref[:, at : at + block] = pack_right(other)
+    for copy in loads:
+        copy.wait()
+
+    def beside(a):
+        base = pl.multiple_of(a * block * cycles, block)
+        for h in range(sides):
+            across = slice(h * cycles * block, (h + 1) * cycles * block)
+            update = outer_sum(left_ref[a], right_ref[:, across]) * share
+            for k in range(1, cycles):
+                here = pl.ds(base + k, block, stride=cycles)
+                slab_ref[h, here, :] = (
+                    slab_ref[h, here, :] + update[:, k * block : (k + 1) * block]
+                )
+
     work_ref[top + queries :, :] = jnp.zeros((total - top - queries, width), jnp.float32)
     for i in range(width // 128):
         work_ref[top + queries : top + queries + seqs, i * 128 : (i + 1) * 128] = feat_ref[
             i, pl.ds(0, seqs, stride=cycles), :
         ]
-    factor(work_ref, inv_ref, upper_ref, root_ref)
+    factor(work_ref, inv_ref, upper_ref, root_ref, beside)
     lanes = pl.ds(pl.multiple_of(col * band, 128), band)
     rows = pl.ds(pl.multiple_of(row * block, block), block)
     mine = work_ref[rows, lanes] * jnp.concatenate([root_ref[rows, :]] * (band // block), axis=1)
     row_at = row * block + lax.broadcasted_iota(jnp.int32, mine.shape, 0)
     col_at = col * band + lax.broadcasted_iota(jnp.int32, mine.shape, 1)
-    part_ref[:block, :] = jnp.where(col_at <= row_at, mine, 0.0)
-    part_ref[block:, :] = work_ref[width:top, lanes]
+    mine = jnp.where(col_at <= row_at, mine, 0.0)
+    stores = []
+    for a in range(cycles):
+        if a > 0:
+            mine = work_ref[width + (a - 1) * block : width + a * block, lanes]
+        for h in range(sides):
+            here = pl.ds(a * block * cycles, block, stride=cycles)
+            slab_ref[h, here, :] = mine[:, h * block : (h + 1) * block]
+    for h in range(sides):
+        there = done_ref.at[:, h * block : (h + 1) * block]
+        stores.append(pltpu.make_async_copy(slab_ref.at[h], there, slab_sem.at[h]))
+    for copy in stores:
+        copy.start()
     solved = work_ref[top : top + queries, :]
     product = mm_t(solved, work_ref[width:top, :])
     next_ref[pl.ds(0, queries, stride=cycles), :] = work_ref[
@@ -302,9 +346,11 @@
         here = pl.ds(a, queries, stride=cycles)
         next_ref[here, :] = query_ref[here, :] - product[:, (a - 1) * block : a * block]
     score_ref[...] = mm_t(solved, work_ref[top + queries : top + queries + 8, :])[:, :seqs]
-
-
-def panel(spot, diags, belows, near, far, heads, queries, seqs, share):
+    for copy in stores:
+        copy.wait()
+
+
+def panel(spot, diags, belows, near, far, heads, queries, gram, seqs, share):
     low, band = belows[0].shape
     width = diags[0].shape[0]
     cycles = low // block + 1
@@ -314,56 +360,24 @@
     return pl.pallas_call(
         functools.partial(panel_kernel, share, seqs),
         out_shape=[
-            jax.ShapeDtypeStruct((cycles * block, band), jnp.float32),
             jax.ShapeDtypeStruct(queries.shape, jnp.float32),
             jax.ShapeDtypeStruct((count, seqs), jnp.float32),
-            jax.ShapeDtypeStruct((cycles, near.shape[0] // cycles, block), jnp.float32),
+            jax.ShapeDtypeStruct(gram.shape, jnp.float32),
         ],
-        in_specs=[pl.BlockSpec(memory_space=pltpu.SMEM)] + [whole] * 12,
-        out_specs=[whole] * 4,
+        in_specs=[pl.BlockSpec(memory_space=pltpu.SMEM)] + [whole] * 12
+        + [pl.BlockSpec(memory_space=pl.ANY)],
+        out_specs=[whole] * 2 + [pl.BlockSpec(memory_space=pl.ANY)],
         scratch_shapes=factor_scratch(total, width)
-        + [pltpu.VMEM((width // 128, near.shape[0], 128), jnp.float32)],
+        + [
+            pltpu.VMEM((width // 128, near.shape[0], 128), jnp.float32),
+            pltpu.VMEM((band // block, gram.shape[0], block), jnp.float32),
+            pltpu.VMEM((cycles, 6 * near.shape[0] // cycles, block), jnp.bfloat16),
+            pltpu.VMEM((6 * near.shape[0] // cycles, cycles * band), jnp.bfloat16),
+            pltpu.SemaphoreType.DMA((band // block,)),
+        ],
         compiler_params=pltpu.CompilerParams(vmem_limit_bytes=vmem_limit),
         name="panel_factor",
-    )(spot, *diags, *belows, near, far, heads, queries)
-
-
-def gram_kernel(share, gram_ref, own_ref, col_ref, panel_ref, out_ref):
-    steps, seqs, count = own_ref.shape
-    cycles, lanes = col_ref.shape[0] // seqs, col_ref.shape[1]
-    right = jnp.concatenate(
-        [pack_right(col_ref[pl.ds(b, seqs, stride=cycles), :]) for b in range(cycles)], axis=1
-    )
-    for a in range(steps):
-        base = a * count * cycles
-        out_ref[pl.ds(base, count, stride=cycles), :] = panel_ref[a]
-        update = outer_sum(pack_left(own_ref[a]), right) * share
-        for b in range(1, cycles):
-            here = pl.ds(base + b, count, stride=cycles)
-            out_ref[here, :] = gram_ref[here, :] + update[:, b * lanes : (b + 1) * lanes]
-
-
-def gram_update(gram_in, own, col, part, share):
-    cycles, seqs, count = own.shape
-    rows, width = col.shape
-    lanes = 128
-    steps = 2 if cycles % 2 == 0 else 1
-    gram = gram_in.reshape(cycles * count * cycles, width)
-    tall = pl.BlockSpec((steps * count * cycles, lanes), lambda v, a: (a, v))
-    return pl.pallas_call(
-        functools.partial(gram_kernel, share),
-        out_shape=jax.ShapeDtypeStruct(gram.shape, jnp.float32),
-        grid=(width // lanes, cycles // steps),
-        in_specs=[
-            tall,
-            pl.BlockSpec((steps, seqs, count), lambda v, a: (a, 0, 0)),
-            pl.BlockSpec((rows, lanes), lambda v, a: (0, v)),
-            pl.BlockSpec((steps, count, lanes), lambda v, a: (a, 0, v)),
-        ],
-        out_specs=tall,
-        compiler_params=pltpu.CompilerParams(vmem_limit_bytes=vmem_limit),
-        name="gram_update",
-    )(gram, own, col, part.reshape(cycles, count, width)).reshape(gram_in.shape)
+    )(spot, *diags, *belows, near, far, heads, queries, gram)
 
 
 def sequence_features(proj_inner, proj_outer, lengths, loss_mask):
@@ -499,28 +513,25 @@
     for i in range(16):
         ref = (far if i % 2 else near)[i // 2]
         col = ((y + i % 4 // 2) % 2) * 2 + (core + i % 2) % 2
-        there = token_buf.at[i // 4, :, :, pl.ds(pl.multiple_of(col * band, 128), band)]
+        slot = slice(i // 4 * height, (i // 4 + 1) * height)
+        there = token_buf.at[:, slot, pl.ds(pl.multiple_of(col * band, 128), band)]
         token_copies.append(pltpu.make_async_copy(ref, there, token_sem.at[i]))
     for copy in weight_copies + token_copies:
         copy.start()
     for copy in weight_copies:
         copy.wait()
+    for copy in token_copies:
+        copy.wait()
+    inner_ref[...] = jnp.dot(
+        token_buf[0, :height], in_proj_ref[...], preferred_element_type=jnp.float32
+    )
+    over = (((1,), (1,)), ((), ()))
+    gate = lax.dot_general(token_buf[0], weight_buf[0], over, preferred_element_type=jnp.float32)
+    hidden = lax.dot_general(token_buf[1], weight_buf[1], over, preferred_element_type=jnp.float32)
+    grad = (hidden * (gate / (1.0 + jnp.exp(-gate)))).astype(jnp.bfloat16)
+    outer = jnp.dot(grad, out_proj_ref[...], preferred_element_type=jnp.float32)
     for s in range(4):
-        for copy in token_copies[4 * s : 4 * s + 4]:
-            copy.wait()
-        if s == 0:
-            inner_ref[...] = jnp.dot(
-                token_buf[0, 0], in_proj_ref[...], preferred_element_type=jnp.float32
-            )
-        over = (((1,), (1,)), ((), ()))
-        gate = lax.dot_general(
-            token_buf[s, 0], weight_buf[0], over, preferred_element_type=jnp.float32
-        )
-        hidden = lax.dot_general(
-            token_buf[s, 1], weight_buf[1], over, preferred_element_type=jnp.float32
-        )
-        grad = (hidden * (gate / (1.0 + jnp.exp(-gate)))).astype(jnp.bfloat16)
-        outer_ref[s] = jnp.dot(grad, out_proj_ref[...], preferred_element_type=jnp.float32)
+        outer_ref[s] = outer[s * height : (s + 1) * height]
 
 
 def gradient(spot, tokens, weights, out_proj, in_proj):
@@ -538,7 +549,7 @@
         in_specs=[pl.BlockSpec(memory_space=pltpu.SMEM)] + [hbm] * 21 + [whole] * 2,
         out_specs=[whole] * 2,
         scratch_shapes=[
-            pltpu.VMEM((4, kinds, height, full), jnp.bfloat16),
+            pltpu.VMEM((kinds, 4 * height, full), jnp.bfloat16),
             pltpu.VMEM((kinds, share, full), jnp.bfloat16),
             pltpu.SemaphoreType.DMA((16,)),
             pltpu.SemaphoreType.DMA((8,)),
@@ -558,7 +569,7 @@
     return lax.optimization_barrier((*values, *after))[:count]
 
 
-def rounds(tokens, cotangent, gate_weight, down_weight, gram_in, queries, me):
+def rounds(tokens, cotangent, gate_weight, down_weight, gram_in, queries, me, early):
     z = me["z"]
     both = jnp.stack([tokens, cotangent])
     depth, width = gate_weight.shape
@@ -594,8 +605,8 @@
     wz2 = shift(p2, "z", 2)
     below_y = shift(below, "y", 1)
     group = jnp.stack([both, y_own, slot_a, y_a])
-    last, wz2, y_b, wx3, below_y, group, small = tie(
-        (last, wz2, y_b, wx3, below_y, group, small)
+    last, wz2, y_b, wx3, below_y, group, small, *early = tie(
+        (last, wz2, y_b, wx3, below_y, group, small, *early)
     )
 
     slot_c = jnp.where(z == 0, last, jnp.where(z == 1, down2, jnp.where(z == 2, up2, last)))
@@ -617,7 +628,7 @@
     belows = [below, below_c, below_y, below_cy]
     pieces = [both, y_own, slot_a, y_a, slot_b, y_b, slot_c, y_c, core_1, c_b, cy_b, c_c, cy_c]
     weights = [piece[0], wx0, wz1, wx1, wz2, wx2, wz3, wx3]
-    return pieces, weights, small, across, belows
+    return pieces, weights, small, across, belows, early
 
 
 def local(
@@ -634,12 +645,16 @@
 ):
     row_index, col_index = lax.axis_index("rows"), lax.axis_index("cols")
     me = {"z": row_index // 2, "x": row_index % 2, "y": col_index // 2, "core": col_index % 2}
-    pieces, weights, small, across, belows = rounds(
-        tokens, cotangent, gate_weight, down_weight, gram_in, queries, me
-    )
-    share = weights[0].shape[1]
+    share = gate_weight.shape[1] // 4
     out_proj = lax.dynamic_slice_in_dim(proj_out, me["z"] * share, share, 0)
     spot = jnp.stack([me["z"], me["x"], me["y"], me["core"]]).astype(jnp.int32)
+    where = jnp.stack([row_index, col_index]).astype(jnp.int32)
+    table = jnp.array(slot_of, jnp.int32)
+    early = [spot, where, out_proj] + [table[me["z"], s] for s in range(1, 4)]
+    pieces, weights, small, across, belows, early = rounds(
+        tokens, cotangent, gate_weight, down_weight, gram_in, queries, me, early
+    )
+    spot, where, out_proj, *order = early
     outer, proj_inner = gradient(spot, pieces, weights, out_proj, proj_in)
     tied = tie((outer, small, across, *belows))
     outer, small, across, belows = tied[0], tied[1], tied[2], tied[3:]
@@ -650,9 +665,8 @@
     heads = jnp.concatenate([part[band_rows:] for part in parts], axis=0)
     diag_y = shift(diag, "y", 1)
     proj_outer = outer[0]
-    table = jnp.array(slot_of, jnp.int32)
     for s in range(1, 4):
-        part = lax.dynamic_index_in_dim(outer, table[me["z"], s], 0, False)
+        part = lax.dynamic_index_in_dim(outer, order[s - 1], 0, False)
         proj_outer = proj_outer + shift(part, "z", -s)
     over_y, over_core = shift(proj_outer, "y", 1), shift(proj_outer, "core", 1)
     proj_outer = (proj_outer + over_core) + (over_y + shift(proj_outer, "both", 1))
@@ -671,13 +685,19 @@
     near = jnp.concatenate([pair] + [shift(pair, "z", s) for s in range(1, 4)], axis=0)
     far = shift(near, "core", 1)
     share = cycles / near.shape[0]
-    where = jnp.stack([row_index, col_index]).astype(jnp.int32)
-    part, query_next, scores, own = panel(
-        where, diags, belows, near, far, heads, queries.reshape(-1, band_rows), seqs, share
-    )
-    col = lax.dynamic_slice_in_dim(near, me["y"] * band_cols, band_cols, 1)
-    gram_next = gram_update(gram_in, own, col, part, share)
-    return gram_next, query_next.reshape(queries.shape), scores
+    query_next, scores, gram_next = panel(
+        where,
+        diags,
+        belows,
+        near,
+        far,
+        heads,
+        queries.reshape(-1, band_rows),
+        gram_in.reshape(-1, band_cols),
+        seqs,
+        share,
+    )
+    return gram_next.reshape(gram_in.shape), query_next.reshape(queries.shape), scores
 
 
 def solution(mesh):

time: 345 us -> 347 us (level); the launches traced: 341 us -> 350 us
  Pallas kernels: 92.4 us -> 104 us
  waiting for transfers between devices: 147 us -> 139 us
    pallas_call x1, Pallas kernels: 61 us -> 84 us  [panel(): pl.pallas_call(functools.partial(panel_kernel, share, seqs), out_shape=[j...]
    pallas_call x1 -> x0, Pallas kernels: 10.8 us -> none  [gram_update(): pl.pallas_call(functools.partial(gram_kernel, share), out_shape=jax.Shape...]
    ppermute x41, waiting for transfers between devices: 147 us -> 139 us  [shift(): return lax.ppermute(value, ('rows', 'cols'), pairs)]
    unnamed x81 -> x68, local copies, waits for them, and re-layouts: 16.6 us -> 18.2 us
  transfers between devices with their start and end apart: 41 -> 41, of which waited for: 15 -> 15; matrix products, arithmetic and copies ran while one was open for 9% -> 10% of each run, Pallas kernels for 6% -> 6%
where the time goes in v5:
time: 347 us; the launch traced here: 350 us
  waiting for transfers between devices  139 us (40%)
  Pallas kernels  104 us (30%)
  starting transfers between devices  53.4 us (15%)
  local copies, waits for them, and re-layouts  28.3 us (8%)
  other arithmetic  17.2 us (5%)
  between operations  7.23 us (2%)
    ppermute x41, waiting for transfers between devices, shift(): return lax.ppermute(value, ('rows', 'cols'), pairs)  139 us
    pallas_call x1, Pallas kernels, panel(): pl.pallas_call(functools.partial(panel_kernel, share, seqs), out_shape=[j...  84 us
    ppermute x41, starting transfers between devices, shift(): return lax.ppermute(value, ('rows', 'cols'), pairs)  53.4 us
    pallas_call x1, Pallas kernels, gradient(): pl.pallas_call(gradient_kernel, out_shape=[jax.ShapeDtypeStruct((4, heigh...  20 us
    unnamed x68, local copies, waits for them, and re-layouts  18.2 us
  transfers between devices with their start and end apart: 41, of which 15 were waited for; matrix products, arithmetic and copies ran while one was open for 10% of the time, Pallas kernels for 6%

profile of v5, /device:TPU:9, one launch (start us, length us, event | category | flops | bytes accessed | tf_op | source)
XLA Modules:
  0.0 349.7 jit_solution(12124603520910216210)
XLA Ops:
  0.6 2.7 fusion.13
  3.4 3.2 collective-permute-start
  6.6 2.1 collective-permute-start.1
  10.0 2.8 copy.23
  12.9 3.8 %copy.24 = bf16[512,1792]{0,1:T(8,128)(2,1)} copy(bf16[512,1792]{1,0:T(8,128)(2,1)} %param.14) | data formatting | bytes 3670016 | tf_op args[3]
  16.7 3.4 fusion.1
  22.5 26.6 %collective-permute-done.2.refs_15_ = bf16[2,448,512]{2,1,0:T(8,128)(2,1)S(1)} collective-permute-done((bf16[2,448,512]{2,1,0:T(8,128)(2,1)}, bf16[2,448,512]{2,1,0:T(8,128)(2,1)S(1)}, u32[]{:S(2)}, u32[]{:S(2)}) %collective-permute-start.2) | collective-permute-done | bytes 917536 | tf_op jit(solution)/shard_map/ppermute | solution.py:492
  50.4 3.2 collective-permute-start.5
  53.6 5.1 %collective-permute-start.6 = (bf16[2,256,1024]{2,1,0:T(8,128)(2,1)}, bf16[2,256,1024]{2,1,0:T(8,128)(2,1)S(1)}, u32[]{:S(2)}, u32[]{:S(2)}) collective-permute-start(bf16[2,256,1024]{2,1,0:T(8,128)(2,1)} %collective-permute-done.1), channel_id=1, source_target_pairs={{8,0},{9,1},{10,2},{11,3},{12,4},{13,5},{14,6},{15,7},{16,8},{17,9... | collective-permute-start | bytes 3145736 | tf_op jit(solution)/shard_map/ppermute | solution.py:492
  58.8 2.3 broadcast_select_fusion.refs_2_
  63.6 4.5 %slice.96 = f32[7,128,1,256]{3,2,1,0:T(1,128)} slice(f32[8,128,8,256]{3,2,1,0:T(8,128)} %param.19), slice={[1:8], [0:128], [0:1], [0:256]} | slice | bytes 1835008 | tf_op jit(solution)/shard_map/slice | solution.py:583
  70.0 2.2 copy.35
  73.1 26.2 %collective-permute-done.7.refs_19_ = bf16[2,448,512]{2,1,0:T(8,128)(2,1)} collective-permute-done((bf16[2,448,512]{2,1,0:T(8,128)(2,1)}, bf16[2,448,512]{2,1,0:T(8,128)(2,1)}, u32[]{:S(2)}, u32[]{:S(2)}) %collective-permute-start.7) | collective-permute-done | bytes 917536 | tf_op jit(solution)/shard_map/ppermute | solution.py:492
  102.2 5.5 %collective-permute-start.10 = (bf16[2,256,1024]{2,1,0:T(8,128)(2,1)}, bf16[2,256,1024]{2,1,0:T(8,128)(2,1)}, u32[]{:S(2)}, u32[]{:S(2)}) collective-permute-start(bf16[2,256,1024]{2,1,0:T(8,128)(2,1)} %get-tuple-element.116), channel_id=1, source_target_pairs={{8,0},{9,1},{10,2},{11,3},{12,4},{13,5},{14,6},{15,7},{16,24},{17,... | collective-permute-start | bytes 3145736 | tf_op jit(solution)/shard_map/ppermute | solution.py:492
  112.9 2.4 pad_maximum_fusion
  115.4 3.3 collective-permute-done.14.b2_ref
  118.7 30.6 %collective-permute-done.11.refs_17_ = bf16[2,448,512]{2,1,0:T(8,128)(2,1)S(1)} collective-permute-done((bf16[2,448,512]{2,1,0:T(8,128)(2,1)}, bf16[2,448,512]{2,1,0:T(8,128)(2,1)S(1)}, u32[]{:S(2)}, u32[]{:S(2)}) %collective-permute-start.11) | collective-permute-done | bytes 917536 | tf_op jit(solution)/shard_map/ppermute | solution.py:492
  151.0 2.4 select_select_fusion.refs_6_
  157.3 3.2 collective-permute-done.19
  160.5 3.1 collective-permute-start.20
  163.6 14.4 %collective-permute-done.20 = f32[320,256]{1,0:T(8,128)S(1)} collective-permute-done((f32[320,256]{1,0:T(8,128)S(1)}, f32[320,256]{1,0:T(8,128)S(1)}, u32[]{:S(2)}, u32[]{:S(2)}) %collective-permute-start.20) | collective-permute-done | bytes 327712 | tf_op jit(solution)/shard_map/ppermute | solution.py:492
  188.9 20.0 %gradient.1 = (f32[4,256,64]{2,1,0:T(8,128)}, f32[256,128]{1,0:T(8,128)}) custom-call(s32[4]{0:T(128)} %pad_add_fusion.spot_ref, bf16[2,256,1024]{2,1,0:T(8,128)(2,1)} %get-tuple-element.118.refs_0_, bf16[2,256,1024]{2,1,0:T(8,128)(2,1)} %collective-permute-done.3.refs_1_, bf16[2,256,1024]{2,1,0:T(8,128)(2,1)} %broadcast_select_fusion.refs_2_, ...), custom_call_target="tpu_custom_call" | custom-call | flops 15032385536 | bytes 24117248 | tf_op jit(solution)/shard_map/gradient/pallas_call | solution.py:543
  211.6 3.4 collective-permute-start.29
  216.2 7.0 %collective-permute-done.29 = f32[256,64]{1,0:T(8,128)S(1)} collective-permute-done((f32[256,64]{1,0:T(8,128)S(1)}, f32[256,64]{1,0:T(8,128)S(1)}, u32[]{:S(2)}, u32[]{:S(2)}) %collective-permute-start.29) | collective-permute-done | bytes 65568 | tf_op jit(solution)/shard_map/ppermute | solution.py:492
  223.1 4.0 %collective-permute-done.28 = f32[256,64]{1,0:T(8,128)S(1)} collective-permute-done((f32[256,64]{1,0:T(8,128)S(1)}, f32[256,64]{1,0:T(8,128)S(1)}, u32[]{:S(2)}, u32[]{:S(2)}) %collective-permute-start.28) | collective-permute-done | bytes 65568 | tf_op jit(solution)/shard_map/ppermute | solution.py:492
  230.4 6.0 %collective-permute-done.32 = f32[256,64]{1,0:T(8,128)S(1)} collective-permute-done((f32[256,64]{1,0:T(8,128)S(1)}, f32[256,64]{1,0:T(8,128)S(1)}, u32[]{:S(2)}, u32[]{:S(2)}) %collective-permute-start.32) | collective-permute-done | bytes 65568 | tf_op jit(solution)/shard_map/ppermute | solution.py:492
  236.3 3.4 collective-permute-done.33
  241.8 2.7 collective-permute-done.34
  244.6 3.5 %collective-permute-start.38 = (f32[64,512]{1,0:T(8,128)S(1)}, f32[64,512]{1,0:T(8,128)S(1)}, u32[]{:S(2)}, u32[]{:S(2)}) collective-permute-start(f32[64,512]{1,0:T(8,128)S(1)} %pad_maximum_fusion.4), channel_id=1, source_target_pairs={{0,16},{1,17},{2,18},{3,19},{4,20},{5,21},{6,22},{7,23},{8,24},{9,... | collective-permute-start | bytes 393224 | tf_op jit(solution)/shard_map/ppermute | solution.py:492
  250.4 5.8 %collective-permute-done.38 = f32[64,512]{1,0:T(8,128)S(1)} collective-permute-done((f32[64,512]{1,0:T(8,128)S(1)}, f32[64,512]{1,0:T(8,128)S(1)}, u32[]{:S(2)}, u32[]{:S(2)}) %collective-permute-start.38) | collective-permute-done | bytes 131104 | tf_op jit(solution)/shard_map/ppermute | solution.py:492
  256.3 4.0 %collective-permute-done.39 = f32[64,512]{1,0:T(8,128)S(1)} collective-permute-done((f32[64,512]{1,0:T(8,128)S(1)}, f32[64,512]{1,0:T(8,128)S(1)}, u32[]{:S(2)}, u32[]{:S(2)}) %collective-permute-start.39) | collective-permute-done | bytes 131104 | tf_op jit(solution)/shard_map/ppermute | solution.py:492
  264.1 84.0 %panel_factor.1 = (f32[512,128]{1,0:T(8,128)}, f32[64,4]{1,0:T(8,128)}, f32[8192,256]{1,0:T(8,128)}) custom-call(s32[2]{0:T(128)} %pad_add_fusion.1.spot_ref, f32[1024,256]{1,0:T(8,128)} %copy-done.3, f32[1024,256]{1,0:T(8,128)} %copy-done.4, f32[1024,256]{1,0:T(8,128)} %collective-permute-done.27.d2_ref, f32[1024,256]{1,0:T(8,128)} %copy-done.5, ...), custom_call_target="tpu_custom_call" | custom-call | tf_op jit(solution)/shard_map/panel_factor/pallas_call | solution.py:360
  (150 shorter events, 45.4 us)
Async XLA Ops:
  3.4 45.8 %collective-permute-start = (bf16[2,256,1024]{2,1,0:T(8,128)(2,1)}, bf16[2,256,1024]{2,1,0:T(8,128)(2,1)S(1)}, u32[]{:S(2)}, u32[]{:S(2)}) collective-permute-start(bf16[2,256,1024]{2,1,0:T(8,128)(2,1)} %get-tuple-element.118.refs_0_), channel_id=1, source_target_pairs={{0,8},{1,9},{2,10},{3,11},{4,12},{5,13},{6,14},{7,15},{8,16},{9,17... | collective-permute-start | bytes 3145736 | tf_op jit(solution)/shard_map/ppermute | solution.py:492
  6.6 42.6 %collective-permute-start.1 = (bf16[2,256,1024]{2,1,0:T(8,128)(2,1)}, bf16[2,256,1024]{2,1,0:T(8,128)(2,1)}, u32[]{:S(2)}, u32[]{:S(2)}) collective-permute-start(bf16[2,256,1024]{2,1,0:T(8,128)(2,1)} %get-tuple-element.118.refs_0_), channel_id=1, source_target_pairs={{8,0},{9,1},{10,2},{11,3},{12,4},{13,5},{14,6},{15,7},{16,8},{17,9... | collective-permute-start | bytes 3145736 | tf_op jit(solution)/shard_map/ppermute | solution.py:492
  8.7 40.5 %collective-permute-start.3 = (bf16[2,256,1024]{2,1,0:T(8,128)(2,1)}, bf16[2,256,1024]{2,1,0:T(8,128)(2,1)}, u32[]{:S(2)}, u32[]{:S(2)}) collective-permute-start(bf16[2,256,1024]{2,1,0:T(8,128)(2,1)} %get-tuple-element.118.refs_0_), channel_id=1, source_target_pairs={{0,2},{1,3},{2,0},{3,1},{4,6},{5,7},{6,4},{7,5},{8,10},{9,11},{10,... | collective-permute-start | bytes 3145736 | tf_op jit(solution)/shard_map/ppermute | solution.py:492
  20.1 29.1 %collective-permute-start.2 = (bf16[2,448,512]{2,1,0:T(8,128)(2,1)}, bf16[2,448,512]{2,1,0:T(8,128)(2,1)S(1)}, u32[]{:S(2)}, u32[]{:S(2)}) collective-permute-start(bf16[2,448,512]{2,1,0:T(8,128)(2,1)} %get-tuple-element.112), channel_id=1, source_target_pairs={{0,8},{1,9},{2,10},{3,11},{4,12},{5,13},{6,14},{7,15},{8,16},{9,17... | collective-permute-start | bytes 2752520 | tf_op jit(solution)/shard_map/ppermute | solution.py:492
  21.3 27.9 %collective-permute-start.4 = (bf16[2,448,512]{2,1,0:T(8,128)(2,1)}, bf16[2,448,512]{2,1,0:T(8,128)(2,1)S(1)}, u32[]{:S(2)}, u32[]{:S(2)}) collective-permute-start(bf16[2,448,512]{2,1,0:T(8,128)(2,1)} %get-tuple-element.113.refs_13_), channel_id=1, source_target_pairs={{0,4},{1,5},{2,6},{3,7},{4,0},{5,1},{6,2},{7,3},{8,12},{9,13},{10,... | collective-permute-start | bytes 2752520 | tf_op jit(solution)/shard_map/ppermute | solution.py:492
  50.4 50.1 %collective-permute-start.5 = (bf16[2,256,1024]{2,1,0:T(8,128)(2,1)S(1)}, bf16[2,256,1024]{2,1,0:T(8,128)(2,1)S(1)}, u32[]{:S(2)}, u32[]{:S(2)}) collective-permute-start(bf16[2,256,1024]{2,1,0:T(8,128)(2,1)S(1)} %collective-permute-done), channel_id=1, source_target_pairs={{0,8},{1,9},{2,10},{3,11},{4,12},{5,13},{6,14},{7,15},{8,16},{9,17... | collective-permute-start | bytes 3145736 | tf_op jit(solution)/shard_map/ppermute | solution.py:492
  53.6 46.9 %collective-permute-start.6 = (bf16[2,256,1024]{2,1,0:T(8,128)(2,1)}, bf16[2,256,1024]{2,1,0:T(8,128)(2,1)S(1)}, u32[]{:S(2)}, u32[]{:S(2)}) collective-permute-start(bf16[2,256,1024]{2,1,0:T(8,128)(2,1)} %collective-permute-done.1), channel_id=1, source_target_pairs={{8,0},{9,1},{10,2},{11,3},{12,4},{13,5},{14,6},{15,7},{16,8},{17,9... | collective-permute-start | bytes 3145736 | tf_op jit(solution)/shard_map/ppermute | solution.py:492
  61.1 39.5 %collective-permute-start.8 = (bf16[2,256,1024]{2,1,0:T(8,128)(2,1)}, bf16[2,256,1024]{2,1,0:T(8,128)(2,1)}, u32[]{:S(2)}, u32[]{:S(2)}) collective-permute-start(bf16[2,256,1024]{2,1,0:T(8,128)(2,1)} %broadcast_select_fusion.refs_2_), channel_id=1, source_target_pairs={{0,2},{1,3},{2,0},{3,1},{4,6},{5,7},{6,4},{7,5},{8,10},{9,11},{10,... | collective-permute-start | bytes 3145736 | tf_op jit(solution)/shard_map/ppermute | solution.py:492
  62.3 37.0 %collective-permute-start.7 = (bf16[2,448,512]{2,1,0:T(8,128)(2,1)}, bf16[2,448,512]{2,1,0:T(8,128)(2,1)}, u32[]{:S(2)}, u32[]{:S(2)}) collective-permute-start(bf16[2,448,512]{2,1,0:T(8,128)(2,1)} %get-tuple-element.56), channel_id=1, source_target_pairs={{0,24},{1,25},{2,26},{3,27},{4,28},{5,29},{6,30},{7,31},{8,0},{9,1... | collective-permute-start | bytes 2752520 | tf_op jit(solution)/shard_map/ppermute | solution.py:492
  62.3 38.2 %collective-permute-start.9 = (bf16[2,448,512]{2,1,0:T(8,128)(2,1)}, bf16[2,448,512]{2,1,0:T(8,128)(2,1)}, u32[]{:S(2)}, u32[]{:S(2)}) collective-permute-start(bf16[2,448,512]{2,1,0:T(8,128)(2,1)} %copy-done.17), channel_id=1, source_target_pairs={{0,4},{1,5},{2,6},{3,7},{4,0},{5,1},{6,2},{7,3},{8,12},{9,13},{10,... | collective-permute-start | bytes 2752520 | tf_op jit(solution)/shard_map/ppermute | solution.py:492
  99.3 19.4 %collective-permute-start.14 = (f32[896,256]{1,0:T(8,128)}, f32[896,256]{1,0:T(8,128)}, u32[]{:S(2)}, u32[]{:S(2)}) collective-permute-start(f32[896,256]{1,0:T(8,128)} %bitcast.62), channel_id=1, source_target_pairs={{0,2},{1,3},{2,0},{3,1},{4,6},{5,7},{6,4},{7,5},{8,10},{9,11},{10,... | collective-permute-start | bytes 2752520 | tf_op jit(solution)/shard_map/ppermute | solution.py:492
  102.2 47.2 %collective-permute-start.10 = (bf16[2,256,1024]{2,1,0:T(8,128)(2,1)}, bf16[2,256,1024]{2,1,0:T(8,128)(2,1)}, u32[]{:S(2)}, u32[]{:S(2)}) collective-permute-start(bf16[2,256,1024]{2,1,0:T(8,128)(2,1)} %get-tuple-element.116), channel_id=1, source_target_pairs={{8,0},{9,1},{10,2},{11,3},{12,4},{13,5},{14,6},{15,7},{16,24},{17,... | collective-permute-start | bytes 3145736 | tf_op jit(solution)/shard_map/ppermute | solution.py:492
  107.7 41.6 %collective-permute-start.12 = (bf16[2,256,1024]{2,1,0:T(8,128)(2,1)}, bf16[2,256,1024]{2,1,0:T(8,128)(2,1)}, u32[]{:S(2)}, u32[]{:S(2)}) collective-permute-start(bf16[2,256,1024]{2,1,0:T(8,128)(2,1)} %get-tuple-element.115.refs_4_), channel_id=1, source_target_pairs={{0,2},{1,3},{2,0},{3,1},{4,6},{5,7},{6,4},{7,5},{8,10},{9,11},{10,... | collective-permute-start | bytes 3145736 | tf_op jit(solution)/shard_map/ppermute | solution.py:492
  109.5 39.8 %collective-permute-start.11 = (bf16[2,448,512]{2,1,0:T(8,128)(2,1)}, bf16[2,448,512]{2,1,0:T(8,128)(2,1)S(1)}, u32[]{:S(2)}, u32[]{:S(2)}) collective-permute-start(bf16[2,448,512]{2,1,0:T(8,128)(2,1)} %get-tuple-element.60), channel_id=1, source_target_pairs={{0,16},{1,17},{2,18},{3,19},{4,20},{5,21},{6,22},{7,23},{8,24},{9,... | collective-permute-start | bytes 2752520 | tf_op jit(solution)/shard_map/ppermute | solution.py:492
  109.5 39.8 %collective-permute-start.13 = (bf16[2,448,512]{2,1,0:T(8,128)(2,1)}, bf16[2,448,512]{2,1,0:T(8,128)(2,1)S(1)}, u32[]{:S(2)}, u32[]{:S(2)}) collective-permute-start(bf16[2,448,512]{2,1,0:T(8,128)(2,1)} %collective-permute-done.7.refs_19_), channel_id=1, source_target_pairs={{0,4},{1,5},{2,6},{3,7},{4,0},{5,1},{6,2},{7,3},{8,12},{9,13},{10,... | collective-permute-start | bytes 2752520 | tf_op jit(solution)/shard_map/ppermute | solution.py:492
  150.3 28.4 %collective-permute-start.17 = (bf16[4,2,256,1024]{3,2,1,0:T(8,128)(2,1)S(1)}, bf16[4,2,256,1024]{3,2,1,0:T(8,128)(2,1)S(1)}, u32[]{:S(2)}, u32[]{:S(2)}) collective-permute-start(bf16[4,2,256,1024]{3,2,1,0:T(8,128)(2,1)S(1)} %pad_maximum_fusion), channel_id=1, source_target_pairs={{0,1},{1,0},{2,3},{3,2},{4,5},{5,4},{6,7},{7,6},{8,9},{9,8},{10,11... | collective-permute-start | bytes 12582920 | tf_op jit(solution)/shard_map/ppermute | solution.py:492
  151.0 27.6 %collective-permute-start.18 = (bf16[2,256,1024]{2,1,0:T(8,128)(2,1)}, bf16[2,256,1024]{2,1,0:T(8,128)(2,1)S(1)}, u32[]{:S(2)}, u32[]{:S(2)}) collective-permute-start(bf16[2,256,1024]{2,1,0:T(8,128)(2,1)} %get-tuple-element.115.refs_4_), channel_id=1, source_target_pairs={{0,1},{1,0},{2,3},{3,2},{4,5},{5,4},{6,7},{7,6},{8,9},{9,8},{10,11... | collective-permute-start | bytes 3145736 | tf_op jit(solution)/shard_map/ppermute | solution.py:492
  153.4 25.3 %collective-permute-start.15 = (bf16[2,256,1024]{2,1,0:T(8,128)(2,1)}, bf16[2,256,1024]{2,1,0:T(8,128)(2,1)S(1)}, u32[]{:S(2)}, u32[]{:S(2)}) collective-permute-start(bf16[2,256,1024]{2,1,0:T(8,128)(2,1)} %select_select_fusion.refs_6_), channel_id=1, source_target_pairs={{0,2},{1,3},{2,0},{3,1},{4,6},{5,7},{6,4},{7,5},{8,10},{9,11},{10,... | collective-permute-start | bytes 3145736 | tf_op jit(solution)/shard_map/ppermute | solution.py:492
  154.7 24.0 %collective-permute-start.16 = (bf16[2,448,512]{2,1,0:T(8,128)(2,1)S(1)}, bf16[2,448,512]{2,1,0:T(8,128)(2,1)S(1)}, u32[]{:S(2)}, u32[]{:S(2)}) collective-permute-start(bf16[2,448,512]{2,1,0:T(8,128)(2,1)S(1)} %collective-permute-done.11.refs_17_), channel_id=1, source_target_pairs={{0,4},{1,5},{2,6},{3,7},{4,0},{5,1},{6,2},{7,3},{8,12},{9,13},{10,... | collective-permute-start | bytes 2752520 | tf_op jit(solution)/shard_map/ppermute | solution.py:492
  160.5 17.5 %collective-permute-start.20 = (f32[320,256]{1,0:T(8,128)S(1)}, f32[320,256]{1,0:T(8,128)S(1)}, u32[]{:S(2)}, u32[]{:S(2)}) collective-permute-start(f32[320,256]{1,0:T(8,128)S(1)} %pad_maximum_fusion.3), channel_id=1, source_target_pairs={{0,16},{1,17},{2,18},{3,19},{4,20},{5,21},{6,22},{7,23},{8,24},{9,... | collective-permute-start | bytes 983048 | tf_op jit(solution)/shard_map/ppermute | solution.py:492
  178.0 10.0 %collective-permute-start.22 = (bf16[2,256,1024]{2,1,0:T(8,128)(2,1)}, bf16[2,256,1024]{2,1,0:T(8,128)(2,1)}, u32[]{:S(2)}, u32[]{:S(2)}) collective-permute-start(bf16[2,256,1024]{2,1,0:T(8,128)(2,1)} %select_select_fusion.refs_6_), channel_id=1, source_target_pairs={{0,1},{1,0},{2,3},{3,2},{4,5},{5,4},{6,7},{7,6},{8,9},{9,8},{10,11... | collective-permute-start | bytes 3145736 | tf_op jit(solution)/shard_map/ppermute | solution.py:492
  188.0 20.9 %collective-permute-start.24 = (f32[640,256]{1,0:T(8,128)S(1)}, f32[640,256]{1,0:T(8,128)S(1)}, u32[]{:S(2)}, u32[]{:S(2)}) collective-permute-start(f32[640,256]{1,0:T(8,128)S(1)} %pad_maximum_fusion.2), channel_id=1, source_target_pairs={{0,4},{1,5},{2,6},{3,7},{4,0},{5,1},{6,2},{7,3},{8,12},{9,13},{10,... | collective-permute-start | bytes 1966088 | tf_op jit(solution)/shard_map/ppermute | solution.py:492
  188.4 20.5 %collective-permute-start.25 = (f32[896,256]{1,0:T(8,128)S(1)}, f32[896,256]{1,0:T(8,128)S(1)}, u32[]{:S(2)}, u32[]{:S(2)}) collective-permute-start(f32[896,256]{1,0:T(8,128)S(1)} %bitcast.64), channel_id=1, source_target_pairs={{0,1},{1,0},{2,3},{3,2},{4,5},{5,4},{6,7},{7,6},{8,9},{9,8},{10,11... | collective-permute-start | bytes 2752520 | tf_op jit(solution)/shard_map/ppermute | solution.py:492
  188.9 20.1 %collective-permute-start.26 = (f32[896,256]{1,0:T(8,128)}, f32[896,256]{1,0:T(8,128)S(1)}, u32[]{:S(2)}, u32[]{:S(2)}) collective-permute-start(f32[896,256]{1,0:T(8,128)} %collective-permute-done.14.b2_ref), channel_id=1, source_target_pairs={{0,1},{1,0},{2,3},{3,2},{4,5},{5,4},{6,7},{7,6},{8,9},{9,8},{10,11... | collective-permute-start | bytes 2752520 | tf_op jit(solution)/shard_map/ppermute | solution.py:492
  209.2 35.4 %collective-permute-start.27 = (f32[1024,256]{1,0:T(8,128)S(1)}, f32[1024,256]{1,0:T(8,128)}, u32[]{:S(2)}, u32[]{:S(2)}) collective-permute-start(f32[1024,256]{1,0:T(8,128)S(1)} %slice_dynamic-update-slice_fusion.d0_ref), channel_id=1, source_target_pairs={{0,2},{1,3},{2,0},{3,1},{4,6},{5,7},{6,4},{7,5},{8,10},{9,11},{10,... | collective-permute-start | bytes 3145736 | tf_op jit(solution)/shard_map/ppermute | solution.py:492
  211.6 11.5 %collective-permute-start.29 = (f32[256,64]{1,0:T(8,128)S(1)}, f32[256,64]{1,0:T(8,128)S(1)}, u32[]{:S(2)}, u32[]{:S(2)}) collective-permute-start(f32[256,64]{1,0:T(8,128)S(1)} %get-tuple-element.121), channel_id=1, source_target_pairs={{0,16},{1,17},{2,18},{3,19},{4,20},{5,21},{6,22},{7,23},{8,24},{9,... | collective-permute-start | bytes 196616 | tf_op jit(solution)/shard_map/ppermute | solution.py:492
  215.0 12.1 %collective-permute-start.28 = (f32[256,64]{1,0:T(8,128)S(1)}, f32[256,64]{1,0:T(8,128)S(1)}, u32[]{:S(2)}, u32[]{:S(2)}) collective-permute-start(f32[256,64]{1,0:T(8,128)S(1)} %get-tuple-element.119), channel_id=1, source_target_pairs={{0,24},{1,25},{2,26},{3,27},{4,28},{5,29},{6,30},{7,31},{8,0},{9,1... | collective-permute-start | bytes 196616 | tf_op jit(solution)/shard_map/ppermute | solution.py:492
  228.9 10.8 %collective-permute-start.33 = (f32[256,64]{1,0:T(8,128)S(1)}, f32[256,64]{1,0:T(8,128)S(1)}, u32[]{:S(2)}, u32[]{:S(2)}) collective-permute-start(f32[256,64]{1,0:T(8,128)S(1)} %fusion.9), channel_id=1, source_target_pairs={{0,3},{1,2},{2,1},{3,0},{4,7},{5,6},{6,5},{7,4},{8,11},{9,10},{10,... | collective-permute-start | bytes 196616 | tf_op jit(solution)/shard_map/ppermute | solution.py:492
  244.6 11.6 %collective-permute-start.38 = (f32[64,512]{1,0:T(8,128)S(1)}, f32[64,512]{1,0:T(8,128)S(1)}, u32[]{:S(2)}, u32[]{:S(2)}) collective-permute-start(f32[64,512]{1,0:T(8,128)S(1)} %pad_maximum_fusion.4), channel_id=1, source_target_pairs={{0,16},{1,17},{2,18},{3,19},{4,20},{5,21},{6,22},{7,23},{8,24},{9,... | collective-permute-start | bytes 393224 | tf_op jit(solution)/shard_map/ppermute | solution.py:492
  248.2 14.4 %collective-permute-start.35 = (f32[1024,256]{1,0:T(8,128)S(1)}, f32[1024,256]{1,0:T(8,128)S(1)}, u32[]{:S(2)}, u32[]{:S(2)}) collective-permute-start(f32[1024,256]{1,0:T(8,128)S(1)} %slice_dynamic-update-slice_fusion.d0_ref), channel_id=1, source_target_pairs={{0,1},{1,0},{2,3},{3,2},{4,5},{5,4},{6,7},{7,6},{8,9},{9,8},{10,11... | collective-permute-start | bytes 3145736 | tf_op jit(solution)/shard_map/ppermute | solution.py:492
  249.4 13.2 %collective-permute-start.36 = (f32[1024,256]{1,0:T(8,128)}, f32[1024,256]{1,0:T(8,128)S(1)}, u32[]{:S(2)}, u32[]{:S(2)}) collective-permute-start(f32[1024,256]{1,0:T(8,128)} %collective-permute-done.27.d2_ref), channel_id=1, source_target_pairs={{0,1},{1,0},{2,3},{3,2},{4,5},{5,4},{6,7},{7,6},{8,9},{9,8},{10,11... | collective-permute-start | bytes 3145736 | tf_op jit(solution)/shard_map/ppermute | solution.py:492
  249.4 10.8 %collective-permute-start.39 = (f32[64,512]{1,0:T(8,128)S(1)}, f32[64,512]{1,0:T(8,128)S(1)}, u32[]{:S(2)}, u32[]{:S(2)}) collective-permute-start(f32[64,512]{1,0:T(8,128)S(1)} %pad_maximum_fusion.4), channel_id=1, source_target_pairs={{0,24},{1,25},{2,26},{3,27},{4,28},{5,29},{6,30},{7,31},{8,0},{9,1... | collective-permute-start | bytes 393224 | tf_op jit(solution)/shard_map/ppermute | solution.py:492
  (32 other events, 690.5 us)

commit v6 on v4

--- a/solution.py
+++ b/solution.py
@@ -328,12 +328,17 @@
     )(spot, *diags, *belows, near, far, heads, queries)
 
 
-def gram_kernel(share, gram_ref, own_ref, col_ref, panel_ref, out_ref):
+def gram_kernel(share, gram_ref, own_ref, col_ref, panel_ref, out_ref, right_ref):
     steps, seqs, count = own_ref.shape
     cycles, lanes = col_ref.shape[0] // seqs, col_ref.shape[1]
-    right = jnp.concatenate(
-        [pack_right(col_ref[pl.ds(b, seqs, stride=cycles), :]) for b in range(cycles)], axis=1
-    )
+
+    @pl.when(pl.program_id(1) == 0)
+    def _():
+        for b in range(cycles):
+            side = pack_right(col_ref[pl.ds(b, seqs, stride=cycles), :])
+            right_ref[:, b * lanes : (b + 1) * lanes] = side
+
+    right = right_ref[...]
     for a in range(steps):
         base = a * count * cycles
         out_ref[pl.ds(base, count, stride=cycles), :] = panel_ref[a]
@@ -361,6 +366,7 @@
             pl.BlockSpec((steps, count, lanes), lambda v, a: (a, 0, v)),
         ],
         out_specs=tall,
+        scratch_shapes=[pltpu.VMEM((6 * seqs, cycles * lanes), jnp.bfloat16)],
         compiler_params=pltpu.CompilerParams(vmem_limit_bytes=vmem_limit),
         name="gram_update",
     )(gram, own, col, part.reshape(cycles, count, width)).reshape(gram_in.shape)
@@ -484,43 +490,52 @@
 def gradient_kernel(spot_ref, *refs):
     token_refs, refs = refs[:13], refs[13:]
     weight_refs, refs = refs[:8], refs[8:]
-    out_proj_ref, in_proj_ref, outer_ref, inner_ref, token_buf, weight_buf, token_sem, weight_sem = refs
+    out_proj_ref, in_proj_ref, outer_ref, inner_ref, weight_buf, weight_sem = refs
     z, x, y, core = (spot_ref[i] for i in range(4))
     height, band = token_refs[0].shape[1:]
-    near, group = token_refs[:8], token_refs[8]
-    far = [group.at[i] for i in range(4)] + list(token_refs[9:])
     depth = weight_refs[0].shape[2]
-    weight_copies = []
+    copies = []
     for i, ref in enumerate(weight_refs):
         row = ((z - i // 2) % 4) * 2 + (x + i % 2) % 2
         there = weight_buf.at[:, :, pl.ds(pl.multiple_of(row * depth, 128), depth)]
-        weight_copies.append(pltpu.make_async_copy(ref, there, weight_sem.at[i]))
-    token_copies = []
-    for i in range(16):
-        ref = (far if i % 2 else near)[i // 2]
-        col = ((y + i % 4 // 2) % 2) * 2 + (core + i % 2) % 2
-        there = token_buf.at[i // 4, :, :, pl.ds(pl.multiple_of(col * band, 128), band)]
-        token_copies.append(pltpu.make_async_copy(ref, there, token_sem.at[i]))
-    for copy in weight_copies + token_copies:
+        copies.append(pltpu.make_async_copy(ref, there, weight_sem.at[i]))
+    for copy in copies:
         copy.start()
-    for copy in weight_copies:
+    near, group = token_refs[:8], token_refs[8]
+    far = [group.at[i] for i in range(4)] + list(token_refs[9:])
+    sides = [far, near]
+    starts = []
+    for j in range(4):
+        col = ((y + j // 2) % 2) * 2 + (core + j % 2) % 2
+        starts.append(pl.multiple_of(col * band, 128))
+    inner = jnp.zeros(inner_ref.shape, jnp.float32)
+    for j in range(4):
+        piece = sides[(j + 1) % 2][j // 2][0]
+        inner = inner + jnp.dot(
+            piece, in_proj_ref[pl.ds(starts[j], band), :], preferred_element_type=jnp.float32
+        )
+    inner_ref[...] = inner
+    for copy in copies:
         copy.wait()
+
+    def product(kind):
+        result = None
+        for j in range(4):
+            rows = [sides[(j + 1) % 2][2 * s + j // 2][kind] for s in range(4)]
+            term = lax.dot_general(
+                jnp.concatenate(rows, axis=0),
+                weight_buf[kind, :, pl.ds(starts[j], band)],
+                (((1,), (1,)), ((), ())),
+                preferred_element_type=jnp.float32,
+            )
+            result = term if result is None else result + term
+        return result
+
+    gate, hidden = product(0), product(1)
+    grad = (hidden * (gate / (1.0 + jnp.exp(-gate)))).astype(jnp.bfloat16)
+    outer = jnp.dot(grad, out_proj_ref[...], preferred_element_type=jnp.float32)
     for s in range(4):
-        for copy in token_copies[4 * s : 4 * s + 4]:
-            copy.wait()
-        if s == 0:
-            inner_ref[...] = jnp.dot(
-                token_buf[0, 0], in_proj_ref[...], preferred_element_type=jnp.float32
-            )
-        over = (((1,), (1,)), ((), ()))
-        gate = lax.dot_general(
-            token_buf[s, 0], weight_buf[0], over, preferred_element_type=jnp.float32
-        )
-        hidden = lax.dot_general(
-            token_buf[s, 1], weight_buf[1], over, preferred_element_type=jnp.float32
-        )
-        grad = (hidden * (gate / (1.0 + jnp.exp(-gate)))).astype(jnp.bfloat16)
-        outer_ref[s] = jnp.dot(grad, out_proj_ref[...], preferred_element_type=jnp.float32)
+        outer_ref[s] = outer[s * height : (s + 1) * height]
 
 
 def gradient(spot, tokens, weights, out_proj, in_proj):
@@ -535,12 +550,10 @@
             jax.ShapeDtypeStruct((4, height, out_proj.shape[1]), jnp.float32),
             jax.ShapeDtypeStruct((height, in_proj.shape[1]), jnp.float32),
         ],
-        in_specs=[pl.BlockSpec(memory_space=pltpu.SMEM)] + [hbm] * 21 + [whole] * 2,
+        in_specs=[pl.BlockSpec(memory_space=pltpu.SMEM)] + [whole] * 13 + [hbm] * 8 + [whole] * 2,
         out_specs=[whole] * 2,
         scratch_shapes=[
-            pltpu.VMEM((4, kinds, height, full), jnp.bfloat16),
             pltpu.VMEM((kinds, share, full), jnp.bfloat16),
-            pltpu.SemaphoreType.DMA((16,)),
             pltpu.SemaphoreType.DMA((8,)),
         ],
         compiler_params=pltpu.CompilerParams(vmem_limit_bytes=vmem_limit),
@@ -558,7 +571,7 @@
     return lax.optimization_barrier((*values, *after))[:count]
 
 
-def rounds(tokens, cotangent, gate_weight, down_weight, gram_in, queries, me):
+def rounds(tokens, cotangent, gate_weight, down_weight, gram_in, queries, me, early):
     z = me["z"]
     both = jnp.stack([tokens, cotangent])
     depth, width = gate_weight.shape
@@ -594,8 +607,8 @@
     wz2 = shift(p2, "z", 2)
     below_y = shift(below, "y", 1)
     group = jnp.stack([both, y_own, slot_a, y_a])
-    last, wz2, y_b, wx3, below_y, group, small = tie(
-        (last, wz2, y_b, wx3, below_y, group, small)
+    last, wz2, y_b, wx3, below_y, group, small, *early = tie(
+        (last, wz2, y_b, wx3, below_y, group, small, *early)
     )
 
     slot_c = jnp.where(z == 0, last, jnp.where(z == 1, down2, jnp.where(z == 2, up2, last)))
@@ -617,7 +630,7 @@
     belows = [below, below_c, below_y, below_cy]
     pieces = [both, y_own, slot_a, y_a, slot_b, y_b, slot_c, y_c, core_1, c_b, cy_b, c_c, cy_c]
     weights = [piece[0], wx0, wz1, wx1, wz2, wx2, wz3, wx3]
-    return pieces, weights, small, across, belows
+    return pieces, weights, small, across, belows, early
 
 
 def local(
@@ -634,12 +647,16 @@
 ):
     row_index, col_index = lax.axis_index("rows"), lax.axis_index("cols")
     me = {"z": row_index // 2, "x": row_index % 2, "y": col_index // 2, "core": col_index % 2}
-    pieces, weights, small, across, belows = rounds(
-        tokens, cotangent, gate_weight, down_weight, gram_in, queries, me
-    )
-    share = weights[0].shape[1]
+    share = gate_weight.shape[1] // 4
     out_proj = lax.dynamic_slice_in_dim(proj_out, me["z"] * share, share, 0)
     spot = jnp.stack([me["z"], me["x"], me["y"], me["core"]]).astype(jnp.int32)
+    where = jnp.stack([row_index, col_index]).astype(jnp.int32)
+    table = jnp.array(slot_of, jnp.int32)
+    early = [spot, where, out_proj] + [table[me["z"], s] for s in range(1, 4)]
+    pieces, weights, small, across, belows, early = rounds(
+        tokens, cotangent, gate_weight, down_weight, gram_in, queries, me, early
+    )
+    spot, where, out_proj, *order = early
     outer, proj_inner = gradient(spot, pieces, weights, out_proj, proj_in)
     tied = tie((outer, small, across, *belows))
     outer, small, across, belows = tied[0], tied[1], tied[2], tied[3:]
@@ -648,14 +665,14 @@
     parts = [side[i * rows : (i + 1) * rows] for i in range(4) for side in (small, across)]
     diag = jnp.concatenate([part[:band_rows] for part in parts], axis=0)
     heads = jnp.concatenate([part[band_rows:] for part in parts], axis=0)
-    diag_y = shift(diag, "y", 1)
     proj_outer = outer[0]
-    table = jnp.array(slot_of, jnp.int32)
     for s in range(1, 4):
-        part = lax.dynamic_index_in_dim(outer, table[me["z"], s], 0, False)
+        part = lax.dynamic_index_in_dim(outer, order[s - 1], 0, False)
         proj_outer = proj_outer + shift(part, "z", -s)
     over_y, over_core = shift(proj_outer, "y", 1), shift(proj_outer, "core", 1)
     proj_outer = (proj_outer + over_core) + (over_y + shift(proj_outer, "both", 1))
+    diag, proj_outer = tie((diag, proj_outer))
+    diag_y = shift(diag, "y", 1)
     features = sequence_features(proj_inner, proj_outer, lengths, loss_mask)
     cycles, band_rows, _, band_cols = gram_in.shape
     seqs = features.shape[0]
@@ -666,12 +683,11 @@
     ]
     mine = jnp.concatenate(mine, axis=1)
     pair = jnp.concatenate([mine, shift(mine, "x", 1)], axis=0)
-    diag, diag_y, pair = tie((diag, diag_y, pair))
+    near = jnp.concatenate([pair] + [shift(pair, "z", s) for s in range(1, 4)], axis=0)
+    diag, diag_y, near = tie((diag, diag_y, near))
+    far = shift(near, "core", 1)
     diags = [diag, shift(diag, "core", 1), diag_y, shift(diag_y, "core", 1)]
-    near = jnp.concatenate([pair] + [shift(pair, "z", s) for s in range(1, 4)], axis=0)
-    far = shift(near, "core", 1)
     share = cycles / near.shape[0]
-    where = jnp.stack([row_index, col_index]).astype(jnp.int32)
     part, query_next, scores, own = panel(
         where, diags, belows, near, far, heads, queries.reshape(-1, band_rows), seqs, share
     )

time: 345 us -> 351 us (1.017); the launches traced: 341 us -> 354 us
  Pallas kernels: 92.4 us -> 106 us
  starting transfers between devices: 53.3 us -> 48.9 us
    pallas_call x1, Pallas kernels: 61 us -> 74.9 us  [panel(): pl.pallas_call(functools.partial(panel_kernel, share, seqs), out_shape=[j...]
    ppermute x41, starting transfers between devices: 53.3 us -> 48.9 us  [shift(): return lax.ppermute(value, ('rows', 'cols'), pairs)]
    unnamed x81 -> x68, local copies, waits for them, and re-layouts: 16.6 us -> 18.1 us
  transfers between devices with their start and end apart: 41 -> 41, of which waited for: 15 -> 18; matrix products, arithmetic and copies ran while one was open for 9% -> 10% of each run, Pallas kernels for 6% -> 6%
where the time goes in v6:
time: 351 us; the launch traced here: 354 us
  waiting for transfers between devices  145 us (41%)
  Pallas kernels  106 us (30%)
  starting transfers between devices  48.9 us (14%)
  local copies, waits for them, and re-layouts  29.5 us (8%)
  other arithmetic  17.3 us (5%)
  between operations  6.83 us (2%)
    ppermute x41, waiting for transfers between devices, shift(): return lax.ppermute(value, ('rows', 'cols'), pairs)  145 us
    pallas_call x1, Pallas kernels, panel(): pl.pallas_call(functools.partial(panel_kernel, share, seqs), out_shape=[j...  74.9 us
    ppermute x41, starting transfers between devices, shift(): return lax.ppermute(value, ('rows', 'cols'), pairs)  48.9 us
    pallas_call x1, Pallas kernels, gradient(): pl.pallas_call(gradient_kernel, out_shape=[jax.ShapeDtypeStruct((4, heigh...  19.8 us
    unnamed x68, local copies, waits for them, and re-layouts  18.1 us
    pallas_call x1, Pallas kernels, gram_update(): pl.pallas_call(functools.partial(gram_kernel, share), out_shape=jax.Shape...  11 us
  transfers between devices with their start and end apart: 41, of which 18 were waited for; matrix products, arithmetic and copies ran while one was open for 10% of the time, Pallas kernels for 6%

profile of v6, /device:TPU:9, one launch (start us, length us, event | category | flops | bytes accessed | tf_op | source)
XLA Modules:
  0.0 354.1 jit_solution(18088395847280098530)
XLA Ops:
  0.6 2.7 fusion.13
  3.4 3.2 collective-permute-start
  10.0 2.8 copy.23
  12.9 3.8 %copy.24 = bf16[512,1792]{0,1:T(8,128)(2,1)} copy(bf16[512,1792]{1,0:T(8,128)(2,1)} %param.14) | data formatting | bytes 3670016 | tf_op args[3]
  16.7 3.4 fusion.1
  22.5 26.6 %collective-permute-done.2.refs_15_ = bf16[2,448,512]{2,1,0:T(8,128)(2,1)S(1)} collective-permute-done((bf16[2,448,512]{2,1,0:T(8,128)(2,1)}, bf16[2,448,512]{2,1,0:T(8,128)(2,1)S(1)}, u32[]{:S(2)}, u32[]{:S(2)}) %collective-permute-start.2) | collective-permute-done | bytes 917536 | tf_op jit(solution)/shard_map/ppermute | solution.py:484
  50.4 3.2 collective-permute-start.5
  53.6 5.1 %collective-permute-start.6 = (bf16[2,256,1024]{2,1,0:T(8,128)(2,1)}, bf16[2,256,1024]{2,1,0:T(8,128)(2,1)S(1)}, u32[]{:S(2)}, u32[]{:S(2)}) collective-permute-start(bf16[2,256,1024]{2,1,0:T(8,128)(2,1)} %collective-permute-done.1), channel_id=1, source_target_pairs={{8,0},{9,1},{10,2},{11,3},{12,4},{13,5},{14,6},{15,7},{16,8},{17,9... | collective-permute-start | bytes 3145736 | tf_op jit(solution)/shard_map/ppermute | solution.py:484
  58.8 2.3 broadcast_select_fusion.refs_2_
  63.6 4.5 %slice.96 = f32[7,128,1,256]{3,2,1,0:T(1,128)} slice(f32[8,128,8,256]{3,2,1,0:T(8,128)} %param.19), slice={[1:8], [0:128], [0:1], [0:256]} | slice | bytes 1835008 | tf_op jit(solution)/shard_map/slice | solution.py:585
  70.0 2.2 copy.35
  73.1 26.2 %collective-permute-done.7.refs_19_ = bf16[2,448,512]{2,1,0:T(8,128)(2,1)} collective-permute-done((bf16[2,448,512]{2,1,0:T(8,128)(2,1)}, bf16[2,448,512]{2,1,0:T(8,128)(2,1)}, u32[]{:S(2)}, u32[]{:S(2)}) %collective-permute-start.7) | collective-permute-done | bytes 917536 | tf_op jit(solution)/shard_map/ppermute | solution.py:484
  102.2 5.5 %collective-permute-start.10 = (bf16[2,256,1024]{2,1,0:T(8,128)(2,1)}, bf16[2,256,1024]{2,1,0:T(8,128)(2,1)}, u32[]{:S(2)}, u32[]{:S(2)}) collective-permute-start(bf16[2,256,1024]{2,1,0:T(8,128)(2,1)} %get-tuple-element.122), channel_id=1, source_target_pairs={{8,0},{9,1},{10,2},{11,3},{12,4},{13,5},{14,6},{15,7},{16,24},{17,... | collective-permute-start | bytes 3145736 | tf_op jit(solution)/shard_map/ppermute | solution.py:484
  113.0 2.4 pad_maximum_fusion
  115.5 3.2 collective-permute-done.14.b2_ref
  118.7 30.5 %collective-permute-done.11.refs_17_ = bf16[2,448,512]{2,1,0:T(8,128)(2,1)S(1)} collective-permute-done((bf16[2,448,512]{2,1,0:T(8,128)(2,1)}, bf16[2,448,512]{2,1,0:T(8,128)(2,1)S(1)}, u32[]{:S(2)}, u32[]{:S(2)}) %collective-permute-start.11) | collective-permute-done | bytes 917536 | tf_op jit(solution)/shard_map/ppermute | solution.py:484
  151.0 2.4 select_select_fusion.refs_6_
  157.2 3.2 collective-permute-done.19
  160.5 3.1 collective-permute-start.20
  163.6 14.4 %collective-permute-done.20 = f32[320,256]{1,0:T(8,128)S(1)} collective-permute-done((f32[320,256]{1,0:T(8,128)S(1)}, f32[320,256]{1,0:T(8,128)S(1)}, u32[]{:S(2)}, u32[]{:S(2)}) %collective-permute-start.20) | collective-permute-done | bytes 327712 | tf_op jit(solution)/shard_map/ppermute | solution.py:484
  188.6 19.8 %gradient.1 = (f32[4,256,64]{2,1,0:T(8,128)}, f32[256,128]{1,0:T(8,128)}) custom-call(s32[4]{0:T(128)} %pad_add_fusion.spot_ref, bf16[2,256,1024]{2,1,0:T(8,128)(2,1)} %get-tuple-element.124.refs_0_, bf16[2,256,1024]{2,1,0:T(8,128)(2,1)} %collective-permute-done.3.refs_1_, bf16[2,256,1024]{2,1,0:T(8,128)(2,1)} %broadcast_select_fusion.refs_2_, ...), custom_call_target="tpu_custom_call" | custom-call | flops 15032385536 | bytes 24117248 | tf_op jit(solution)/shard_map/gradient/pallas_call | solution.py:547
  210.2 3.6 %collective-permute-start.28 = (f32[256,64]{1,0:T(8,128)S(1)}, f32[256,64]{1,0:T(8,128)S(1)}, u32[]{:S(2)}, u32[]{:S(2)}) collective-permute-start(f32[256,64]{1,0:T(8,128)S(1)} %get-tuple-element.127), channel_id=1, source_target_pairs={{0,16},{1,17},{2,18},{3,19},{4,20},{5,21},{6,22},{7,23},{8,24},{9,... | collective-permute-start | bytes 196616 | tf_op jit(solution)/shard_map/ppermute | solution.py:484
  214.9 7.0 %collective-permute-done.28 = f32[256,64]{1,0:T(8,128)S(1)} collective-permute-done((f32[256,64]{1,0:T(8,128)S(1)}, f32[256,64]{1,0:T(8,128)S(1)}, u32[]{:S(2)}, u32[]{:S(2)}) %collective-permute-start.28) | collective-permute-done | bytes 65568 | tf_op jit(solution)/shard_map/ppermute | solution.py:484
  221.9 3.8 %collective-permute-done.27 = f32[256,64]{1,0:T(8,128)S(1)} collective-permute-done((f32[256,64]{1,0:T(8,128)S(1)}, f32[256,64]{1,0:T(8,128)S(1)}, u32[]{:S(2)}, u32[]{:S(2)}) %collective-permute-start.27) | collective-permute-done | bytes 65568 | tf_op jit(solution)/shard_map/ppermute | solution.py:484
  231.0 3.7 %collective-permute-done.32 = f32[256,64]{1,0:T(8,128)S(1)} collective-permute-done((f32[256,64]{1,0:T(8,128)S(1)}, f32[256,64]{1,0:T(8,128)S(1)}, u32[]{:S(2)}, u32[]{:S(2)}) %collective-permute-start.32) | collective-permute-done | bytes 65568 | tf_op jit(solution)/shard_map/ppermute | solution.py:484
  237.1 3.8 %collective-permute-done.34 = f32[32,512]{1,0:T(8,128)S(1)} collective-permute-done((f32[32,512]{1,0:T(8,128)S(1)}, f32[32,512]{1,0:T(8,128)S(1)}, u32[]{:S(2)}, u32[]{:S(2)}) %collective-permute-start.34) | collective-permute-done | bytes 65568 | tf_op jit(solution)/shard_map/ppermute | solution.py:484
  242.4 3.1 collective-permute-done.35
  245.6 6.4 %collective-permute-done.36 = f32[64,512]{1,0:T(8,128)S(1)} collective-permute-done((f32[64,512]{1,0:T(8,128)S(1)}, f32[64,512]{1,0:T(8,128)S(1)}, u32[]{:S(2)}, u32[]{:S(2)}) %collective-permute-start.36) | collective-permute-done | bytes 131104 | tf_op jit(solution)/shard_map/ppermute | solution.py:484
  254.2 5.6 %collective-permute-done.33.d2_ref = f32[1024,256]{1,0:T(8,128)} collective-permute-done((f32[1024,256]{1,0:T(8,128)S(1)}, f32[1024,256]{1,0:T(8,128)}, u32[]{:S(2)}, u32[]{:S(2)}) %collective-permute-start.33) | collective-permute-done | bytes 1048608 | tf_op jit(solution)/shard_map/ppermute | solution.py:484
  262.0 3.1 collective-permute-done.40.far_ref
  266.5 74.9 %panel_factor.1 = (f32[1024,256]{1,0:T(8,128)}, f32[512,128]{1,0:T(8,128)}, f32[64,4]{1,0:T(8,128)}, f32[8,32,128]{2,1,0:T(8,128)}) custom-call(s32[2]{0:T(128)} %pad_add_fusion.1.spot_ref, f32[1024,256]{1,0:T(8,128)} %copy-done.4, f32[1024,256]{1,0:T(8,128)} %copy-done.5, f32[1024,256]{1,0:T(8,128)} %collective-permute-done.33.d2_ref, ...), custom_call_target="tpu_custom_call" | custom-call | tf_op jit(solution)/shard_map/panel_factor/pallas_call | solution.py:314
  342.8 11.0 %gram_update.1 = f32[8192,256]{1,0:T(8,128)} custom-call(f32[8192,256]{1,0:T(8,128)} %bitcast.60, f32[8,32,128]{2,1,0:T(8,128)} %get-tuple-element.107.own_ref, f32[256,256]{1,0:T(8,128)} %constant_dynamic-slice_fusion.col_ref, f32[8,128,256]{2,1,0:T(8,128)} %bitcast.67), custom_call_target="tpu_custom_call" | custom-call | tf_op jit(solution)/shard_map/gram_update/pallas_call | solution.py:358
  (152 shorter events, 50.4 us)
Async XLA Ops:
  3.4 45.8 %collective-permute-start = (bf16[2,256,1024]{2,1,0:T(8,128)(2,1)}, bf16[2,256,1024]{2,1,0:T(8,128)(2,1)S(1)}, u32[]{:S(2)}, u32[]{:S(2)}) collective-permute-start(bf16[2,256,1024]{2,1,0:T(8,128)(2,1)} %get-tuple-element.124.refs_0_), channel_id=1, source_target_pairs={{0,8},{1,9},{2,10},{3,11},{4,12},{5,13},{6,14},{7,15},{8,16},{9,17... | collective-permute-start | bytes 3145736 | tf_op jit(solution)/shard_map/ppermute | solution.py:484
  6.6 42.6 %collective-permute-start.1 = (bf16[2,256,1024]{2,1,0:T(8,128)(2,1)}, bf16[2,256,1024]{2,1,0:T(8,128)(2,1)}, u32[]{:S(2)}, u32[]{:S(2)}) collective-permute-start(bf16[2,256,1024]{2,1,0:T(8,128)(2,1)} %get-tuple-element.124.refs_0_), channel_id=1, source_target_pairs={{8,0},{9,1},{10,2},{11,3},{12,4},{13,5},{14,6},{15,7},{16,8},{17,9... | collective-permute-start | bytes 3145736 | tf_op jit(solution)/shard_map/ppermute | solution.py:484
  8.7 40.5 %collective-permute-start.3 = (bf16[2,256,1024]{2,1,0:T(8,128)(2,1)}, bf16[2,256,1024]{2,1,0:T(8,128)(2,1)}, u32[]{:S(2)}, u32[]{:S(2)}) collective-permute-start(bf16[2,256,1024]{2,1,0:T(8,128)(2,1)} %get-tuple-element.124.refs_0_), channel_id=1, source_target_pairs={{0,2},{1,3},{2,0},{3,1},{4,6},{5,7},{6,4},{7,5},{8,10},{9,11},{10,... | collective-permute-start | bytes 3145736 | tf_op jit(solution)/shard_map/ppermute | solution.py:484
  20.1 29.1 %collective-permute-start.2 = (bf16[2,448,512]{2,1,0:T(8,128)(2,1)}, bf16[2,448,512]{2,1,0:T(8,128)(2,1)S(1)}, u32[]{:S(2)}, u32[]{:S(2)}) collective-permute-start(bf16[2,448,512]{2,1,0:T(8,128)(2,1)} %get-tuple-element.118), channel_id=1, source_target_pairs={{0,8},{1,9},{2,10},{3,11},{4,12},{5,13},{6,14},{7,15},{8,16},{9,17... | collective-permute-start | bytes 2752520 | tf_op jit(solution)/shard_map/ppermute | solution.py:484
  21.3 27.9 %collective-permute-start.4 = (bf16[2,448,512]{2,1,0:T(8,128)(2,1)}, bf16[2,448,512]{2,1,0:T(8,128)(2,1)S(1)}, u32[]{:S(2)}, u32[]{:S(2)}) collective-permute-start(bf16[2,448,512]{2,1,0:T(8,128)(2,1)} %get-tuple-element.119.refs_13_), channel_id=1, source_target_pairs={{0,4},{1,5},{2,6},{3,7},{4,0},{5,1},{6,2},{7,3},{8,12},{9,13},{10,... | collective-permute-start | bytes 2752520 | tf_op jit(solution)/shard_map/ppermute | solution.py:484
  50.4 50.1 %collective-permute-start.5 = (bf16[2,256,1024]{2,1,0:T(8,128)(2,1)S(1)}, bf16[2,256,1024]{2,1,0:T(8,128)(2,1)S(1)}, u32[]{:S(2)}, u32[]{:S(2)}) collective-permute-start(bf16[2,256,1024]{2,1,0:T(8,128)(2,1)S(1)} %collective-permute-done), channel_id=1, source_target_pairs={{0,8},{1,9},{2,10},{3,11},{4,12},{5,13},{6,14},{7,15},{8,16},{9,17... | collective-permute-start | bytes 3145736 | tf_op jit(solution)/shard_map/ppermute | solution.py:484
  53.6 46.9 %collective-permute-start.6 = (bf16[2,256,1024]{2,1,0:T(8,128)(2,1)}, bf16[2,256,1024]{2,1,0:T(8,128)(2,1)S(1)}, u32[]{:S(2)}, u32[]{:S(2)}) collective-permute-start(bf16[2,256,1024]{2,1,0:T(8,128)(2,1)} %collective-permute-done.1), channel_id=1, source_target_pairs={{8,0},{9,1},{10,2},{11,3},{12,4},{13,5},{14,6},{15,7},{16,8},{17,9... | collective-permute-start | bytes 3145736 | tf_op jit(solution)/shard_map/ppermute | solution.py:484
  61.1 39.5 %collective-permute-start.8 = (bf16[2,256,1024]{2,1,0:T(8,128)(2,1)}, bf16[2,256,1024]{2,1,0:T(8,128)(2,1)}, u32[]{:S(2)}, u32[]{:S(2)}) collective-permute-start(bf16[2,256,1024]{2,1,0:T(8,128)(2,1)} %broadcast_select_fusion.refs_2_), channel_id=1, source_target_pairs={{0,2},{1,3},{2,0},{3,1},{4,6},{5,7},{6,4},{7,5},{8,10},{9,11},{10,... | collective-permute-start | bytes 3145736 | tf_op jit(solution)/shard_map/ppermute | solution.py:484
  62.4 37.0 %collective-permute-start.7 = (bf16[2,448,512]{2,1,0:T(8,128)(2,1)}, bf16[2,448,512]{2,1,0:T(8,128)(2,1)}, u32[]{:S(2)}, u32[]{:S(2)}) collective-permute-start(bf16[2,448,512]{2,1,0:T(8,128)(2,1)} %get-tuple-element.59), channel_id=1, source_target_pairs={{0,24},{1,25},{2,26},{3,27},{4,28},{5,29},{6,30},{7,31},{8,0},{9,1... | collective-permute-start | bytes 2752520 | tf_op jit(solution)/shard_map/ppermute | solution.py:484
  62.4 38.2 %collective-permute-start.9 = (bf16[2,448,512]{2,1,0:T(8,128)(2,1)}, bf16[2,448,512]{2,1,0:T(8,128)(2,1)}, u32[]{:S(2)}, u32[]{:S(2)}) collective-permute-start(bf16[2,448,512]{2,1,0:T(8,128)(2,1)} %copy-done.17), channel_id=1, source_target_pairs={{0,4},{1,5},{2,6},{3,7},{4,0},{5,1},{6,2},{7,3},{8,12},{9,13},{10,... | collective-permute-start | bytes 2752520 | tf_op jit(solution)/shard_map/ppermute | solution.py:484
  99.3 19.4 %collective-permute-start.14 = (f32[896,256]{1,0:T(8,128)}, f32[896,256]{1,0:T(8,128)}, u32[]{:S(2)}, u32[]{:S(2)}) collective-permute-start(f32[896,256]{1,0:T(8,128)} %bitcast.64), channel_id=1, source_target_pairs={{0,2},{1,3},{2,0},{3,1},{4,6},{5,7},{6,4},{7,5},{8,10},{9,11},{10,... | collective-permute-start | bytes 2752520 | tf_op jit(solution)/shard_map/ppermute | solution.py:484
  102.2 47.1 %collective-permute-start.10 = (bf16[2,256,1024]{2,1,0:T(8,128)(2,1)}, bf16[2,256,1024]{2,1,0:T(8,128)(2,1)}, u32[]{:S(2)}, u32[]{:S(2)}) collective-permute-start(bf16[2,256,1024]{2,1,0:T(8,128)(2,1)} %get-tuple-element.122), channel_id=1, source_target_pairs={{8,0},{9,1},{10,2},{11,3},{12,4},{13,5},{14,6},{15,7},{16,24},{17,... | collective-permute-start | bytes 3145736 | tf_op jit(solution)/shard_map/ppermute | solution.py:484
  107.7 41.6 %collective-permute-start.12 = (bf16[2,256,1024]{2,1,0:T(8,128)(2,1)}, bf16[2,256,1024]{2,1,0:T(8,128)(2,1)}, u32[]{:S(2)}, u32[]{:S(2)}) collective-permute-start(bf16[2,256,1024]{2,1,0:T(8,128)(2,1)} %get-tuple-element.121.refs_4_), channel_id=1, source_target_pairs={{0,2},{1,3},{2,0},{3,1},{4,6},{5,7},{6,4},{7,5},{8,10},{9,11},{10,... | collective-permute-start | bytes 3145736 | tf_op jit(solution)/shard_map/ppermute | solution.py:484
  109.5 39.7 %collective-permute-start.11 = (bf16[2,448,512]{2,1,0:T(8,128)(2,1)}, bf16[2,448,512]{2,1,0:T(8,128)(2,1)S(1)}, u32[]{:S(2)}, u32[]{:S(2)}) collective-permute-start(bf16[2,448,512]{2,1,0:T(8,128)(2,1)} %get-tuple-element.63), channel_id=1, source_target_pairs={{0,16},{1,17},{2,18},{3,19},{4,20},{5,21},{6,22},{7,23},{8,24},{9,... | collective-permute-start | bytes 2752520 | tf_op jit(solution)/shard_map/ppermute | solution.py:484
  109.5 39.7 %collective-permute-start.13 = (bf16[2,448,512]{2,1,0:T(8,128)(2,1)}, bf16[2,448,512]{2,1,0:T(8,128)(2,1)S(1)}, u32[]{:S(2)}, u32[]{:S(2)}) collective-permute-start(bf16[2,448,512]{2,1,0:T(8,128)(2,1)} %collective-permute-done.7.refs_19_), channel_id=1, source_target_pairs={{0,4},{1,5},{2,6},{3,7},{4,0},{5,1},{6,2},{7,3},{8,12},{9,13},{10,... | collective-permute-start | bytes 2752520 | tf_op jit(solution)/shard_map/ppermute | solution.py:484
  150.2 28.5 %collective-permute-start.17 = (bf16[4,2,256,1024]{3,2,1,0:T(8,128)(2,1)S(1)}, bf16[4,2,256,1024]{3,2,1,0:T(8,128)(2,1)S(1)}, u32[]{:S(2)}, u32[]{:S(2)}) collective-permute-start(bf16[4,2,256,1024]{3,2,1,0:T(8,128)(2,1)S(1)} %pad_maximum_fusion), channel_id=1, source_target_pairs={{0,1},{1,0},{2,3},{3,2},{4,5},{5,4},{6,7},{7,6},{8,9},{9,8},{10,11... | collective-permute-start | bytes 12582920 | tf_op jit(solution)/shard_map/ppermute | solution.py:484
  151.0 27.5 %collective-permute-start.18 = (bf16[2,256,1024]{2,1,0:T(8,128)(2,1)}, bf16[2,256,1024]{2,1,0:T(8,128)(2,1)S(1)}, u32[]{:S(2)}, u32[]{:S(2)}) collective-permute-start(bf16[2,256,1024]{2,1,0:T(8,128)(2,1)} %get-tuple-element.121.refs_4_), channel_id=1, source_target_pairs={{0,1},{1,0},{2,3},{3,2},{4,5},{5,4},{6,7},{7,6},{8,9},{9,8},{10,11... | collective-permute-start | bytes 3145736 | tf_op jit(solution)/shard_map/ppermute | solution.py:484
  153.4 25.3 %collective-permute-start.15 = (bf16[2,256,1024]{2,1,0:T(8,128)(2,1)}, bf16[2,256,1024]{2,1,0:T(8,128)(2,1)S(1)}, u32[]{:S(2)}, u32[]{:S(2)}) collective-permute-start(bf16[2,256,1024]{2,1,0:T(8,128)(2,1)} %select_select_fusion.refs_6_), channel_id=1, source_target_pairs={{0,2},{1,3},{2,0},{3,1},{4,6},{5,7},{6,4},{7,5},{8,10},{9,11},{10,... | collective-permute-start | bytes 3145736 | tf_op jit(solution)/shard_map/ppermute | solution.py:484
  154.6 24.0 %collective-permute-start.16 = (bf16[2,448,512]{2,1,0:T(8,128)(2,1)S(1)}, bf16[2,448,512]{2,1,0:T(8,128)(2,1)S(1)}, u32[]{:S(2)}, u32[]{:S(2)}) collective-permute-start(bf16[2,448,512]{2,1,0:T(8,128)(2,1)S(1)} %collective-permute-done.11.refs_17_), channel_id=1, source_target_pairs={{0,4},{1,5},{2,6},{3,7},{4,0},{5,1},{6,2},{7,3},{8,12},{9,13},{10,... | collective-permute-start | bytes 2752520 | tf_op jit(solution)/shard_map/ppermute | solution.py:484
  160.5 17.5 %collective-permute-start.20 = (f32[320,256]{1,0:T(8,128)S(1)}, f32[320,256]{1,0:T(8,128)S(1)}, u32[]{:S(2)}, u32[]{:S(2)}) collective-permute-start(f32[320,256]{1,0:T(8,128)S(1)} %pad_maximum_fusion.3), channel_id=1, source_target_pairs={{0,16},{1,17},{2,18},{3,19},{4,20},{5,21},{6,22},{7,23},{8,24},{9,... | collective-permute-start | bytes 983048 | tf_op jit(solution)/shard_map/ppermute | solution.py:484
  178.0 9.6 %collective-permute-start.22 = (bf16[2,256,1024]{2,1,0:T(8,128)(2,1)}, bf16[2,256,1024]{2,1,0:T(8,128)(2,1)}, u32[]{:S(2)}, u32[]{:S(2)}) collective-permute-start(bf16[2,256,1024]{2,1,0:T(8,128)(2,1)} %select_select_fusion.refs_6_), channel_id=1, source_target_pairs={{0,1},{1,0},{2,3},{3,2},{4,5},{5,4},{6,7},{7,6},{8,9},{9,8},{10,11... | collective-permute-start | bytes 3145736 | tf_op jit(solution)/shard_map/ppermute | solution.py:484
  178.6 9.0 %collective-permute-start.21 = (bf16[2,256,1024]{2,1,0:T(8,128)(2,1)}, bf16[2,256,1024]{2,1,0:T(8,128)(2,1)}, u32[]{:S(2)}, u32[]{:S(2)}) collective-permute-start(bf16[2,256,1024]{2,1,0:T(8,128)(2,1)} %collective-permute-done.12.refs_5_), channel_id=1, source_target_pairs={{0,1},{1,0},{2,3},{3,2},{4,5},{5,4},{6,7},{7,6},{8,9},{9,8},{10,11... | collective-permute-start | bytes 3145736 | tf_op jit(solution)/shard_map/ppermute | solution.py:484
  181.9 5.8 %collective-permute-start.23 = (bf16[2,256,1024]{2,1,0:T(8,128)(2,1)S(1)}, bf16[2,256,1024]{2,1,0:T(8,128)(2,1)}, u32[]{:S(2)}, u32[]{:S(2)}) collective-permute-start(bf16[2,256,1024]{2,1,0:T(8,128)(2,1)S(1)} %collective-permute-done.15.refs_7_), channel_id=1, source_target_pairs={{0,1},{1,0},{2,3},{3,2},{4,5},{5,4},{6,7},{7,6},{8,9},{9,8},{10,11... | collective-permute-start | bytes 3145736 | tf_op jit(solution)/shard_map/ppermute | solution.py:484
  187.6 20.8 %collective-permute-start.24 = (f32[640,256]{1,0:T(8,128)S(1)}, f32[640,256]{1,0:T(8,128)S(1)}, u32[]{:S(2)}, u32[]{:S(2)}) collective-permute-start(f32[640,256]{1,0:T(8,128)S(1)} %pad_maximum_fusion.2), channel_id=1, source_target_pairs={{0,4},{1,5},{2,6},{3,7},{4,0},{5,1},{6,2},{7,3},{8,12},{9,13},{10,... | collective-permute-start | bytes 1966088 | tf_op jit(solution)/shard_map/ppermute | solution.py:484
  188.1 20.4 %collective-permute-start.25 = (f32[896,256]{1,0:T(8,128)S(1)}, f32[896,256]{1,0:T(8,128)S(1)}, u32[]{:S(2)}, u32[]{:S(2)}) collective-permute-start(f32[896,256]{1,0:T(8,128)S(1)} %bitcast.66), channel_id=1, source_target_pairs={{0,1},{1,0},{2,3},{3,2},{4,5},{5,4},{6,7},{7,6},{8,9},{9,8},{10,11... | collective-permute-start | bytes 2752520 | tf_op jit(solution)/shard_map/ppermute | solution.py:484
  188.5 20.0 %collective-permute-start.26 = (f32[896,256]{1,0:T(8,128)}, f32[896,256]{1,0:T(8,128)S(1)}, u32[]{:S(2)}, u32[]{:S(2)}) collective-permute-start(f32[896,256]{1,0:T(8,128)} %collective-permute-done.14.b2_ref), channel_id=1, source_target_pairs={{0,1},{1,0},{2,3},{3,2},{4,5},{5,4},{6,7},{7,6},{8,9},{9,8},{10,11... | collective-permute-start | bytes 2752520 | tf_op jit(solution)/shard_map/ppermute | solution.py:484
  210.2 11.7 %collective-permute-start.28 = (f32[256,64]{1,0:T(8,128)S(1)}, f32[256,64]{1,0:T(8,128)S(1)}, u32[]{:S(2)}, u32[]{:S(2)}) collective-permute-start(f32[256,64]{1,0:T(8,128)S(1)} %get-tuple-element.127), channel_id=1, source_target_pairs={{0,16},{1,17},{2,18},{3,19},{4,20},{5,21},{6,22},{7,23},{8,24},{9,... | collective-permute-start | bytes 196616 | tf_op jit(solution)/shard_map/ppermute | solution.py:484
  213.8 11.9 %collective-permute-start.27 = (f32[256,64]{1,0:T(8,128)S(1)}, f32[256,64]{1,0:T(8,128)S(1)}, u32[]{:S(2)}, u32[]{:S(2)}) collective-permute-start(f32[256,64]{1,0:T(8,128)S(1)} %get-tuple-element.125), channel_id=1, source_target_pairs={{0,24},{1,25},{2,26},{3,27},{4,28},{5,29},{6,30},{7,31},{8,0},{9,1... | collective-permute-start | bytes 196616 | tf_op jit(solution)/shard_map/ppermute | solution.py:484
  227.9 6.8 %collective-permute-start.32 = (f32[256,64]{1,0:T(8,128)S(1)}, f32[256,64]{1,0:T(8,128)S(1)}, u32[]{:S(2)}, u32[]{:S(2)}) collective-permute-start(f32[256,64]{1,0:T(8,128)S(1)} %fusion.9), channel_id=1, source_target_pairs={{0,3},{1,2},{2,1},{3,0},{4,7},{5,6},{6,5},{7,4},{8,11},{9,10},{10,... | collective-permute-start | bytes 196616 | tf_op jit(solution)/shard_map/ppermute | solution.py:484
  234.8 25.0 %collective-permute-start.33 = (f32[1024,256]{1,0:T(8,128)S(1)}, f32[1024,256]{1,0:T(8,128)}, u32[]{:S(2)}, u32[]{:S(2)}) collective-permute-start(f32[1024,256]{1,0:T(8,128)S(1)} %slice_dynamic-update-slice_fusion.d0_ref), channel_id=1, source_target_pairs={{0,2},{1,3},{2,0},{3,1},{4,6},{5,7},{6,4},{7,5},{8,10},{9,11},{10,... | collective-permute-start | bytes 3145736 | tf_op jit(solution)/shard_map/ppermute | solution.py:484
  241.0 11.0 %collective-permute-start.36 = (f32[64,512]{1,0:T(8,128)S(1)}, f32[64,512]{1,0:T(8,128)S(1)}, u32[]{:S(2)}, u32[]{:S(2)}) collective-permute-start(f32[64,512]{1,0:T(8,128)S(1)} %pad_maximum_fusion.4), channel_id=1, source_target_pairs={{0,16},{1,17},{2,18},{3,19},{4,20},{5,21},{6,22},{7,23},{8,24},{9,... | collective-permute-start | bytes 393224 | tf_op jit(solution)/shard_map/ppermute | solution.py:484
  241.7 12.5 %collective-permute-start.37 = (f32[64,512]{1,0:T(8,128)S(1)}, f32[64,512]{1,0:T(8,128)S(1)}, u32[]{:S(2)}, u32[]{:S(2)}) collective-permute-start(f32[64,512]{1,0:T(8,128)S(1)} %pad_maximum_fusion.4), channel_id=1, source_target_pairs={{0,24},{1,25},{2,26},{3,27},{4,28},{5,29},{6,30},{7,31},{8,0},{9,1... | collective-permute-start | bytes 393224 | tf_op jit(solution)/shard_map/ppermute | solution.py:484
  (32 other events, 601.6 us)

commit v7 on v6

--- a/solution.py
+++ b/solution.py
@@ -241,6 +241,7 @@
     upper_ref,
     root_ref,
     feat_ref,
+    load_sem,
 ):
     total, width = work_ref.shape
     low, band = b0_ref.shape
@@ -250,15 +251,19 @@
     queries = query_ref.shape[0] // cycles
     top = width + low
     diag_refs, below_refs = (d0_ref, d1_ref, d2_ref, d3_ref), (b0_ref, b1_ref, b2_ref, b3_ref)
+    loads = []
     for i, (diag_ref, below_ref) in enumerate(zip(diag_refs, below_refs)):
         there = ((y + i // 2) % 2) * 2 + (core + i % 2) % 2
         lanes = pl.ds(pl.multiple_of(there * band, 128), band)
-        work_ref[width:top, lanes] = below_ref[...]
+        pairs = [(below_ref, work_ref.at[pl.ds(width, low), lanes])]
         for k in range(8):
-            at = band_of(row, k) * block
-            work_ref[pl.ds(pl.multiple_of(at, block), block), lanes] = diag_ref[
-                k * block : (k + 1) * block, :
-            ]
+            at = pl.multiple_of(band_of(row, k) * block, block)
+            source = diag_ref.at[pl.ds(k * block, block), :]
+            pairs.append((source, work_ref.at[pl.ds(at, block), lanes]))
+        for source, target in pairs:
+            loads.append(pltpu.make_async_copy(source, target, load_sem.at[len(loads)]))
+    for copy in loads:
+        copy.start()
     half = queries // 2
     for k in range(8):
         lanes = pl.ds(pl.multiple_of(band_of(row, k) * block, block), block)
@@ -272,6 +277,8 @@
     every = feat_ref.shape[1] // cycles
     first = [feat_ref[i, pl.ds(0, every, stride=cycles), :] for i in range(width // 128)]
     right = pack_right(jnp.concatenate(first, axis=1))
+    for copy in loads:
+        copy.wait()
     for i, here in enumerate(spans(0, width, block)):
         work_ref[here, :] = work_ref[here, :] + outer_sum(pack_left(first[i]), right) * share
     for a in range(cycles):
@@ -319,10 +326,14 @@
             jax.ShapeDtypeStruct((count, seqs), jnp.float32),
             jax.ShapeDtypeStruct((cycles, near.shape[0] // cycles, block), jnp.float32),
         ],
-        in_specs=[pl.BlockSpec(memory_space=pltpu.SMEM)] + [whole] * 12,
+        in_specs=[pl.BlockSpec(memory_space=pltpu.SMEM)] + [pl.BlockSpec(memory_space=pl.ANY)] * 8
+        + [whole] * 4,
         out_specs=[whole] * 4,
         scratch_shapes=factor_scratch(total, width)
-        + [pltpu.VMEM((width // 128, near.shape[0], 128), jnp.float32)],
+        + [
+            pltpu.VMEM((width // 128, near.shape[0], 128), jnp.float32),
+            pltpu.SemaphoreType.DMA((36,)),
+        ],
         compiler_params=pltpu.CompilerParams(vmem_limit_bytes=vmem_limit),
         name="panel_factor",
     )(spot, *diags, *belows, near, far, heads, queries)

time: 351 us -> 352 us (level)
  no operation moved by 1% of the time
where the time goes in v7:
time: 352 us; the launch traced here: 355 us
  waiting for transfers between devices  145 us (41%)
  Pallas kernels  106 us (30%)
  starting transfers between devices  48.9 us (14%)
  local copies, waits for them, and re-layouts  29.5 us (8%)
  other arithmetic  17.3 us (5%)
  between operations  6.84 us (2%)
    ppermute x41, waiting for transfers between devices, shift(): return lax.ppermute(value, ('rows', 'cols'), pairs)  145 us
    pallas_call x1, Pallas kernels, panel(): pl.pallas_call(functools.partial(panel_kernel, share, seqs), out_shape=[j...  75.5 us
    ppermute x41, starting transfers between devices, shift(): return lax.ppermute(value, ('rows', 'cols'), pairs)  48.9 us
    pallas_call x1, Pallas kernels, gradient(): pl.pallas_call(gradient_kernel, out_shape=[jax.ShapeDtypeStruct((4, heigh...  19.8 us
    unnamed x68, local copies, waits for them, and re-layouts  18.1 us
    pallas_call x1, Pallas kernels, gram_update(): pl.pallas_call(functools.partial(gram_kernel, share), out_shape=jax.Shape...  11 us
  transfers between devices with their start and end apart: 41, of which 18 were waited for; matrix products, arithmetic and copies ran while one was open for 10% of the time, Pallas kernels for 6%

profile of v7, /device:TPU:9, one launch (start us, length us, event | category | flops | bytes accessed | tf_op | source)
XLA Modules:
  0.0 354.7 jit_solution(12051667959302047227)
XLA Ops:
  0.6 2.7 fusion.13
  3.4 3.2 collective-permute-start
  10.0 2.8 copy.23
  12.9 3.8 %copy.24 = bf16[512,1792]{0,1:T(8,128)(2,1)} copy(bf16[512,1792]{1,0:T(8,128)(2,1)} %param.14) | data formatting | bytes 3670016 | tf_op args[3]
  16.7 3.4 fusion.1
  22.5 26.6 %collective-permute-done.2.refs_15_ = bf16[2,448,512]{2,1,0:T(8,128)(2,1)S(1)} collective-permute-done((bf16[2,448,512]{2,1,0:T(8,128)(2,1)}, bf16[2,448,512]{2,1,0:T(8,128)(2,1)S(1)}, u32[]{:S(2)}, u32[]{:S(2)}) %collective-permute-start.2) | collective-permute-done | bytes 917536 | tf_op jit(solution)/shard_map/ppermute | solution.py:495
  50.4 3.2 collective-permute-start.5
  53.6 5.1 %collective-permute-start.6 = (bf16[2,256,1024]{2,1,0:T(8,128)(2,1)}, bf16[2,256,1024]{2,1,0:T(8,128)(2,1)S(1)}, u32[]{:S(2)}, u32[]{:S(2)}) collective-permute-start(bf16[2,256,1024]{2,1,0:T(8,128)(2,1)} %collective-permute-done.1), channel_id=1, source_target_pairs={{8,0},{9,1},{10,2},{11,3},{12,4},{13,5},{14,6},{15,7},{16,8},{17,9... | collective-permute-start | bytes 3145736 | tf_op jit(solution)/shard_map/ppermute | solution.py:495
  58.8 2.3 broadcast_select_fusion.refs_2_
  63.6 4.5 %slice.96 = f32[7,128,1,256]{3,2,1,0:T(1,128)} slice(f32[8,128,8,256]{3,2,1,0:T(8,128)} %param.19), slice={[1:8], [0:128], [0:1], [0:256]} | slice | bytes 1835008 | tf_op jit(solution)/shard_map/slice | solution.py:596
  70.0 2.2 copy.35
  73.1 26.2 %collective-permute-done.7.refs_19_ = bf16[2,448,512]{2,1,0:T(8,128)(2,1)} collective-permute-done((bf16[2,448,512]{2,1,0:T(8,128)(2,1)}, bf16[2,448,512]{2,1,0:T(8,128)(2,1)}, u32[]{:S(2)}, u32[]{:S(2)}) %collective-permute-start.7) | collective-permute-done | bytes 917536 | tf_op jit(solution)/shard_map/ppermute | solution.py:495
  102.2 5.5 %collective-permute-start.10 = (bf16[2,256,1024]{2,1,0:T(8,128)(2,1)}, bf16[2,256,1024]{2,1,0:T(8,128)(2,1)}, u32[]{:S(2)}, u32[]{:S(2)}) collective-permute-start(bf16[2,256,1024]{2,1,0:T(8,128)(2,1)} %get-tuple-element.122), channel_id=1, source_target_pairs={{8,0},{9,1},{10,2},{11,3},{12,4},{13,5},{14,6},{15,7},{16,24},{17,... | collective-permute-start | bytes 3145736 | tf_op jit(solution)/shard_map/ppermute | solution.py:495
  113.0 2.4 pad_maximum_fusion
  115.5 3.2 collective-permute-done.14.b2_ref
  118.7 30.5 %collective-permute-done.11.refs_17_ = bf16[2,448,512]{2,1,0:T(8,128)(2,1)S(1)} collective-permute-done((bf16[2,448,512]{2,1,0:T(8,128)(2,1)}, bf16[2,448,512]{2,1,0:T(8,128)(2,1)S(1)}, u32[]{:S(2)}, u32[]{:S(2)}) %collective-permute-start.11) | collective-permute-done | bytes 917536 | tf_op jit(solution)/shard_map/ppermute | solution.py:495
  151.0 2.4 select_select_fusion.refs_6_
  157.2 3.2 collective-permute-done.19
  160.5 3.1 collective-permute-start.20
  163.6 14.4 %collective-permute-done.20 = f32[320,256]{1,0:T(8,128)S(1)} collective-permute-done((f32[320,256]{1,0:T(8,128)S(1)}, f32[320,256]{1,0:T(8,128)S(1)}, u32[]{:S(2)}, u32[]{:S(2)}) %collective-permute-start.20) | collective-permute-done | bytes 327712 | tf_op jit(solution)/shard_map/ppermute | solution.py:495
  188.6 19.8 %gradient.1 = (f32[4,256,64]{2,1,0:T(8,128)}, f32[256,128]{1,0:T(8,128)}) custom-call(s32[4]{0:T(128)} %pad_add_fusion.spot_ref, bf16[2,256,1024]{2,1,0:T(8,128)(2,1)} %get-tuple-element.124.refs_0_, bf16[2,256,1024]{2,1,0:T(8,128)(2,1)} %collective-permute-done.3.refs_1_, bf16[2,256,1024]{2,1,0:T(8,128)(2,1)} %broadcast_select_fusion.refs_2_, ...), custom_call_target="tpu_custom_call" | custom-call | flops 15032385536 | bytes 24117248 | tf_op jit(solution)/shard_map/gradient/pallas_call | solution.py:558
  210.2 3.6 %collective-permute-start.28 = (f32[256,64]{1,0:T(8,128)S(1)}, f32[256,64]{1,0:T(8,128)S(1)}, u32[]{:S(2)}, u32[]{:S(2)}) collective-permute-start(f32[256,64]{1,0:T(8,128)S(1)} %get-tuple-element.127), channel_id=1, source_target_pairs={{0,16},{1,17},{2,18},{3,19},{4,20},{5,21},{6,22},{7,23},{8,24},{9,... | collective-permute-start | bytes 196616 | tf_op jit(solution)/shard_map/ppermute | solution.py:495
  214.9 7.0 %collective-permute-done.28 = f32[256,64]{1,0:T(8,128)S(1)} collective-permute-done((f32[256,64]{1,0:T(8,128)S(1)}, f32[256,64]{1,0:T(8,128)S(1)}, u32[]{:S(2)}, u32[]{:S(2)}) %collective-permute-start.28) | collective-permute-done | bytes 65568 | tf_op jit(solution)/shard_map/ppermute | solution.py:495
  221.9 3.8 %collective-permute-done.27 = f32[256,64]{1,0:T(8,128)S(1)} collective-permute-done((f32[256,64]{1,0:T(8,128)S(1)}, f32[256,64]{1,0:T(8,128)S(1)}, u32[]{:S(2)}, u32[]{:S(2)}) %collective-permute-start.27) | collective-permute-done | bytes 65568 | tf_op jit(solution)/shard_map/ppermute | solution.py:495
  231.0 3.7 %collective-permute-done.32 = f32[256,64]{1,0:T(8,128)S(1)} collective-permute-done((f32[256,64]{1,0:T(8,128)S(1)}, f32[256,64]{1,0:T(8,128)S(1)}, u32[]{:S(2)}, u32[]{:S(2)}) %collective-permute-start.32) | collective-permute-done | bytes 65568 | tf_op jit(solution)/shard_map/ppermute | solution.py:495
  237.1 3.8 %collective-permute-done.34 = f32[32,512]{1,0:T(8,128)S(1)} collective-permute-done((f32[32,512]{1,0:T(8,128)S(1)}, f32[32,512]{1,0:T(8,128)S(1)}, u32[]{:S(2)}, u32[]{:S(2)}) %collective-permute-start.34) | collective-permute-done | bytes 65568 | tf_op jit(solution)/shard_map/ppermute | solution.py:495
  242.4 3.1 collective-permute-done.35
  245.6 6.4 %collective-permute-done.36 = f32[64,512]{1,0:T(8,128)S(1)} collective-permute-done((f32[64,512]{1,0:T(8,128)S(1)}, f32[64,512]{1,0:T(8,128)S(1)}, u32[]{:S(2)}, u32[]{:S(2)}) %collective-permute-start.36) | collective-permute-done | bytes 131104 | tf_op jit(solution)/shard_map/ppermute | solution.py:495
  254.2 5.6 %collective-permute-done.33.d2_ref = f32[1024,256]{1,0:T(8,128)} collective-permute-done((f32[1024,256]{1,0:T(8,128)S(1)}, f32[1024,256]{1,0:T(8,128)}, u32[]{:S(2)}, u32[]{:S(2)}) %collective-permute-start.33) | collective-permute-done | bytes 1048608 | tf_op jit(solution)/shard_map/ppermute | solution.py:495
  262.0 3.1 collective-permute-done.40.far_ref
  266.5 75.5 %panel_factor.1 = (f32[1024,256]{1,0:T(8,128)}, f32[512,128]{1,0:T(8,128)}, f32[64,4]{1,0:T(8,128)}, f32[8,32,128]{2,1,0:T(8,128)}) custom-call(s32[2]{0:T(128)} %pad_add_fusion.1.spot_ref, f32[1024,256]{1,0:T(8,128)} %copy-done.4, f32[1024,256]{1,0:T(8,128)} %copy-done.5, f32[1024,256]{1,0:T(8,128)} %collective-permute-done.33.d2_ref, ...), custom_call_target="tpu_custom_call" | custom-call | tf_op jit(solution)/shard_map/panel_factor/pallas_call | solution.py:321
  343.4 11.0 %gram_update.1 = f32[8192,256]{1,0:T(8,128)} custom-call(f32[8192,256]{1,0:T(8,128)} %bitcast.60, f32[8,32,128]{2,1,0:T(8,128)} %get-tuple-element.107.own_ref, f32[256,256]{1,0:T(8,128)} %constant_dynamic-slice_fusion.col_ref, f32[8,128,256]{2,1,0:T(8,128)} %bitcast.67), custom_call_target="tpu_custom_call" | custom-call | tf_op jit(solution)/shard_map/gram_update/pallas_call | solution.py:369
  (152 shorter events, 50.4 us)
Async XLA Ops:
  3.4 45.8 %collective-permute-start = (bf16[2,256,1024]{2,1,0:T(8,128)(2,1)}, bf16[2,256,1024]{2,1,0:T(8,128)(2,1)S(1)}, u32[]{:S(2)}, u32[]{:S(2)}) collective-permute-start(bf16[2,256,1024]{2,1,0:T(8,128)(2,1)} %get-tuple-element.124.refs_0_), channel_id=1, source_target_pairs={{0,8},{1,9},{2,10},{3,11},{4,12},{5,13},{6,14},{7,15},{8,16},{9,17... | collective-permute-start | bytes 3145736 | tf_op jit(solution)/shard_map/ppermute | solution.py:495
  6.6 42.6 %collective-permute-start.1 = (bf16[2,256,1024]{2,1,0:T(8,128)(2,1)}, bf16[2,256,1024]{2,1,0:T(8,128)(2,1)}, u32[]{:S(2)}, u32[]{:S(2)}) collective-permute-start(bf16[2,256,1024]{2,1,0:T(8,128)(2,1)} %get-tuple-element.124.refs_0_), channel_id=1, source_target_pairs={{8,0},{9,1},{10,2},{11,3},{12,4},{13,5},{14,6},{15,7},{16,8},{17,9... | collective-permute-start | bytes 3145736 | tf_op jit(solution)/shard_map/ppermute | solution.py:495
  8.7 40.5 %collective-permute-start.3 = (bf16[2,256,1024]{2,1,0:T(8,128)(2,1)}, bf16[2,256,1024]{2,1,0:T(8,128)(2,1)}, u32[]{:S(2)}, u32[]{:S(2)}) collective-permute-start(bf16[2,256,1024]{2,1,0:T(8,128)(2,1)} %get-tuple-element.124.refs_0_), channel_id=1, source_target_pairs={{0,2},{1,3},{2,0},{3,1},{4,6},{5,7},{6,4},{7,5},{8,10},{9,11},{10,... | collective-permute-start | bytes 3145736 | tf_op jit(solution)/shard_map/ppermute | solution.py:495
  20.1 29.1 %collective-permute-start.2 = (bf16[2,448,512]{2,1,0:T(8,128)(2,1)}, bf16[2,448,512]{2,1,0:T(8,128)(2,1)S(1)}, u32[]{:S(2)}, u32[]{:S(2)}) collective-permute-start(bf16[2,448,512]{2,1,0:T(8,128)(2,1)} %get-tuple-element.118), channel_id=1, source_target_pairs={{0,8},{1,9},{2,10},{3,11},{4,12},{5,13},{6,14},{7,15},{8,16},{9,17... | collective-permute-start | bytes 2752520 | tf_op jit(solution)/shard_map/ppermute | solution.py:495
  21.3 27.9 %collective-permute-start.4 = (bf16[2,448,512]{2,1,0:T(8,128)(2,1)}, bf16[2,448,512]{2,1,0:T(8,128)(2,1)S(1)}, u32[]{:S(2)}, u32[]{:S(2)}) collective-permute-start(bf16[2,448,512]{2,1,0:T(8,128)(2,1)} %get-tuple-element.119.refs_13_), channel_id=1, source_target_pairs={{0,4},{1,5},{2,6},{3,7},{4,0},{5,1},{6,2},{7,3},{8,12},{9,13},{10,... | collective-permute-start | bytes 2752520 | tf_op jit(solution)/shard_map/ppermute | solution.py:495
  50.4 50.1 %collective-permute-start.5 = (bf16[2,256,1024]{2,1,0:T(8,128)(2,1)S(1)}, bf16[2,256,1024]{2,1,0:T(8,128)(2,1)S(1)}, u32[]{:S(2)}, u32[]{:S(2)}) collective-permute-start(bf16[2,256,1024]{2,1,0:T(8,128)(2,1)S(1)} %collective-permute-done), channel_id=1, source_target_pairs={{0,8},{1,9},{2,10},{3,11},{4,12},{5,13},{6,14},{7,15},{8,16},{9,17... | collective-permute-start | bytes 3145736 | tf_op jit(solution)/shard_map/ppermute | solution.py:495
  53.6 46.9 %collective-permute-start.6 = (bf16[2,256,1024]{2,1,0:T(8,128)(2,1)}, bf16[2,256,1024]{2,1,0:T(8,128)(2,1)S(1)}, u32[]{:S(2)}, u32[]{:S(2)}) collective-permute-start(bf16[2,256,1024]{2,1,0:T(8,128)(2,1)} %collective-permute-done.1), channel_id=1, source_target_pairs={{8,0},{9,1},{10,2},{11,3},{12,4},{13,5},{14,6},{15,7},{16,8},{17,9... | collective-permute-start | bytes 3145736 | tf_op jit(solution)/shard_map/ppermute | solution.py:495
  61.1 39.5 %collective-permute-start.8 = (bf16[2,256,1024]{2,1,0:T(8,128)(2,1)}, bf16[2,256,1024]{2,1,0:T(8,128)(2,1)}, u32[]{:S(2)}, u32[]{:S(2)}) collective-permute-start(bf16[2,256,1024]{2,1,0:T(8,128)(2,1)} %broadcast_select_fusion.refs_2_), channel_id=1, source_target_pairs={{0,2},{1,3},{2,0},{3,1},{4,6},{5,7},{6,4},{7,5},{8,10},{9,11},{10,... | collective-permute-start | bytes 3145736 | tf_op jit(solution)/shard_map/ppermute | solution.py:495
  62.4 37.0 %collective-permute-start.7 = (bf16[2,448,512]{2,1,0:T(8,128)(2,1)}, bf16[2,448,512]{2,1,0:T(8,128)(2,1)}, u32[]{:S(2)}, u32[]{:S(2)}) collective-permute-start(bf16[2,448,512]{2,1,0:T(8,128)(2,1)} %get-tuple-element.59), channel_id=1, source_target_pairs={{0,24},{1,25},{2,26},{3,27},{4,28},{5,29},{6,30},{7,31},{8,0},{9,1... | collective-permute-start | bytes 2752520 | tf_op jit(solution)/shard_map/ppermute | solution.py:495
  62.4 38.2 %collective-permute-start.9 = (bf16[2,448,512]{2,1,0:T(8,128)(2,1)}, bf16[2,448,512]{2,1,0:T(8,128)(2,1)}, u32[]{:S(2)}, u32[]{:S(2)}) collective-permute-start(bf16[2,448,512]{2,1,0:T(8,128)(2,1)} %copy-done.17), channel_id=1, source_target_pairs={{0,4},{1,5},{2,6},{3,7},{4,0},{5,1},{6,2},{7,3},{8,12},{9,13},{10,... | collective-permute-start | bytes 2752520 | tf_op jit(solution)/shard_map/ppermute | solution.py:495
  99.3 19.4 %collective-permute-start.14 = (f32[896,256]{1,0:T(8,128)}, f32[896,256]{1,0:T(8,128)}, u32[]{:S(2)}, u32[]{:S(2)}) collective-permute-start(f32[896,256]{1,0:T(8,128)} %bitcast.64), channel_id=1, source_target_pairs={{0,2},{1,3},{2,0},{3,1},{4,6},{5,7},{6,4},{7,5},{8,10},{9,11},{10,... | collective-permute-start | bytes 2752520 | tf_op jit(solution)/shard_map/ppermute | solution.py:495
  102.2 47.1 %collective-permute-start.10 = (bf16[2,256,1024]{2,1,0:T(8,128)(2,1)}, bf16[2,256,1024]{2,1,0:T(8,128)(2,1)}, u32[]{:S(2)}, u32[]{:S(2)}) collective-permute-start(bf16[2,256,1024]{2,1,0:T(8,128)(2,1)} %get-tuple-element.122), channel_id=1, source_target_pairs={{8,0},{9,1},{10,2},{11,3},{12,4},{13,5},{14,6},{15,7},{16,24},{17,... | collective-permute-start | bytes 3145736 | tf_op jit(solution)/shard_map/ppermute | solution.py:495
  107.7 41.6 %collective-permute-start.12 = (bf16[2,256,1024]{2,1,0:T(8,128)(2,1)}, bf16[2,256,1024]{2,1,0:T(8,128)(2,1)}, u32[]{:S(2)}, u32[]{:S(2)}) collective-permute-start(bf16[2,256,1024]{2,1,0:T(8,128)(2,1)} %get-tuple-element.121.refs_4_), channel_id=1, source_target_pairs={{0,2},{1,3},{2,0},{3,1},{4,6},{5,7},{6,4},{7,5},{8,10},{9,11},{10,... | collective-permute-start | bytes 3145736 | tf_op jit(solution)/shard_map/ppermute | solution.py:495
  109.5 39.7 %collective-permute-start.11 = (bf16[2,448,512]{2,1,0:T(8,128)(2,1)}, bf16[2,448,512]{2,1,0:T(8,128)(2,1)S(1)}, u32[]{:S(2)}, u32[]{:S(2)}) collective-permute-start(bf16[2,448,512]{2,1,0:T(8,128)(2,1)} %get-tuple-element.63), channel_id=1, source_target_pairs={{0,16},{1,17},{2,18},{3,19},{4,20},{5,21},{6,22},{7,23},{8,24},{9,... | collective-permute-start | bytes 2752520 | tf_op jit(solution)/shard_map/ppermute | solution.py:495
  109.5 39.7 %collective-permute-start.13 = (bf16[2,448,512]{2,1,0:T(8,128)(2,1)}, bf16[2,448,512]{2,1,0:T(8,128)(2,1)S(1)}, u32[]{:S(2)}, u32[]{:S(2)}) collective-permute-start(bf16[2,448,512]{2,1,0:T(8,128)(2,1)} %collective-permute-done.7.refs_19_), channel_id=1, source_target_pairs={{0,4},{1,5},{2,6},{3,7},{4,0},{5,1},{6,2},{7,3},{8,12},{9,13},{10,... | collective-permute-start | bytes 2752520 | tf_op jit(solution)/shard_map/ppermute | solution.py:495
  150.2 28.5 %collective-permute-start.17 = (bf16[4,2,256,1024]{3,2,1,0:T(8,128)(2,1)S(1)}, bf16[4,2,256,1024]{3,2,1,0:T(8,128)(2,1)S(1)}, u32[]{:S(2)}, u32[]{:S(2)}) collective-permute-start(bf16[4,2,256,1024]{3,2,1,0:T(8,128)(2,1)S(1)} %pad_maximum_fusion), channel_id=1, source_target_pairs={{0,1},{1,0},{2,3},{3,2},{4,5},{5,4},{6,7},{7,6},{8,9},{9,8},{10,11... | collective-permute-start | bytes 12582920 | tf_op jit(solution)/shard_map/ppermute | solution.py:495
  151.0 27.5 %collective-permute-start.18 = (bf16[2,256,1024]{2,1,0:T(8,128)(2,1)}, bf16[2,256,1024]{2,1,0:T(8,128)(2,1)S(1)}, u32[]{:S(2)}, u32[]{:S(2)}) collective-permute-start(bf16[2,256,1024]{2,1,0:T(8,128)(2,1)} %get-tuple-element.121.refs_4_), channel_id=1, source_target_pairs={{0,1},{1,0},{2,3},{3,2},{4,5},{5,4},{6,7},{7,6},{8,9},{9,8},{10,11... | collective-permute-start | bytes 3145736 | tf_op jit(solution)/shard_map/ppermute | solution.py:495
  153.4 25.3 %collective-permute-start.15 = (bf16[2,256,1024]{2,1,0:T(8,128)(2,1)}, bf16[2,256,1024]{2,1,0:T(8,128)(2,1)S(1)}, u32[]{:S(2)}, u32[]{:S(2)}) collective-permute-start(bf16[2,256,1024]{2,1,0:T(8,128)(2,1)} %select_select_fusion.refs_6_), channel_id=1, source_target_pairs={{0,2},{1,3},{2,0},{3,1},{4,6},{5,7},{6,4},{7,5},{8,10},{9,11},{10,... | collective-permute-start | bytes 3145736 | tf_op jit(solution)/shard_map/ppermute | solution.py:495
  154.6 24.0 %collective-permute-start.16 = (bf16[2,448,512]{2,1,0:T(8,128)(2,1)S(1)}, bf16[2,448,512]{2,1,0:T(8,128)(2,1)S(1)}, u32[]{:S(2)}, u32[]{:S(2)}) collective-permute-start(bf16[2,448,512]{2,1,0:T(8,128)(2,1)S(1)} %collective-permute-done.11.refs_17_), channel_id=1, source_target_pairs={{0,4},{1,5},{2,6},{3,7},{4,0},{5,1},{6,2},{7,3},{8,12},{9,13},{10,... | collective-permute-start | bytes 2752520 | tf_op jit(solution)/shard_map/ppermute | solution.py:495
  160.5 17.5 %collective-permute-start.20 = (f32[320,256]{1,0:T(8,128)S(1)}, f32[320,256]{1,0:T(8,128)S(1)}, u32[]{:S(2)}, u32[]{:S(2)}) collective-permute-start(f32[320,256]{1,0:T(8,128)S(1)} %pad_maximum_fusion.3), channel_id=1, source_target_pairs={{0,16},{1,17},{2,18},{3,19},{4,20},{5,21},{6,22},{7,23},{8,24},{9,... | collective-permute-start | bytes 983048 | tf_op jit(solution)/shard_map/ppermute | solution.py:495
  178.0 9.6 %collective-permute-start.22 = (bf16[2,256,1024]{2,1,0:T(8,128)(2,1)}, bf16[2,256,1024]{2,1,0:T(8,128)(2,1)}, u32[]{:S(2)}, u32[]{:S(2)}) collective-permute-start(bf16[2,256,1024]{2,1,0:T(8,128)(2,1)} %select_select_fusion.refs_6_), channel_id=1, source_target_pairs={{0,1},{1,0},{2,3},{3,2},{4,5},{5,4},{6,7},{7,6},{8,9},{9,8},{10,11... | collective-permute-start | bytes 3145736 | tf_op jit(solution)/shard_map/ppermute | solution.py:495
  178.6 9.0 %collective-permute-start.21 = (bf16[2,256,1024]{2,1,0:T(8,128)(2,1)}, bf16[2,256,1024]{2,1,0:T(8,128)(2,1)}, u32[]{:S(2)}, u32[]{:S(2)}) collective-permute-start(bf16[2,256,1024]{2,1,0:T(8,128)(2,1)} %collective-permute-done.12.refs_5_), channel_id=1, source_target_pairs={{0,1},{1,0},{2,3},{3,2},{4,5},{5,4},{6,7},{7,6},{8,9},{9,8},{10,11... | collective-permute-start | bytes 3145736 | tf_op jit(solution)/shard_map/ppermute | solution.py:495
  181.9 5.8 %collective-permute-start.23 = (bf16[2,256,1024]{2,1,0:T(8,128)(2,1)S(1)}, bf16[2,256,1024]{2,1,0:T(8,128)(2,1)}, u32[]{:S(2)}, u32[]{:S(2)}) collective-permute-start(bf16[2,256,1024]{2,1,0:T(8,128)(2,1)S(1)} %collective-permute-done.15.refs_7_), channel_id=1, source_target_pairs={{0,1},{1,0},{2,3},{3,2},{4,5},{5,4},{6,7},{7,6},{8,9},{9,8},{10,11... | collective-permute-start | bytes 3145736 | tf_op jit(solution)/shard_map/ppermute | solution.py:495
  187.6 20.8 %collective-permute-start.24 = (f32[640,256]{1,0:T(8,128)S(1)}, f32[640,256]{1,0:T(8,128)S(1)}, u32[]{:S(2)}, u32[]{:S(2)}) collective-permute-start(f32[640,256]{1,0:T(8,128)S(1)} %pad_maximum_fusion.2), channel_id=1, source_target_pairs={{0,4},{1,5},{2,6},{3,7},{4,0},{5,1},{6,2},{7,3},{8,12},{9,13},{10,... | collective-permute-start | bytes 1966088 | tf_op jit(solution)/shard_map/ppermute | solution.py:495
  188.1 20.4 %collective-permute-start.25 = (f32[896,256]{1,0:T(8,128)S(1)}, f32[896,256]{1,0:T(8,128)S(1)}, u32[]{:S(2)}, u32[]{:S(2)}) collective-permute-start(f32[896,256]{1,0:T(8,128)S(1)} %bitcast.66), channel_id=1, source_target_pairs={{0,1},{1,0},{2,3},{3,2},{4,5},{5,4},{6,7},{7,6},{8,9},{9,8},{10,11... | collective-permute-start | bytes 2752520 | tf_op jit(solution)/shard_map/ppermute | solution.py:495
  188.5 20.0 %collective-permute-start.26 = (f32[896,256]{1,0:T(8,128)}, f32[896,256]{1,0:T(8,128)S(1)}, u32[]{:S(2)}, u32[]{:S(2)}) collective-permute-start(f32[896,256]{1,0:T(8,128)} %collective-permute-done.14.b2_ref), channel_id=1, source_target_pairs={{0,1},{1,0},{2,3},{3,2},{4,5},{5,4},{6,7},{7,6},{8,9},{9,8},{10,11... | collective-permute-start | bytes 2752520 | tf_op jit(solution)/shard_map/ppermute | solution.py:495
  210.2 11.7 %collective-permute-start.28 = (f32[256,64]{1,0:T(8,128)S(1)}, f32[256,64]{1,0:T(8,128)S(1)}, u32[]{:S(2)}, u32[]{:S(2)}) collective-permute-start(f32[256,64]{1,0:T(8,128)S(1)} %get-tuple-element.127), channel_id=1, source_target_pairs={{0,16},{1,17},{2,18},{3,19},{4,20},{5,21},{6,22},{7,23},{8,24},{9,... | collective-permute-start | bytes 196616 | tf_op jit(solution)/shard_map/ppermute | solution.py:495
  213.8 11.9 %collective-permute-start.27 = (f32[256,64]{1,0:T(8,128)S(1)}, f32[256,64]{1,0:T(8,128)S(1)}, u32[]{:S(2)}, u32[]{:S(2)}) collective-permute-start(f32[256,64]{1,0:T(8,128)S(1)} %get-tuple-element.125), channel_id=1, source_target_pairs={{0,24},{1,25},{2,26},{3,27},{4,28},{5,29},{6,30},{7,31},{8,0},{9,1... | collective-permute-start | bytes 196616 | tf_op jit(solution)/shard_map/ppermute | solution.py:495
  227.9 6.8 %collective-permute-start.32 = (f32[256,64]{1,0:T(8,128)S(1)}, f32[256,64]{1,0:T(8,128)S(1)}, u32[]{:S(2)}, u32[]{:S(2)}) collective-permute-start(f32[256,64]{1,0:T(8,128)S(1)} %fusion.9), channel_id=1, source_target_pairs={{0,3},{1,2},{2,1},{3,0},{4,7},{5,6},{6,5},{7,4},{8,11},{9,10},{10,... | collective-permute-start | bytes 196616 | tf_op jit(solution)/shard_map/ppermute | solution.py:495
  234.8 25.0 %collective-permute-start.33 = (f32[1024,256]{1,0:T(8,128)S(1)}, f32[1024,256]{1,0:T(8,128)}, u32[]{:S(2)}, u32[]{:S(2)}) collective-permute-start(f32[1024,256]{1,0:T(8,128)S(1)} %slice_dynamic-update-slice_fusion.d0_ref), channel_id=1, source_target_pairs={{0,2},{1,3},{2,0},{3,1},{4,6},{5,7},{6,4},{7,5},{8,10},{9,11},{10,... | collective-permute-start | bytes 3145736 | tf_op jit(solution)/shard_map/ppermute | solution.py:495
  241.0 11.0 %collective-permute-start.36 = (f32[64,512]{1,0:T(8,128)S(1)}, f32[64,512]{1,0:T(8,128)S(1)}, u32[]{:S(2)}, u32[]{:S(2)}) collective-permute-start(f32[64,512]{1,0:T(8,128)S(1)} %pad_maximum_fusion.4), channel_id=1, source_target_pairs={{0,16},{1,17},{2,18},{3,19},{4,20},{5,21},{6,22},{7,23},{8,24},{9,... | collective-permute-start | bytes 393224 | tf_op jit(solution)/shard_map/ppermute | solution.py:495
  241.7 12.5 %collective-permute-start.37 = (f32[64,512]{1,0:T(8,128)S(1)}, f32[64,512]{1,0:T(8,128)S(1)}, u32[]{:S(2)}, u32[]{:S(2)}) collective-permute-start(f32[64,512]{1,0:T(8,128)S(1)} %pad_maximum_fusion.4), channel_id=1, source_target_pairs={{0,24},{1,25},{2,26},{3,27},{4,28},{5,29},{6,30},{7,31},{8,0},{9,1... | collective-permute-start | bytes 393224 | tf_op jit(solution)/shard_map/ppermute | solution.py:495
  (32 other events, 601.6 us)
